TPU v7x, 32 devices: a whole 2x2x4 slice. The times are simulated.
32 devices in a mesh: parts: 2 (over x), freq: 16 (over z, y, core).
Axes of the slice: x: 2, y: 2, z: 4, core: 2. Of those that a mesh axis runs over, the one named last changes fastest.
Arguments:
- spectrum: float32 [32, 2, 2, 256, 256], P(('parts', 'freq')), parts along dimension 0, may hold values from -100 to 100
- blocks: bfloat16 [16, 2, 2, 1024, 1024], P('freq'), may hold values from -0.0625 to 0.0625
- scales: float32 [2, 4096], replicated, may hold values from 0.4 to 4
- iterate: float32 [32, 2, 2, 64, 1024], P(('parts', 'freq')), parts along dimension 0, may hold values from -3 to 3
Outputs:
- new_iterate: float32 [32, 2, 2, 64, 1024], P(('parts', 'freq')), parts along dimension 0
- new_residual: float32 [32, 2, 2, 256, 256], P(('parts', 'freq')), parts along dimension 0
There are 2 independent parts, one for each index of `parts`. A program takes and returns all parts, laid end to end along the dimension named above; an argument that names none is the same for every part. Nothing has to cross between parts.
All inputs are finite; a program needn't handle non-finite values.
Results may differ from a plain program's by a relative error of at most 0.0027.
Values may be sent and summed in bfloat16 or wider, within the bound.
No kernel may reach another device: no remote copies, remote signals or barrier semaphores. Data moves between devices by JAX's collectives and lax.ppermute only.
A program may use at most 128 MiB of HBM per device.

v0:
```python
import jax
import jax.numpy as jnp
from jax import lax
from jax.sharding import PartitionSpec as P


def partner(value, axis, distance):
    mask = 2**distance
    pairs = [(source, source ^ mask) for source in range(lax.axis_size(axis))]
    return lax.ppermute(value, axis, pairs)


def complex_forward(operand, blocks):
    with_real = jnp.einsum(
        "fcmk,fkn->fcmn", operand, blocks[:, 0], preferred_element_type=jnp.float32
    )
    with_imag = jnp.einsum(
        "fcmk,fkn->fcmn", operand, blocks[:, 1], preferred_element_type=jnp.float32
    )
    return jnp.stack([with_real[:, 0] - with_imag[:, 1], with_imag[:, 0] + with_real[:, 1]], axis=1)


def complex_adjoint(residual_in, blocks):
    with_real = jnp.einsum(
        "fcmn,fkn->fcmk", residual_in, blocks[:, 0], preferred_element_type=jnp.float32
    )
    with_imag = jnp.einsum(
        "fcmn,fkn->fcmk", residual_in, blocks[:, 1], preferred_element_type=jnp.float32
    )
    return jnp.stack([with_real[:, 0] + with_imag[:, 1], with_real[:, 1] - with_imag[:, 0]], axis=1)


def double_up(own_piece, axis_dim, bit_list, device_index, swapper):
    gathered = own_piece
    for bit_number in bit_list:
        partner_part = swapper(gathered, bit_number)
        upper_bit = device_index // (1 << bit_number) % 2
        gathered = jnp.where(
            upper_bit == 1,
            jnp.concatenate([partner_part, gathered], axis_dim),
            jnp.concatenate([gathered, partner_part], axis_dim),
        )
    return gathered


def halve_down(summand, axis_dim, bit_list, bit_offset, device_index, swapper):
    bit_count = len(bit_list)
    full_shape = summand.shape
    piece_len = full_shape[axis_dim] // (1 << bit_count)
    pieces = summand.reshape(
        full_shape[:axis_dim] + (2,) * bit_count + (piece_len,) + full_shape[axis_dim + 1 :]
    )
    for bit_number in bit_list:
        bit_axis = axis_dim + bit_count - 1 - (bit_number - bit_offset)
        own_bit = device_index // (1 << bit_number) % 2
        kept_half = lax.dynamic_slice_in_dim(pieces, own_bit, 1, bit_axis)
        sent_half = lax.dynamic_slice_in_dim(pieces, 1 - own_bit, 1, bit_axis)
        pieces = kept_half + swapper(sent_half, bit_number)
    return pieces.reshape(full_shape[:axis_dim] + (piece_len,) + full_shape[axis_dim + 1 :])


def body(spectrum, blocks, scales, iterate):
    device_index = lax.axis_index("freq")
    row_bits = [0, 1]
    col_bits = [2, 3]
    row_order = row_bits[::-1]
    row_block = device_index % 4
    col_block = device_index // 4 % 4
    group_index = device_index // 16
    local_blocks = blocks[0]
    current = iterate[0]
    data_slab = spectrum[0]
    row_len = local_blocks.shape[2]
    slab_len = current.shape[2]
    freq_count = local_blocks.shape[0]
    group_scales = lax.dynamic_slice_in_dim(scales, group_index * freq_count, freq_count, 0)
    row_scale = lax.dynamic_slice_in_dim(group_scales, row_block * row_len, row_len, 1)[
        :, None, None, :
    ]
    scaled = (current * row_scale).astype(jnp.bfloat16)
    rows_all = double_up(
        scaled,
        2,
        col_bits,
        device_index,
        lambda shard_part, bit_number: partner(shard_part, "freq", bit_number),
    )
    forward = complex_forward(rows_all, local_blocks)
    image = halve_down(
        forward,
        3,
        row_order,
        0,
        device_index,
        lambda shard_part, bit_number: partner(shard_part, "freq", bit_number),
    )
    residual = data_slab - image
    residual_cols = double_up(
        residual.astype(jnp.bfloat16),
        3,
        row_bits,
        device_index,
        lambda shard_part, bit_number: partner(shard_part, "freq", bit_number),
    )
    partial_back = complex_adjoint(residual_cols, local_blocks) * row_scale
    summed = partial_back
    for bit_number in col_bits:
        summed = summed + partner(summed, "freq", bit_number)
    descent = lax.dynamic_slice_in_dim(summed, col_block * slab_len, slab_len, 2)
    lifted = (summed * row_scale).astype(jnp.bfloat16)
    gradient_squares = jnp.sum(descent * descent)
    gradient_total = lax.psum(gradient_squares, "freq")
    curvature_part = complex_forward(lifted, local_blocks)
    curvature = halve_down(
        curvature_part,
        3,
        row_order,
        0,
        device_index,
        lambda shard_part, bit_number: partner(shard_part, "freq", bit_number),
    )
    curvature_squares = jnp.sum(curvature * curvature)
    curvature_total = lax.psum(curvature_squares, "freq")
    step_size = gradient_total / curvature_total
    new_iterate = current + step_size * descent
    new_residual = residual - step_size * curvature
    return (new_iterate[None], new_residual[None])


def solution(mesh):
    placed = (
        P(("parts", "freq"), None, None, None, None),
        P("freq", None, None, None, None),
        P(),
        P(("parts", "freq"), None, None, None, None),
    )
    return jax.shard_map(
        body,
        mesh=mesh,
        in_specs=placed,
        out_specs=(
            P(("parts", "freq"), None, None, None, None),
            P(("parts", "freq"), None, None, None, None),
        ),
        check_vma=False,
    )
```

profile of v0, /device:TPU:0, one launch (start us, length us, event | category | flops | bytes accessed | tf_op | source)
XLA Modules:
  0.0 584.9 jit_solution(12975543324344690556)
XLA Ops:
  2.7 3.1 collective-permute-start
  5.8 11.9 %collective-permute-done = bf16[2,2,64,1024]{3,2,1,0:T(8,128)(2,1)S(1)} collective-permute-done((bf16[2,2,64,1024]{3,2,1,0:T(8,128)(2,1)S(1)}, bf16[2,2,64,1024]{3,2,1,0:T(8,128)(2,1)S(1)}, u32[]{:S(2)}, u32[]{:S(2)}) %collective-permute-start) | collective-permute-done | bytes 524320 | tf_op jit(solution)/shard_map/ppermute | solution.py:10
  18.2 2.8 collective-permute-start.1
  21.0 7.6 %copy.18 = bf16[1,2,2,1024,1024]{4,3,1,2,0:T(8,128)(2,1)} copy(bf16[1,2,2,1024,1024]{4,3,2,1,0:T(8,128)(2,1)} %param.5) | data formatting | bytes 16777216 | tf_op args[1]
  28.6 37.4 %collective-permute-done.1 = bf16[2,2,128,1024]{3,2,1,0:T(8,128)(2,1)S(1)} collective-permute-done((bf16[2,2,128,1024]{3,2,1,0:T(8,128)(2,1)S(1)}, bf16[2,2,128,1024]{3,2,1,0:T(8,128)(2,1)S(1)}, u32[]{:S(2)}, u32[]{:S(2)}) %collective-permute-start.1) | collective-permute-done | bytes 1048608 | tf_op jit(solution)/shard_map/ppermute | solution.py:10
  66.0 4.3 fusion.5
  70.6 2.4 fusion.2
  73.0 2.9 slice_add_fusion.2
  76.0 3.0 stack.24
  79.0 4.0 stack.23
  88.9 45.4 %collective-permute-done.2 = f32[2,2,256,1,2,256]{5,2,1,0,4,3:T(8,128)} collective-permute-done((f32[2,2,256,1,2,256]{5,2,1,0,4,3:T(8,128)S(1)}, f32[2,2,256,1,2,256]{5,2,1,0,4,3:T(8,128)}, u32[]{:S(2)}, u32[]{:S(2)}) %collective-permute-start.2) | collective-permute-done | bytes 2097184 | tf_op jit(solution)/shard_map/ppermute | solution.py:10
  134.3 2.6 dynamic-slice_add_fusion.1
  137.9 3.0 collective-permute-done.3
  140.9 2.2 fusion.6
  143.3 2.1 collective-permute-done.4
  148.5 24.1 %collective-permute-done.5 = bf16[2,2,256,512]{3,2,1,0:T(8,128)(2,1)} collective-permute-done((bf16[2,2,256,512]{3,2,1,0:T(8,128)(2,1)S(1)}, bf16[2,2,256,512]{3,2,1,0:T(8,128)(2,1)}, u32[]{:S(2)}, u32[]{:S(2)}) %collective-permute-start.5) | collective-permute-done | bytes 1048608 | tf_op jit(solution)/shard_map/ppermute | solution.py:10
  172.6 5.3 fusion.4
  177.8 5.3 fusion.1
  186.9 90.4 %collective-permute-done.6 = f32[2,2,256,1024]{3,2,1,0:T(8,128)S(1)} collective-permute-done((f32[2,2,256,1024]{3,2,1,0:T(8,128)S(1)}, f32[2,2,256,1024]{3,2,1,0:T(8,128)S(1)}, u32[]{:S(2)}, u32[]{:S(2)}) %collective-permute-start.6) | collective-permute-done | bytes 4194336 | tf_op jit(solution)/shard_map/ppermute | solution.py:10
  278.7 3.2 collective-permute-start.7
  281.8 179.3 %collective-permute-done.7 = f32[2,2,256,1024]{3,2,1,0:T(8,128)S(1)} collective-permute-done((f32[2,2,256,1024]{3,2,1,0:T(8,128)S(1)}, f32[2,2,256,1024]{3,2,1,0:T(8,128)S(1)}, u32[]{:S(2)}, u32[]{:S(2)}) %collective-permute-start.7) | collective-permute-done | bytes 4194336 | tf_op jit(solution)/shard_map/ppermute | solution.py:10
  463.1 6.3 %fusion.3 = f32[2,2,256,1024]{3,2,1,0:T(8,128)S(1)} fusion(bf16[2,2,1024,1024]{3,2,0,1:T(8,128)(2,1)} %bitcast.51, f32[2,2,256,1024]{3,2,1,0:T(8,128)S(1)} %fusion.14, f32[2,1024]{1,0:T(2,128)S(1)} %constant_dynamic-slice_fusion.4), kind=kOutput, calls=%fused_computation.8 | convolution fusion | flops 2149580800 | bytes 12591104 | tf_op jit(solution)/shard_map/fcmk,fkn->fcmn/dot_general | solution.py:17
  469.5 4.6 fusion
  474.1 2.9 slice_add_fusion
  477.0 4.0 stack.28
  481.0 4.0 stack.27
  485.0 2.1 copy_dynamic-update-slice_fusion.1
  489.3 45.1 %collective-permute-done.8 = f32[2,2,256,1,2,256]{5,2,1,0,4,3:T(8,128)S(1)} collective-permute-done((f32[2,2,256,1,2,256]{5,2,1,0,4,3:T(8,128)S(1)}, f32[2,2,256,1,2,256]{5,2,1,0,4,3:T(8,128)S(1)}, u32[]{:S(2)}, u32[]{:S(2)}) %collective-permute-start.8) | collective-permute-done | bytes 2097184 | tf_op jit(solution)/shard_map/ppermute | solution.py:10
  540.1 2.4 multiply_reduce_fusion
  542.5 35.2 %all-reduce = (f32[]{:T(128)}, f32[]{:T(128)}) all-reduce(f32[]{:T(128)} %multiply_reduce_fusion.1, f32[]{:T(128)} %multiply_reduce_fusion), channel_id=1, replica_groups=mesh['parts'=2,'freq'=16] {'freq'}, use_global_device_ids=true, to_apply=%region_1.2 | all-reduce | flops 2 | bytes 16 | tf_op jit(solution)/shard_map/psum | solution.py:112
  579.1 2.4 fusion.8
  581.5 3.5 bitcast_subtract_fusion
  (43 shorter events, 28.0 us)
Async XLA Ops:
  0.6 0.8 copy-start
  2.7 15.0 %collective-permute-start = (bf16[2,2,64,1024]{3,2,1,0:T(8,128)(2,1)S(1)}, bf16[2,2,64,1024]{3,2,1,0:T(8,128)(2,1)S(1)}, u32[]{:S(2)}, u32[]{:S(2)}) collective-permute-start(bf16[2,2,64,1024]{3,2,1,0:T(8,128)(2,1)S(1)} %fusion.7), channel_id=1, source_target_pairs={{0,4},{1,5},{2,6},{3,7},{4,0},{5,1},{6,2},{7,3},{8,12},{9,13},{10,... | collective-permute-start | bytes 1572872 | tf_op jit(solution)/shard_map/ppermute | solution.py:10
  18.2 47.8 %collective-permute-start.1 = (bf16[2,2,128,1024]{3,2,1,0:T(8,128)(2,1)S(1)}, bf16[2,2,128,1024]{3,2,1,0:T(8,128)(2,1)S(1)}, u32[]{:S(2)}, u32[]{:S(2)}) collective-permute-start(bf16[2,2,128,1024]{3,2,1,0:T(8,128)(2,1)S(1)} %maximum_select_fusion.2), channel_id=1, source_target_pairs={{0,8},{1,9},{2,10},{3,11},{4,12},{5,13},{6,14},{7,15},{8,0},{9,1},... | collective-permute-start | bytes 3145736 | tf_op jit(solution)/shard_map/ppermute | solution.py:10
  66.0 4.6 copy-start.5
  85.4 2.0 copy-start.3
  87.5 46.8 %collective-permute-start.2 = (f32[2,2,256,1,2,256]{5,2,1,0,4,3:T(8,128)S(1)}, f32[2,2,256,1,2,256]{5,2,1,0,4,3:T(8,128)}, u32[]{:S(2)}, u32[]{:S(2)}) collective-permute-start(f32[2,2,256,1,2,256]{5,2,1,0,4,3:T(8,128)S(1)} %constant_dynamic-slice_fusion.3), channel_id=1, source_target_pairs={{0,2},{1,3},{2,0},{3,1},{4,6},{5,7},{6,4},{7,5},{8,10},{9,11},{10,... | collective-permute-start | bytes 6291464 | tf_op jit(solution)/shard_map/ppermute | solution.py:10
  88.9 52.0 %copy-start.8 = (f32[1,2,2,256,256]{4,3,2,1,0:T(8,128)S(1)}, f32[1,2,2,256,256]{4,3,2,1,0:T(8,128)}, u32[]{:S(2)}) copy-start(f32[1,2,2,256,256]{4,3,2,1,0:T(8,128)} %param.4) | copy-start | bytes 3145732
  137.9 3.0 collective-permute-start.3
  143.1 2.3 collective-permute-start.4
  147.2 25.4 %collective-permute-start.5 = (bf16[2,2,256,512]{3,2,1,0:T(8,128)(2,1)S(1)}, bf16[2,2,256,512]{3,2,1,0:T(8,128)(2,1)}, u32[]{:S(2)}, u32[]{:S(2)}) collective-permute-start(bf16[2,2,256,512]{3,2,1,0:T(8,128)(2,1)S(1)} %maximum_select_fusion.3), channel_id=1, source_target_pairs={{0,2},{1,3},{2,0},{3,1},{4,6},{5,7},{6,4},{7,5},{8,10},{9,11},{10,... | collective-permute-start | bytes 3145736 | tf_op jit(solution)/shard_map/ppermute | solution.py:10
  185.4 91.9 %collective-permute-start.6 = (f32[2,2,256,1024]{3,2,1,0:T(8,128)S(1)}, f32[2,2,256,1024]{3,2,1,0:T(8,128)S(1)}, u32[]{:S(2)}, u32[]{:S(2)}) collective-permute-start(f32[2,2,256,1024]{3,2,1,0:T(8,128)S(1)} %maximum_multiply_fusion), channel_id=1, source_target_pairs={{0,4},{1,5},{2,6},{3,7},{4,0},{5,1},{6,2},{7,3},{8,12},{9,13},{10,... | collective-permute-start | bytes 12582920 | tf_op jit(solution)/shard_map/ppermute | solution.py:10
  278.7 182.5 %collective-permute-start.7 = (f32[2,2,256,1024]{3,2,1,0:T(8,128)S(1)}, f32[2,2,256,1024]{3,2,1,0:T(8,128)S(1)}, u32[]{:S(2)}, u32[]{:S(2)}) collective-permute-start(f32[2,2,256,1024]{3,2,1,0:T(8,128)S(1)} %fusion.13), channel_id=1, source_target_pairs={{0,8},{1,9},{2,10},{3,11},{4,12},{5,13},{6,14},{7,15},{8,0},{9,1},... | collective-permute-start | bytes 12582920 | tf_op jit(solution)/shard_map/ppermute | solution.py:10
  463.1 6.3 %copy-start.4 = (f32[2,2,256,1024]{3,2,1,0:T(8,128)}, f32[2,2,256,1024]{3,2,1,0:T(8,128)S(1)}, u32[]{:S(2)}) copy-start(f32[2,2,256,1024]{3,2,1,0:T(8,128)S(1)} %fusion.14) | copy-start | bytes 12582916
  485.0 2.2 copy-start.6
  487.7 46.7 %collective-permute-start.8 = (f32[2,2,256,1,2,256]{5,2,1,0,4,3:T(8,128)S(1)}, f32[2,2,256,1,2,256]{5,2,1,0,4,3:T(8,128)S(1)}, u32[]{:S(2)}, u32[]{:S(2)}) collective-permute-start(f32[2,2,256,1,2,256]{5,2,1,0,4,3:T(8,128)S(1)} %constant_dynamic-slice_fusion.1), channel_id=1, source_target_pairs={{0,2},{1,3},{2,0},{3,1},{4,6},{5,7},{6,4},{7,5},{8,10},{9,11},{10,... | collective-permute-start | bytes 6291464 | tf_op jit(solution)/shard_map/ppermute | solution.py:10
  534.7 1.3 copy-start.2
  536.0 43.1 %copy-start.7 = (f32[1,2,2,64,1024]{4,3,2,1,0:T(8,128)S(1)}, f32[1,2,2,64,1024]{4,3,2,1,0:T(8,128)}, u32[]{:S(2)}) copy-start(f32[1,2,2,64,1024]{4,3,2,1,0:T(8,128)} %param.7) | copy-start | bytes 3145732
  537.1 3.0 collective-permute-start.9
  577.7 7.2 %copy-start.1 = (f32[2,4096]{1,0:T(2,128)S(1)}, f32[2,4096]{1,0:T(2,128)}, u32[]{:S(2)}) copy-start(f32[2,4096]{1,0:T(2,128)} %param.6) | copy-start | bytes 98308
where the time goes:
time: 586 us; the launch traced here: 585 us
  waiting for transfers between devices  439 us (75%)
  blocking collectives  35.2 us (6%)
  local copies, waits for them, and re-layouts  34.4 us (6%)
  other arithmetic  30.5 us (5%)
  matrix products  28.2 us (5%)
  starting transfers between devices  15 us (3%)
    ppermute x10, waiting for transfers between devices, partner(): return lax.ppermute(value, axis, pairs)  439 us
    psum x1, blocking collectives, body(): gradient_total = lax.psum(gradient_squares, 'freq')  35.2 us
    unnamed x21, local copies, waits for them, and re-layouts  16.2 us
    another operation x6, local copies, waits for them, and re-layouts, complex_forward(): jnp.stack([with_real[:, 0] - with_imag[:, 1], with_imag[:, 0] + with_real...  15.8 us
    ppermute x10, starting transfers between devices, partner(): return lax.ppermute(value, axis, pairs)  15 us
  transfers between devices with their start and end apart: 10, of which 10 were waited for; matrix products, arithmetic and copies ran while one was open for 2% of the time, Pallas kernels for 0%

commit v1 on v0

v1 whole, which is shorter than its diff:
```python
import jax
import jax.numpy as jnp
from jax import lax
from jax.sharding import PartitionSpec as P

ROWS = 4
COLS = 4
TEAM = ROWS * COLS
SPLIT = 1


def team_pairs(pairs):
    groups = lax.axis_size("freq") // TEAM
    return [(TEAM * g + a, TEAM * g + b) for g in range(groups) for a, b in pairs]


def along_columns(value, moves):
    pairs = [(ROWS * a + r, ROWS * b + r) for a, b in moves for r in range(ROWS)]
    return lax.ppermute(value, "freq", team_pairs(pairs))


def swap(value, bit):
    return lax.ppermute(value, "freq", team_pairs([(d, d ^ (1 << bit)) for d in range(TEAM)]))


def forward_product(field, matrix):
    real, imag = field[0], field[1]
    left = jnp.stack([jnp.stack([real, -imag], 1), jnp.stack([imag, real], 1)], 0)
    return lax.dot_general(
        left, matrix, (((2, 3), (0, 1)), ((), ())), preferred_element_type=jnp.float32
    )


def adjoint_product(field, matrix):
    real, imag = field[0], field[1]
    left = jnp.stack([jnp.stack([real, imag], 1), jnp.stack([imag, -real], 1)], 0)
    return lax.dot_general(
        left, matrix, (((2, 3), (0, 2)), ((), ())), preferred_element_type=jnp.float32
    )


def body(spectrum, blocks, scales, iterate):
    f32, bf16 = jnp.float32, jnp.bfloat16
    index = lax.axis_index("freq")
    core = index % 2
    y = index // 2 % 2
    row_block = index % ROWS
    col = index // ROWS % COLS
    group = index // TEAM
    matrix = blocks[0]
    current = iterate[0]
    data = spectrum[0]
    freqs, _, row_len, col_len = matrix.shape
    slab = current.shape[2]
    piece = slab // SPLIT
    part_len = col_len // ROWS
    own_scales = lax.dynamic_slice(
        scales, (group * freqs, row_block * row_len), (freqs, row_len)
    )
    is_hub = (col == 1) | (col == 2)

    def gather_columns(own):
        other = along_columns(own, [(0, 1), (1, 0), (2, 3), (3, 2)])
        odd = col % 2 == 1
        pair = jnp.where(odd, jnp.stack([other, own], 1), jnp.stack([own, other], 1))
        far_hub = along_columns(pair, [(1, 2), (2, 1)])
        far_end = along_columns(far_hub, [(1, 0), (2, 3)])
        far = jnp.where(is_hub, far_hub, far_end)
        both = jnp.where(
            col < 2, jnp.concatenate([pair, far], 1), jnp.concatenate([far, pair], 1)
        )
        return both.reshape(2, COLS * own.shape[1], own.shape[2])

    def scatter_rows(part):
        count = part.shape[1]
        pieces = part.reshape(2, count, 2, 2, part_len)
        sent = jnp.where(core == 0, pieces[:, :, :, 1], pieces[:, :, :, 0])
        kept = jnp.where(core == 0, pieces[:, :, :, 0], pieces[:, :, :, 1])
        half = kept + swap(sent, 0)
        sent = jnp.where(y == 0, half[:, :, 1], half[:, :, 0]).astype(bf16)
        kept = jnp.where(y == 0, half[:, :, 0], half[:, :, 1])
        return kept + swap(sent, 1).astype(f32)

    def gather_rows(own):
        other = swap(own, 1)
        pair = jnp.where(y == 0, jnp.stack([own, other], 2), jnp.stack([other, own], 2))
        far = swap(pair, 0)
        both = jnp.where(core == 0, jnp.stack([pair, far], 3), jnp.stack([far, pair], 3))
        return both.reshape(2, own.shape[1], col_len)

    def sum_columns(part):
        first = along_columns(part.astype(bf16), [(0, 1), (3, 2)]).astype(f32)
        second = along_columns((part + first).astype(bf16), [(1, 2), (2, 1)]).astype(f32)
        third = along_columns((part + second).astype(bf16), [(1, 0), (2, 3)]).astype(f32)
        return (part + first) + (second + third)

    chunks = [(f, h) for f in range(freqs) for h in range(SPLIT)]

    def data_rows(f, h):
        rows = data[f].reshape(2, COLS, SPLIT, piece, part_len)[:, :, h]
        return rows.reshape(2, COLS * piece, part_len)

    gathered = []
    for f, h in chunks:
        own = current[f, :, h * piece : (h + 1) * piece] * own_scales[f]
        gathered.append(gather_columns(own.astype(bf16)))
    residuals, descents, curvatures = [], [], []
    gamma, bent = 0.0, 0.0
    for (f, h), field in zip(chunks, gathered):
        image = scatter_rows(forward_product(field, matrix[f]))
        residual = data_rows(f, h) - image
        residuals.append(residual)
        summed = sum_columns(adjoint_product(gather_rows(residual.astype(bf16)), matrix[f]))
        descent = summed * own_scales[f]
        own = lax.dynamic_slice_in_dim(descent, col * piece, piece, 1)
        descents.append(own)
        gamma = gamma + jnp.sum(own * own)
        lifted = (descent * own_scales[f]).astype(bf16)
        curvature = scatter_rows(forward_product(lifted, matrix[f]))
        curvatures.append(curvature)
        bent = bent + jnp.sum(curvature * curvature)
    sums = jnp.stack([jnp.full((8, 128), gamma), jnp.full((8, 128), bent)])
    for bit in range(4):
        sums = sums + swap(sums, bit)
    step = sums[0, 0, 0] / sums[1, 0, 0]

    new_iterate, new_residual = [], []
    for f in range(freqs):
        mine = [n for n, (g, _) in enumerate(chunks) if g == f]
        descent = jnp.concatenate([descents[n] for n in mine], 1)
        new_iterate.append(current[f] + step * descent)
        fresh = [residuals[n] - step * curvatures[n] for n in mine]
        fresh = jnp.stack([r.reshape(2, COLS, piece, part_len) for r in fresh], 2)
        new_residual.append(fresh.reshape(2, COLS * slab, part_len))
    return (jnp.stack(new_iterate)[None], jnp.stack(new_residual)[None])


def solution(mesh):
    placed = P(("parts", "freq"), None, None, None, None)
    return jax.shard_map(
        body,
        mesh=mesh,
        in_specs=(placed, P("freq", None, None, None, None), P(), placed),
        out_specs=(placed, placed),
        check_vma=False,
    )
```

time: 586 us -> 271 us (0.46)
  waiting for transfers between devices: 439 us -> 125 us
  blocking collectives: 35.2 us -> 0 us
  starting transfers between devices: 15 us -> 34.6 us
  other arithmetic: 30.5 us -> 41.2 us
  local copies, waits for them, and re-layouts: 34.4 us -> 43.8 us
  matrix products: 28.2 us -> 19.6 us
    ppermute x10 -> x28, waiting for transfers between devices: 439 us -> 125 us  [the longest x12 93.4 us: along_columns(): return lax.ppermute(value, 'freq', team_pairs(pairs))]
    psum x1 -> x0, blocking collectives: 35.2 us -> none  [body(): gradient_total = lax.psum(gradient_squares, 'freq')]
    ppermute x10 -> x28, starting transfers between devices: 15 us -> 34.6 us  [the longest x12 23.1 us: along_columns(): return lax.ppermute(value, 'freq', team_pairs(pairs))]
    dot_general x0 -> x3, local copies, waits for them, and re-layouts: none -> 18.5 us  [forward_product(): lax.dot_general(left, matrix, (((2, 3), (0, 1)), ((), ())), preferred_ele...]
    another operation x6, local copies, waits for them, and re-layouts: 15.8 us -> 4.65 us  [the longest x4 4.57 us: adjoint_product(): jnp.stack([real, imag], 1)]
    add x7 -> x8, other arithmetic: 13.5 us -> 3.62 us  [the longest x4 3.47 us: scatter_rows(): half = kept + swap(sent, 0)]
    convert_element_type x2 -> x14, other arithmetic: 3.53 us -> 13.3 us  [the longest x2 5.65 us: body(): lifted = (descent * own_scales[f]).astype(bf16)]
    dot_general x6, matrix products: 28.2 us -> 19.6 us  [the longest x2 10.1 us: adjoint_product(): lax.dot_general(left, matrix, (((2, 3), (0, 2)), ((), ())), preferred_ele...]
  transfers between devices with their start and end apart: 10 -> 28, of which waited for: 10 -> 19; matrix products, arithmetic and copies ran while one was open for 2% -> 28% of each run, Pallas kernels for 0% -> 0%
where the time goes in v1:
time: 271 us; the launch traced here: 270 us
  waiting for transfers between devices  125 us (46%)
  local copies, waits for them, and re-layouts  43.8 us (16%)
  other arithmetic  41.2 us (15%)
  starting transfers between devices  34.6 us (13%)
  matrix products  19.6 us (7%)
  between operations  5.26 us (2%)
    ppermute x12, waiting for transfers between devices, along_columns(): return lax.ppermute(value, 'freq', team_pairs(pairs))  93.4 us
    ppermute x16, waiting for transfers between devices, swap(): lax.ppermute(value, 'freq', team_pairs([(d, d ^ 1 << bit) for d in range(...  31.7 us
    ppermute x12, starting transfers between devices, along_columns(): return lax.ppermute(value, 'freq', team_pairs(pairs))  23.1 us
    dot_general x3, local copies, waits for them, and re-layouts, forward_product(): lax.dot_general(left, matrix, (((2, 3), (0, 1)), ((), ())), preferred_ele...  18.5 us
    unnamed x35, local copies, waits for them, and re-layouts  12.9 us
    ppermute x16, starting transfers between devices, swap(): lax.ppermute(value, 'freq', team_pairs([(d, d ^ 1 << bit) for d in range(...  11.6 us
    dot_general x2, matrix products, adjoint_product(): lax.dot_general(left, matrix, (((2, 3), (0, 2)), ((), ())), preferred_ele...  10.1 us
    dot_general x4, matrix products, forward_product(): lax.dot_general(left, matrix, (((2, 3), (0, 1)), ((), ())), preferred_ele...  9.43 us
  transfers between devices with their start and end apart: 28, of which 19 were waited for; matrix products, arithmetic and copies ran while one was open for 28% of the time, Pallas kernels for 0%

profile of v1, /device:TPU:0, one launch (start us, length us, event | category | flops | bytes accessed | tf_op | source)
XLA Modules:
  0.0 269.5 jit_solution(16833062069713724853)
XLA Ops:
  2.8 3.1 %collective-permute-start = (bf16[2,64,1024]{2,1,0:T(8,128)(2,1)S(1)}, bf16[2,64,1024]{2,1,0:T(8,128)(2,1)S(1)}, u32[]{:S(2)}, u32[]{:S(2)}) collective-permute-start(bf16[2,64,1024]{2,1,0:T(8,128)(2,1)S(1)} %get-tuple-element.31), channel_id=1, source_target_pairs={{0,4},{1,5},{2,6},{3,7},{4,0},{5,1},{6,2},{7,3},{8,12},{9,13},{10,... | collective-permute-start | bytes 786440 | tf_op jit(solution)/shard_map/ppermute | solution.py:19
  6.1 6.9 %collective-permute-done = bf16[2,64,1024]{2,1,0:T(8,128)(2,1)S(1)} collective-permute-done((bf16[2,64,1024]{2,1,0:T(8,128)(2,1)S(1)}, bf16[2,64,1024]{2,1,0:T(8,128)(2,1)S(1)}, u32[]{:S(2)}, u32[]{:S(2)}) %collective-permute-start) | collective-permute-done | bytes 262176 | tf_op jit(solution)/shard_map/ppermute | solution.py:19
  13.9 4.0 %collective-permute-done.10 = bf16[2,64,1024]{2,1,0:T(8,128)(2,1)S(1)} collective-permute-done((bf16[2,64,1024]{2,1,0:T(8,128)(2,1)S(1)}, bf16[2,64,1024]{2,1,0:T(8,128)(2,1)S(1)}, u32[]{:S(2)}, u32[]{:S(2)}) %collective-permute-start.10) | collective-permute-done | bytes 262176 | tf_op jit(solution)/shard_map/ppermute | solution.py:19
  21.3 6.0 %slice_bitcast_fusion.1 = (bf16[1024,2,1024]{0,2,1:T(8,128)(2,1)}, bf16[1024,2,1024]{0,2,1:T(8,128)(2,1)}) fusion(bf16[1,2,2,1024,1024]{4,3,2,1,0:T(8,128)(2,1)} %param.5), kind=kLoop, calls=%fused_computation.15 | loop fusion | bytes 16777216 | tf_op jit(solution)/shard_map/dot_general | solution.py:29
  27.2 6.2 %copy.47 = bf16[1024,2,1024]{2,0,1:T(8,128)(2,1)} copy(bf16[1024,2,1024]{0,2,1:T(8,128)(2,1)} %get-tuple-element.15) | data formatting | bytes 8388608 | tf_op jit(solution)/shard_map/dot_general | solution.py:29
  33.5 6.3 %copy.27 = bf16[1024,2,1024]{2,0,1:T(8,128)(2,1)} copy(bf16[1024,2,1024]{0,2,1:T(8,128)(2,1)} %get-tuple-element.14) | data formatting | bytes 8388608 | tf_op jit(solution)/shard_map/dot_general | solution.py:29
  41.8 9.9 %collective-permute-done.12 = bf16[2,2,64,1024]{3,2,0,1:T(8,128)(2,1)} collective-permute-done((bf16[2,2,64,1024]{3,2,0,1:T(8,128)(2,1)S(1)}, bf16[2,2,64,1024]{3,2,0,1:T(8,128)(2,1)}, u32[]{:S(2)}, u32[]{:S(2)}) %collective-permute-start.12) | collective-permute-done | bytes 524320 | tf_op jit(solution)/shard_map/ppermute | solution.py:19
  55.5 2.4 fusion.35
  61.4 2.4 fusion.41
  66.1 2.3 fusion.81
  77.8 5.5 %collective-permute-done.14 = bf16[2,256,256]{1,2,0:T(8,128)(2,1)S(1)} collective-permute-done((bf16[2,256,256]{1,2,0:T(8,128)(2,1)S(1)}, bf16[2,256,256]{1,2,0:T(8,128)(2,1)S(1)}, u32[]{:S(2)}, u32[]{:S(2)}) %collective-permute-start.14) | collective-permute-done | bytes 262176 | tf_op jit(solution)/shard_map/ppermute | solution.py:23
  85.8 3.1 %collective-permute-done.4 = bf16[2,256,256]{1,2,0:T(8,128)(2,1)S(1)} collective-permute-done((bf16[2,256,256]{1,2,0:T(8,128)(2,1)S(1)}, bf16[2,256,256]{1,2,0:T(8,128)(2,1)S(1)}, u32[]{:S(2)}, u32[]{:S(2)}) %collective-permute-start.4) | collective-permute-done | bytes 262176 | tf_op jit(solution)/shard_map/ppermute | solution.py:23
  91.4 3.1 %collective-permute-done.15 = bf16[2,256,256]{1,2,0:T(8,128)(2,1)S(1)} collective-permute-done((bf16[2,256,256]{1,2,0:T(8,128)(2,1)S(1)}, bf16[2,256,256]{1,2,0:T(8,128)(2,1)S(1)}, u32[]{:S(2)}, u32[]{:S(2)}) %collective-permute-start.15) | collective-permute-done | bytes 262176 | tf_op jit(solution)/shard_map/ppermute | solution.py:23
  94.7 4.5 %collective-permute-done.5 = bf16[2,256,256]{1,2,0:T(8,128)(2,1)S(1)} collective-permute-done((bf16[2,256,256]{1,2,0:T(8,128)(2,1)S(1)}, bf16[2,256,256]{1,2,0:T(8,128)(2,1)S(1)}, u32[]{:S(2)}, u32[]{:S(2)}) %collective-permute-start.5) | collective-permute-done | bytes 262176 | tf_op jit(solution)/shard_map/ppermute | solution.py:23
  102.2 5.6 %bitcast_convert_fusion = (bf16[2,256,1024]{2,1,0:T(8,128)(2,1)}, f32[2,256,1024,1]{2,1,3,0:T(8,128)S(1)}) fusion(bf16[1,2,2,1024,1024]{4,3,2,1,0:T(8,128)(2,1)} %param.5, bf16[1,256,2,1024]{3,1,2,0:T(8,128)(2,1)S(1)} %get-tuple-element.48, bf16[1,256,2,1024]{3,1,2,0:T(8,128)(2,1)S(1)} %get-tuple-element.47), kind=kOutput, calls=%fused_computation.46 | convolution fusion | flops 2149056512 | bytes 9437184 | tf_op jit(solution)/shard_map/dot_general | solution.py:37
  107.8 10.5 %collective-permute-start.17 = (bf16[2,256,1024]{2,1,0:T(8,128)(2,1)}, bf16[2,256,1024]{2,1,0:T(8,128)(2,1)}, u32[]{:S(2)}, u32[]{:S(2)}) collective-permute-start(bf16[2,256,1024]{2,1,0:T(8,128)(2,1)} %get-tuple-element.57), channel_id=1, source_target_pairs={{0,4},{1,5},{2,6},{3,7},{12,8},{13,9},{14,10},{15,11},{16,20},{17,... | collective-permute-start | bytes 3145736 | tf_op jit(solution)/shard_map/ppermute | solution.py:19
  121.4 2.1 copy.42
  127.3 2.1 copy.43
  131.1 4.6 %bitcast_convert_fusion.1 = (bf16[2,256,1024]{2,1,0:T(8,128)(2,1)S(1)}, f32[2,256,1024,1]{2,1,3,0:T(8,128)S(1)}) fusion(bf16[1,2,2,1024,1024]{4,3,2,1,0:T(8,128)(2,1)} %param.5, bf16[1,256,2,1024]{3,1,2,0:T(8,128)(2,1)S(1)} %get-tuple-element.44, bf16[1,256,2,1024]{3,1,2,0:T(8,128)(2,1)S(1)} %get-tuple-element.43), kind=kOutput, calls=%fused_computation.48 | convolution fusion | flops 2149056512 | bytes 9437184 | tf_op jit(solution)/shard_map/dot_general | solution.py:37
  137.0 4.1 %collective-permute-done.17 = bf16[2,256,1024]{2,1,0:T(8,128)(2,1)} collective-permute-done((bf16[2,256,1024]{2,1,0:T(8,128)(2,1)}, bf16[2,256,1024]{2,1,0:T(8,128)(2,1)}, u32[]{:S(2)}, u32[]{:S(2)}) %collective-permute-start.17) | collective-permute-done | bytes 1048608 | tf_op jit(solution)/shard_map/ppermute | solution.py:19
  143.4 19.7 %collective-permute-done.7 = bf16[2,256,1024]{2,1,0:T(8,128)(2,1)S(1)} collective-permute-done((bf16[2,256,1024]{2,1,0:T(8,128)(2,1)S(1)}, bf16[2,256,1024]{2,1,0:T(8,128)(2,1)S(1)}, u32[]{:S(2)}, u32[]{:S(2)}) %collective-permute-start.7) | collective-permute-done | bytes 1048608 | tf_op jit(solution)/shard_map/ppermute | solution.py:19
  167.6 27.2 %collective-permute-done.19 = bf16[2,256,1024]{2,1,0:T(8,128)(2,1)S(1)} collective-permute-done((bf16[2,256,1024]{2,1,0:T(8,128)(2,1)S(1)}, bf16[2,256,1024]{2,1,0:T(8,128)(2,1)S(1)}, u32[]{:S(2)}, u32[]{:S(2)}) %collective-permute-start.19) | collective-permute-done | bytes 1048608 | tf_op jit(solution)/shard_map/ppermute | solution.py:19
  194.8 3.4 %multiply_convert_fusion = (bf16[2,256,1024]{2,1,0:T(8,128)(2,1)S(1)}, f32[2,256,1024]{2,1,0:T(8,128)}) fusion(f32[1024]{0:T(1024)S(1)} %bitcast.294, bf16[2,256,1024]{2,1,0:T(8,128)(2,1)S(1)} %collective-permute-done.19, bf16[2,256,1024]{2,1,0:T(8,128)(2,1)S(1)} %collective-permute-done.18, bf16[2,256,1024]{2,1,0:T(8,128)(2,1)} %collective-permute-done.17, ...), kind=kLoop, calls=%fused_computation.49 | loop fusion | flops 4718592 | bytes 8392704 | tf_op jit(solution)/shard_map/convert_element_type | solution.py:118
  198.4 19.5 %collective-permute-done.9 = bf16[2,256,1024]{2,1,0:T(8,128)(2,1)S(1)} collective-permute-done((bf16[2,256,1024]{2,1,0:T(8,128)(2,1)S(1)}, bf16[2,256,1024]{2,1,0:T(8,128)(2,1)S(1)}, u32[]{:S(2)}, u32[]{:S(2)}) %collective-permute-start.9) | collective-permute-done | bytes 1048608 | tf_op jit(solution)/shard_map/ppermute | solution.py:19
  217.8 2.3 multiply_convert_fusion.1
  222.3 2.4 fusion.38
  226.9 2.4 fusion.44
  240.6 4.5 %collective-permute-done.21 = bf16[2,256,256]{1,2,0:T(8,128)(2,1)} collective-permute-done((bf16[2,256,256]{1,2,0:T(8,128)(2,1)}, bf16[2,256,256]{1,2,0:T(8,128)(2,1)}, u32[]{:S(2)}, u32[]{:S(2)}) %collective-permute-start.21) | collective-permute-done | bytes 262176 | tf_op jit(solution)/shard_map/ppermute | solution.py:23
  251.0 2.1 collective-permute-done.25
  253.2 3.6 %collective-permute-done.26 = f32[2,8,128]{2,1,0:T(8,128)S(1)} collective-permute-done((f32[2,8,128]{2,1,0:T(8,128)S(1)}, f32[2,8,128]{2,1,0:T(8,128)S(1)}, u32[]{:S(2)}, u32[]{:S(2)}) %collective-permute-start.26) | collective-permute-done | bytes 8224 | tf_op jit(solution)/shard_map/ppermute | solution.py:23
  257.8 3.5 %collective-permute-done.27 = f32[2,8,128]{2,1,0:T(8,128)S(1)} collective-permute-done((f32[2,8,128]{2,1,0:T(8,128)S(1)}, f32[2,8,128]{2,1,0:T(8,128)S(1)}, u32[]{:S(2)}, u32[]{:S(2)}) %collective-permute-start.27) | collective-permute-done | bytes 8224 | tf_op jit(solution)/shard_map/ppermute | solution.py:23
  263.4 2.5 fusion.60
  (145 shorter events, 76.7 us)
Async XLA Ops:
  2.8 10.2 %collective-permute-start = (bf16[2,64,1024]{2,1,0:T(8,128)(2,1)S(1)}, bf16[2,64,1024]{2,1,0:T(8,128)(2,1)S(1)}, u32[]{:S(2)}, u32[]{:S(2)}) collective-permute-start(bf16[2,64,1024]{2,1,0:T(8,128)(2,1)S(1)} %get-tuple-element.31), channel_id=1, source_target_pairs={{0,4},{1,5},{2,6},{3,7},{4,0},{5,1},{6,2},{7,3},{8,12},{9,13},{10,... | collective-permute-start | bytes 786440 | tf_op jit(solution)/shard_map/ppermute | solution.py:19
  5.9 11.9 %collective-permute-start.10 = (bf16[2,64,1024]{2,1,0:T(8,128)(2,1)S(1)}, bf16[2,64,1024]{2,1,0:T(8,128)(2,1)S(1)}, u32[]{:S(2)}, u32[]{:S(2)}) collective-permute-start(bf16[2,64,1024]{2,1,0:T(8,128)(2,1)S(1)} %get-tuple-element.32), channel_id=1, source_target_pairs={{0,4},{1,5},{2,6},{3,7},{4,0},{5,1},{6,2},{7,3},{8,12},{9,13},{10,... | collective-permute-start | bytes 786440 | tf_op jit(solution)/shard_map/ppermute | solution.py:19
  13.1 14.1 %copy-start.7 = (bf16[2,2,64,1024]{3,2,0,1:T(8,128)(2,1)}, bf16[2,2,64,1024]{3,2,0,1:T(8,128)(2,1)S(1)}, u32[]{:S(2)}) copy-start(bf16[2,2,64,1024]{3,2,0,1:T(8,128)(2,1)S(1)} %maximum_select_fusion.4) | copy-start | bytes 1572868
  13.2 5.5 %collective-permute-start.1 = (bf16[2,2,64,1024]{3,2,0,1:T(8,128)(2,1)S(1)}, bf16[2,2,64,1024]{3,2,0,1:T(8,128)(2,1)S(1)}, u32[]{:S(2)}, u32[]{:S(2)}) collective-permute-start(bf16[2,2,64,1024]{3,2,0,1:T(8,128)(2,1)S(1)} %maximum_select_fusion.4), channel_id=1, source_target_pairs={{4,8},{5,9},{6,10},{7,11},{8,4},{9,5},{10,6},{11,7},{20,24},{21,25... | collective-permute-start | bytes 1572872 | tf_op jit(solution)/shard_map/ppermute | solution.py:19
  17.9 2.0 collective-permute-start.11
  18.7 23.2 %collective-permute-start.2 = (bf16[2,2,64,1024]{3,2,0,1:T(8,128)(2,1)S(1)}, bf16[2,2,64,1024]{3,2,0,1:T(8,128)(2,1)}, u32[]{:S(2)}, u32[]{:S(2)}) collective-permute-start(bf16[2,2,64,1024]{3,2,0,1:T(8,128)(2,1)S(1)} %collective-permute-done.1), channel_id=1, source_target_pairs={{4,0},{5,1},{6,2},{7,3},{8,12},{9,13},{10,14},{11,15},{20,16},{21,... | collective-permute-start | bytes 1572872 | tf_op jit(solution)/shard_map/ppermute | solution.py:19
  20.0 31.8 %collective-permute-start.12 = (bf16[2,2,64,1024]{3,2,0,1:T(8,128)(2,1)S(1)}, bf16[2,2,64,1024]{3,2,0,1:T(8,128)(2,1)}, u32[]{:S(2)}, u32[]{:S(2)}) collective-permute-start(bf16[2,2,64,1024]{3,2,0,1:T(8,128)(2,1)S(1)} %collective-permute-done.11), channel_id=1, source_target_pairs={{4,0},{5,1},{6,2},{7,3},{8,12},{9,13},{10,14},{11,15},{20,16},{21,... | collective-permute-start | bytes 1572872 | tf_op jit(solution)/shard_map/ppermute | solution.py:19
  59.0 13.5 %collective-permute-start.13 = (f32[2,256,2,256]{1,3,0,2:T(8,128)}, f32[2,256,2,256]{1,3,0,2:T(8,128)}, u32[]{:S(2)}, u32[]{:S(2)}) collective-permute-start(f32[2,256,2,256]{1,3,0,2:T(8,128)} %select_bitcast_fusion.2), channel_id=1, source_target_pairs={{0,1},{1,0},{2,3},{3,2},{4,5},{5,4},{6,7},{7,6},{8,9},{9,8},{10,11... | collective-permute-start | bytes 3145736 | tf_op jit(solution)/shard_map/ppermute | solution.py:23
  65.6 10.1 %collective-permute-start.3 = (f32[2,256,2,256]{1,3,2,0:T(8,128)}, f32[2,256,2,256]{1,3,2,0:T(8,128)}, u32[]{:S(2)}, u32[]{:S(2)}) collective-permute-start(f32[2,256,2,256]{1,3,2,0:T(8,128)} %get-tuple-element.17), channel_id=1, source_target_pairs={{0,1},{1,0},{2,3},{3,2},{4,5},{5,4},{6,7},{7,6},{8,9},{9,8},{10,11... | collective-permute-start | bytes 3145736 | tf_op jit(solution)/shard_map/ppermute | solution.py:23
  74.1 9.2 %collective-permute-start.14 = (bf16[2,256,256]{1,2,0:T(8,128)(2,1)S(1)}, bf16[2,256,256]{1,2,0:T(8,128)(2,1)S(1)}, u32[]{:S(2)}, u32[]{:S(2)}) collective-permute-start(bf16[2,256,256]{1,2,0:T(8,128)(2,1)S(1)} %fusion.62), channel_id=1, source_target_pairs={{0,2},{1,3},{2,0},{3,1},{4,6},{5,7},{6,4},{7,5},{8,10},{9,11},{10,... | collective-permute-start | bytes 786440 | tf_op jit(solution)/shard_map/ppermute | solution.py:23
  77.2 11.8 %copy-start.10 = (f32[1,1,2,256,256]{3,4,2,1,0:T(8,128)S(1)}, f32[1,1,2,256,256]{3,4,2,1,0:T(8,128)}, u32[]{:S(2)}) copy-start(f32[1,1,2,256,256]{3,4,2,1,0:T(8,128)} %copy.86) | copy-start | bytes 1572868
  77.3 11.7 %collective-permute-start.4 = (bf16[2,256,256]{1,2,0:T(8,128)(2,1)S(1)}, bf16[2,256,256]{1,2,0:T(8,128)(2,1)S(1)}, u32[]{:S(2)}, u32[]{:S(2)}) collective-permute-start(bf16[2,256,256]{1,2,0:T(8,128)(2,1)S(1)} %fusion.61), channel_id=1, source_target_pairs={{0,2},{1,3},{2,0},{3,1},{4,6},{5,7},{6,4},{7,5},{8,10},{9,11},{10,... | collective-permute-start | bytes 786440 | tf_op jit(solution)/shard_map/ppermute | solution.py:23
  84.3 10.3 %collective-permute-start.15 = (bf16[2,256,256]{1,2,0:T(8,128)(2,1)S(1)}, bf16[2,256,256]{1,2,0:T(8,128)(2,1)S(1)}, u32[]{:S(2)}, u32[]{:S(2)}) collective-permute-start(bf16[2,256,256]{1,2,0:T(8,128)(2,1)S(1)} %get-tuple-element.12), channel_id=1, source_target_pairs={{0,2},{1,3},{2,0},{3,1},{4,6},{5,7},{6,4},{7,5},{8,10},{9,11},{10,... | collective-permute-start | bytes 786440 | tf_op jit(solution)/shard_map/ppermute | solution.py:23
  89.9 9.3 %collective-permute-start.5 = (bf16[2,256,256]{1,2,0:T(8,128)(2,1)S(1)}, bf16[2,256,256]{1,2,0:T(8,128)(2,1)S(1)}, u32[]{:S(2)}, u32[]{:S(2)}) collective-permute-start(bf16[2,256,256]{1,2,0:T(8,128)(2,1)S(1)} %get-tuple-element.10), channel_id=1, source_target_pairs={{0,2},{1,3},{2,0},{3,1},{4,6},{5,7},{6,4},{7,5},{8,10},{9,11},{10,... | collective-permute-start | bytes 786440 | tf_op jit(solution)/shard_map/ppermute | solution.py:23
  94.6 6.5 %collective-permute-start.16 = (bf16[2,256,2,256]{1,3,0,2:T(8,128)(2,1)S(1)}, bf16[2,256,2,256]{1,3,0,2:T(8,128)(2,1)S(1)}, u32[]{:S(2)}, u32[]{:S(2)}) collective-permute-start(bf16[2,256,2,256]{1,3,0,2:T(8,128)(2,1)S(1)} %maximum_select_fusion.8), channel_id=1, source_target_pairs={{0,1},{1,0},{2,3},{3,2},{4,5},{5,4},{6,7},{7,6},{8,9},{9,8},{10,11... | collective-permute-start | bytes 1572872 | tf_op jit(solution)/shard_map/ppermute | solution.py:23
  100.1 18.1 %collective-permute-start.6 = (bf16[2,256,2,256]{1,3,0,2:T(8,128)(2,1)}, bf16[2,256,2,256]{1,3,0,2:T(8,128)(2,1)}, u32[]{:S(2)}, u32[]{:S(2)}) collective-permute-start(bf16[2,256,2,256]{1,3,0,2:T(8,128)(2,1)} %maximum_select_fusion.5), channel_id=1, source_target_pairs={{0,1},{1,0},{2,3},{3,2},{4,5},{5,4},{6,7},{7,6},{8,9},{9,8},{10,11... | collective-permute-start | bytes 1572872 | tf_op jit(solution)/shard_map/ppermute | solution.py:23
  102.2 16.1 %copy-start.9 = (bf16[2,256,2,1,256]{1,4,0,2,3:T(8,128)(2,1)S(1)}, bf16[2,256,2,1,256]{1,4,0,2,3:T(8,128)(2,1)}, u32[]{:S(2)}) copy-start(bf16[2,256,2,1,256]{1,4,0,2,3:T(8,128)(2,1)} %fusion.50) | copy-start | bytes 1572868
  107.8 33.3 %collective-permute-start.17 = (bf16[2,256,1024]{2,1,0:T(8,128)(2,1)}, bf16[2,256,1024]{2,1,0:T(8,128)(2,1)}, u32[]{:S(2)}, u32[]{:S(2)}) collective-permute-start(bf16[2,256,1024]{2,1,0:T(8,128)(2,1)} %get-tuple-element.57), channel_id=1, source_target_pairs={{0,4},{1,5},{2,6},{3,7},{12,8},{13,9},{14,10},{15,11},{16,20},{17,... | collective-permute-start | bytes 3145736 | tf_op jit(solution)/shard_map/ppermute | solution.py:19
  135.7 27.4 %collective-permute-start.7 = (bf16[2,256,1024]{2,1,0:T(8,128)(2,1)S(1)}, bf16[2,256,1024]{2,1,0:T(8,128)(2,1)S(1)}, u32[]{:S(2)}, u32[]{:S(2)}) collective-permute-start(bf16[2,256,1024]{2,1,0:T(8,128)(2,1)S(1)} %get-tuple-element.55), channel_id=1, source_target_pairs={{0,4},{1,5},{2,6},{3,7},{12,8},{13,9},{14,10},{15,11},{16,20},{17,... | collective-permute-start | bytes 3145736 | tf_op jit(solution)/shard_map/ppermute | solution.py:19
  142.7 21.5 %collective-permute-start.18 = (bf16[2,256,1024]{2,1,0:T(8,128)(2,1)S(1)}, bf16[2,256,1024]{2,1,0:T(8,128)(2,1)S(1)}, u32[]{:S(2)}, u32[]{:S(2)}) collective-permute-start(bf16[2,256,1024]{2,1,0:T(8,128)(2,1)S(1)} %fusion.48), channel_id=1, source_target_pairs={{4,8},{5,9},{6,10},{7,11},{8,4},{9,5},{10,6},{11,7},{20,24},{21,25... | collective-permute-start | bytes 3145736 | tf_op jit(solution)/shard_map/ppermute | solution.py:19
  163.5 2.4 collective-permute-start.8
  164.6 30.2 %collective-permute-start.19 = (bf16[2,256,1024]{2,1,0:T(8,128)(2,1)S(1)}, bf16[2,256,1024]{2,1,0:T(8,128)(2,1)S(1)}, u32[]{:S(2)}, u32[]{:S(2)}) collective-permute-start(bf16[2,256,1024]{2,1,0:T(8,128)(2,1)S(1)} %fusion.18), channel_id=1, source_target_pairs={{4,0},{5,1},{6,2},{7,3},{8,12},{9,13},{10,14},{11,15},{20,16},{21,... | collective-permute-start | bytes 3145736 | tf_op jit(solution)/shard_map/ppermute | solution.py:19
  166.3 51.5 %collective-permute-start.9 = (bf16[2,256,1024]{2,1,0:T(8,128)(2,1)S(1)}, bf16[2,256,1024]{2,1,0:T(8,128)(2,1)S(1)}, u32[]{:S(2)}, u32[]{:S(2)}) collective-permute-start(bf16[2,256,1024]{2,1,0:T(8,128)(2,1)S(1)} %fusion.15), channel_id=1, source_target_pairs={{4,0},{5,1},{6,2},{7,3},{8,12},{9,13},{10,14},{11,15},{20,16},{21,... | collective-permute-start | bytes 3145736 | tf_op jit(solution)/shard_map/ppermute | solution.py:19
  224.9 4.6 %collective-permute-start.22 = (f32[2,256,2,256]{1,3,0,2:T(8,128)S(1)}, f32[2,256,2,256]{1,3,0,2:T(8,128)S(1)}, u32[]{:S(2)}, u32[]{:S(2)}) collective-permute-start(f32[2,256,2,256]{1,3,0,2:T(8,128)S(1)} %select_bitcast_fusion), channel_id=1, source_target_pairs={{0,1},{1,0},{2,3},{3,2},{4,5},{5,4},{6,7},{7,6},{8,9},{9,8},{10,11... | collective-permute-start | bytes 3145736 | tf_op jit(solution)/shard_map/ppermute | solution.py:23
  229.4 2.7 %collective-permute-start.20 = (f32[2,256,2,256]{1,3,0,2:T(8,128)S(1)}, f32[2,256,2,256]{1,3,0,2:T(8,128)S(1)}, u32[]{:S(2)}, u32[]{:S(2)}) collective-permute-start(f32[2,256,2,256]{1,3,0,2:T(8,128)S(1)} %select_bitcast_fusion.1), channel_id=1, source_target_pairs={{0,1},{1,0},{2,3},{3,2},{4,5},{5,4},{6,7},{7,6},{8,9},{9,8},{10,11... | collective-permute-start | bytes 3145736 | tf_op jit(solution)/shard_map/ppermute | solution.py:23
  230.5 9.3 %collective-permute-start.23 = (bf16[2,256,256]{1,2,0:T(8,128)(2,1)}, bf16[2,256,256]{1,2,0:T(8,128)(2,1)S(1)}, u32[]{:S(2)}, u32[]{:S(2)}) collective-permute-start(bf16[2,256,256]{1,2,0:T(8,128)(2,1)} %fusion.64), channel_id=1, source_target_pairs={{0,2},{1,3},{2,0},{3,1},{4,6},{5,7},{6,4},{7,5},{8,10},{9,11},{10,... | collective-permute-start | bytes 786440 | tf_op jit(solution)/shard_map/ppermute | solution.py:23
  233.1 12.0 %collective-permute-start.21 = (bf16[2,256,256]{1,2,0:T(8,128)(2,1)}, bf16[2,256,256]{1,2,0:T(8,128)(2,1)}, u32[]{:S(2)}, u32[]{:S(2)}) collective-permute-start(bf16[2,256,256]{1,2,0:T(8,128)(2,1)} %fusion.63), channel_id=1, source_target_pairs={{0,2},{1,3},{2,0},{3,1},{4,6},{5,7},{6,4},{7,5},{8,10},{9,11},{10,... | collective-permute-start | bytes 786440 | tf_op jit(solution)/shard_map/ppermute | solution.py:23
  248.1 17.8 %copy-start.13 = (f32[2,256,256]{1,2,0:T(8,128)S(1)}, f32[2,256,256]{1,2,0:T(8,128)}, u32[]{:S(2)}) copy-start(f32[2,256,256]{1,2,0:T(8,128)} %get-tuple-element.11) | copy-start | bytes 1572868
  248.2 1.2 collective-permute-start.24
  249.5 3.7 %collective-permute-start.25 = (f32[2,8,128]{2,1,0:T(8,128)S(1)}, f32[2,8,128]{2,1,0:T(8,128)S(1)}, u32[]{:S(2)}, u32[]{:S(2)}) collective-permute-start(f32[2,8,128]{2,1,0:T(8,128)S(1)} %broadcast_add_fusion), channel_id=1, source_target_pairs={{0,2},{1,3},{2,0},{3,1},{4,6},{5,7},{6,4},{7,5},{8,10},{9,11},{10,... | collective-permute-start | bytes 24584 | tf_op jit(solution)/shard_map/ppermute | solution.py:23
  253.2 3.7 %collective-permute-start.26 = (f32[2,8,128]{2,1,0:T(8,128)S(1)}, f32[2,8,128]{2,1,0:T(8,128)S(1)}, u32[]{:S(2)}, u32[]{:S(2)}) collective-permute-start(f32[2,8,128]{2,1,0:T(8,128)S(1)} %fusion.86), channel_id=1, source_target_pairs={{0,4},{1,5},{2,6},{3,7},{4,0},{5,1},{6,2},{7,3},{8,12},{9,13},{10,... | collective-permute-start | bytes 24584 | tf_op jit(solution)/shard_map/ppermute | solution.py:23
  256.8 4.5 %collective-permute-start.27 = (f32[2,8,128]{2,1,0:T(8,128)S(1)}, f32[2,8,128]{2,1,0:T(8,128)S(1)}, u32[]{:S(2)}, u32[]{:S(2)}) collective-permute-start(f32[2,8,128]{2,1,0:T(8,128)S(1)} %add.131), channel_id=1, source_target_pairs={{0,8},{1,9},{2,10},{3,11},{4,12},{5,13},{6,14},{7,15},{8,0},{9,1},... | collective-permute-start | bytes 24584 | tf_op jit(solution)/shard_map/ppermute | solution.py:23
  (12 other events, 35.8 us)

commit v2 on v1

v2 whole, which is shorter than its diff:
```python
import functools

import jax
import jax.numpy as jnp
from jax import lax
from jax.experimental import pallas as pl
from jax.experimental.pallas import tpu as pltpu
from jax.sharding import PartitionSpec as P

ROWS = 4
COLS = 4
TEAM = ROWS * COLS
SPLIT = 2
DIRECT = 4
LAG = {"R": 2, "I": 1, "D": 2, "H": 1, "A": 3, "B": 4, "C": 5, "K": 6, "J": 5}

f32, bf16 = jnp.float32, jnp.bfloat16
VMEM = pl.BlockSpec(memory_space=pltpu.VMEM)
SMEM = pl.BlockSpec(memory_space=pltpu.SMEM)
ANY = pl.BlockSpec(memory_space=pl.ANY)
shape = jax.ShapeDtypeStruct


def team_pairs(pairs):
    groups = lax.axis_size("freq") // TEAM
    return [(TEAM * g + a, TEAM * g + b) for g in range(groups) for a, b in pairs]


def along_columns(value, moves):
    pairs = [(ROWS * a + r, ROWS * b + r) for a, b in moves for r in range(ROWS)]
    return lax.ppermute(value, "freq", team_pairs(pairs))


def swap(value, bit):
    return lax.ppermute(value, "freq", team_pairs([(d, d ^ (1 << bit)) for d in range(TEAM)]))


NEIGHBOURS = [(0, 1), (1, 0), (2, 3), (3, 2)]
INWARD = [(0, 1), (3, 2)]
MIDDLE = [(1, 2), (2, 1)]
OUTWARD = [(1, 0), (2, 3)]


def product(left, right):
    return lax.dot_general(left, right, (((1,), (0,)), ((), ())), preferred_element_type=f32)


def product_transposed(left, right):
    return lax.dot_general(left, right, (((1,), (1,)), ((), ())), preferred_element_type=f32)


def multiply_columns(f, core, left, matrix, keep, *sends):
    count = left.shape[0] // 2
    width = keep.shape[-1]
    for which, outs in ((1 - core, sends), (core, [keep.at[half] for half in range(2)])):
        for half, out in enumerate(outs):
            cols = pl.ds(pl.multiple_of((2 * half + which) * width, width), width)
            with_real = product(left, matrix[f, 0, :, cols])
            with_imag = product(left, matrix[f, 1, :, cols])
            out[0] = with_real[:count] - with_imag[count:]
            out[1] = with_imag[:count] + with_real[count:]


def prepare_kernel(chunks, where, current, scales, *outs):
    core, y, col, group = where[0], where[1], where[2], where[3]
    freqs, _, _, depth = current.shape
    own_scales, outs = outs[0], outs[1:]
    cols = pl.ds(pl.multiple_of((2 * y + core) * depth, depth), depth)
    for f in range(freqs):
        own_scales[f : f + 1, :] = scales[pl.ds(group * freqs + f, 1), cols]
    for (f, start, size), out in zip(chunks, outs):
        for c in range(2):
            rows = current[f, c, start : start + size, :]
            out[c] = (rows * own_scales[f : f + 1, :]).astype(bf16)


def stack_kernel(where, own, other, out):
    out[0] = own[...]
    out[1] = other[...]


def image_kernel(f, direct, where, own, one, two, three, matrix, keep, *refs):
    core, col = where[0], where[2]
    *sends, left = refs
    left[:, col] = own[...]
    if direct:
        for k, ref in ((1, one), (2, two), (3, three)):
            left[:, lax.rem(col + COLS - k, COLS)] = ref[...]
    else:
        left[:, col + 1 - 2 * lax.rem(col, 2)] = one[...]
        low = (col < 2).astype(jnp.int32)
        for s in range(2):
            left[:, low * (2 + s) + (1 - low) * (1 - s)] = two[s] + three[s]
    rows = 2 * COLS * own.shape[1]
    multiply_columns(f, core, left[...].reshape(rows, own.shape[2]), matrix, keep, *sends)


def half_kernel(where, keep, lower, upper, low):
    for half, got in enumerate((lower, upper)):
        low[half] = (keep[half] + got[...]).astype(bf16)


def residual_kernel(f, start, size, where, keep, lower, upper, far, data, other_data, low, residual):
    y = where[1]
    slab = data.shape[2] // COLS
    for half, got in enumerate((lower, upper)):
        for source, mine in ((data, True), (other_data, False)):

            @pl.when((y == half) == mine)
            def _(half=half, got=got, source=source, mine=mine):
                for c in range(2):
                    for s in range(COLS):
                        rows = pl.ds(s * size, size)
                        image = (keep[half, c, rows] + got[c, rows]) + far[half, c, rows].astype(f32)
                        value = source[f, c, pl.ds(s * slab + start, size)] - image
                        low[half, c, rows] = value.astype(bf16)
                        if mine:
                            residual[c, rows] = value


def descent_kernel(f, where, own, other, matrix, low, part, left):
    core = where[0]
    count, width = own.shape[2], own.shape[3]
    for half in range(2):
        for which, ref in ((core, own), (1 - core, other)):
            cols = pl.ds(pl.multiple_of((2 * half + which) * width, width), width)
            left[:, cols] = ref[half].reshape(2 * count, width)
    depth = matrix.shape[2]
    tile = depth // 4
    for k in range(4):
        rows = pl.ds(k * tile, tile)
        with_real = product_transposed(left[...], matrix[f, 0, rows, :])
        with_imag = product_transposed(left[...], matrix[f, 1, rows, :])
        real = with_real[:count] + with_imag[count:]
        imag = with_real[count:] - with_imag[:count]
        part[0, :, rows], part[1, :, rows] = real, imag
        low[0, :, rows], low[1, :, rows] = real.astype(bf16), imag.astype(bf16)


def add_kernel(where, part, got, out):
    out[...] = (part[...] + got[...].astype(f32)).astype(bf16)


def curvature_kernel(f, where, part, first, second, third, scale, matrix, keep, *refs):
    core, col = where[0], where[2]
    *sends, own, left = refs
    count, depth = part.shape[1], part.shape[2]
    piece = own.shape[1]
    row_scale = scale[f : f + 1, :]

    def descent(c, rows):
        inner = part[c, rows] + first[c, rows].astype(f32)
        outer = second[c, rows].astype(f32) + third[c, rows].astype(f32)
        return (inner + outer) * row_scale

    for c in range(2):
        left[c] = (descent(c, pl.ds(0, count)) * row_scale).astype(bf16)
        own[c] = descent(c, pl.ds(pl.multiple_of(col * piece, piece), piece))
    multiply_columns(f, core, left[...].reshape(2 * count, depth), matrix, keep, *sends)


def bend_half_kernel(where, keep, lower, upper, low):
    for half, got in enumerate((lower, upper)):

        @pl.when(where[1] != half)
        def _(half=half, got=got):
            low[...] = (keep[half] + got[...]).astype(bf16)


def squares(value):
    return jnp.sum((value * value).reshape(-1, 8, 128), axis=0)


def bend_kernel(where, keep, lower, upper, far, own, sums, out_sums, curvature):
    for half, got in enumerate((lower, upper)):

        @pl.when(where[1] == half)
        def _(half=half, got=got):
            curvature[...] = (keep[half] + got[...]) + far[...].astype(f32)

    value = curvature[...]
    out_sums[0] = sums[0] + squares(own[...])
    out_sums[1] = sums[1] + squares(value)


def update_kernel(chunks, where, sums, current, *refs):
    n = len(chunks)
    descents, residuals, curvatures = refs[:n], refs[n : 2 * n], refs[2 * n : 3 * n]
    new_iterate, new_residual = refs[3 * n :]
    total = sums[...]
    step = jnp.sum(total[0], keepdims=True) / jnp.sum(total[1], keepdims=True)
    slab = new_residual.shape[3] // COLS
    for (f, start, size), descent, residual, curvature in zip(
        chunks, descents, residuals, curvatures
    ):
        for c in range(2):
            rows = pl.ds(start, size)
            new_iterate[0, f, c, rows] = current[f, c, rows] + step * descent[c]
            for s in range(COLS):
                rows = pl.ds(s * size, size)
                new_residual[0, f, c, pl.ds(s * slab + start, size)] = (
                    residual[c, rows] - step * curvature[c, rows]
                )


class Chain:
    def __init__(self, where):
        self.where = where
        self.last = None

    def __call__(self, kernel, name, out_shape, *operands, scratch=(), flops=0):
        token = [] if self.last is None else [self.last]

        def run(where, *refs):
            return kernel(where, *refs[len(token) :])

        results = pl.pallas_call(
            run,
            in_specs=[SMEM] + [ANY] * len(token) + [VMEM] * len(operands),
            out_specs=[VMEM] * len(out_shape),
            out_shape=out_shape,
            scratch_shapes=list(scratch),
            name=name,
            cost_estimate=pl.CostEstimate(
                flops=0, bytes_accessed=1024, transcendentals=0
            ),
            compiler_params=pltpu.CompilerParams(vmem_limit_bytes=32 << 20),
        )(self.where, *token, *operands)
        self.last = results[0]
        return results


def body(spectrum, blocks, scales, iterate):
    index = lax.axis_index("freq")
    where = jnp.stack([index % 2, index // 2 % 2, index // ROWS % COLS, index // TEAM])
    matrix, current, data = blocks[0], iterate[0], spectrum[0]
    freqs, _, row_len, col_len = matrix.shape
    slab, width = current.shape[2], data.shape[3]
    size = slab // SPLIT
    count = COLS * size
    flops = 8 * count * row_len * col_len
    chunks = [(f, h * size, size) for f in range(freqs) for h in range(SPLIT)]
    chain = Chain(where.astype(jnp.int32))

    other_data = swap(data, 1)
    own_scales, *owns = chain(
        functools.partial(prepare_kernel, chunks),
        "prepare",
        [shape((freqs, row_len), f32)] + [shape((2, s, row_len), bf16) for _, _, s in chunks],
        current,
        scales,
    )
    forward = [shape((2, 2, count, width), f32)] + [shape((2, count, width), f32)] * 2
    values = [{} for _ in chunks]
    totals = [jnp.zeros((2, 8, 128), f32)]

    for n, own in enumerate(owns):
        v = values[n]
        if n < DIRECT:
            shifts = [[(a, (a + k) % COLS) for a in range(COLS)] for k in (1, 2, 3)]
            v["x"] = (own, *(along_columns(own, moves) for moves in shifts))
        else:
            v["x"] = (own, along_columns(own, NEIGHBOURS))

    def step(kind, n):
        f, start, rows = chunks[n]
        v = values[n]
        if kind == "S" and n >= DIRECT:
            own, other = v["x"]
            (pair,) = chain(stack_kernel, "pair", [shape((2, *own.shape), bf16)], own, other)
            far_hub = along_columns(pair, MIDDLE)
            v["x"] = (own, other, far_hub, along_columns(far_hub, OUTWARD))
        elif kind == "I":
            v["keep"], *sends = chain(
                functools.partial(image_kernel, f, n < DIRECT),
                "image",
                forward,
                *v["x"],
                matrix,
                scratch=[pltpu.VMEM((2, COLS, rows, row_len), bf16)],
                flops=flops,
            )
            v["got"] = [swap(send, 0) for send in sends]
        elif kind == "H":
            (low,) = chain(half_kernel, "half", [shape((2, 2, count, width), bf16)], v["keep"], *v["got"])
            v["far"] = swap(low, 1)
        elif kind == "R":
            v["low"], v["residual"] = chain(
                functools.partial(residual_kernel, f, start, rows),
                "residual",
                [shape((2, 2, count, width), bf16), shape((2, count, width), f32)],
                v["keep"],
                *v["got"],
                v["far"],
                data,
                other_data,
            )
            v["other_low"] = swap(v["low"], 0)
        elif kind == "D":
            low, v["part"] = chain(
                functools.partial(descent_kernel, f),
                "descent",
                [shape((2, count, row_len), bf16), shape((2, count, row_len), f32)],
                v["low"],
                v["other_low"],
                matrix,
                scratch=[pltpu.VMEM((2 * count, col_len), bf16)],
                flops=flops,
            )
            v["first"] = along_columns(low, INWARD)
        elif kind in "AB":
            name, source, moves = (
                ("second", "first", MIDDLE) if kind == "A" else ("third", "second", OUTWARD)
            )
            (low,) = chain(add_kernel, "add", [shape((2, count, row_len), bf16)], v["part"], v[source])
            v[name] = along_columns(low, moves)
        elif kind == "C":
            v["keep"], *sends, v["own"] = chain(
                functools.partial(curvature_kernel, f),
                "curvature",
                forward + [shape((2, rows, row_len), f32)],
                v["part"],
                v["first"],
                v["second"],
                v["third"],
                own_scales,
                matrix,
                scratch=[pltpu.VMEM((2, count, row_len), bf16)],
                flops=flops,
            )
            v["got"] = [swap(send, 0) for send in sends]
        elif kind == "J":
            (low,) = chain(
                bend_half_kernel, "bend_half", [shape((2, count, width), bf16)], v["keep"], *v["got"]
            )
            v["far"] = swap(low, 1)
        elif kind == "K":
            totals[0], v["curvature"] = chain(
                bend_kernel,
                "bend",
                [shape((2, 8, 128), f32), shape((2, count, width), f32)],
                v["keep"],
                *v["got"],
                v["far"],
                v["own"],
                totals[0],
            )

    for turn in range(max(LAG.values()) + len(chunks)):
        for kind, lag in LAG.items():
            if 0 <= turn - lag < len(chunks):
                step(kind, turn - lag)

    sums = totals[0]
    for bit in range(4):
        sums = sums + swap(sums, bit)
    return chain(
        functools.partial(update_kernel, chunks),
        "update",
        [shape(iterate.shape, f32), shape(spectrum.shape, f32)],
        sums,
        current,
        *(v[name] for name in ("own", "residual", "curvature") for v in values),
    )


def solution(mesh):
    placed = P(("parts", "freq"), None, None, None, None)
    return jax.shard_map(
        body,
        mesh=mesh,
        in_specs=(placed, P("freq", None, None, None, None), P(), placed),
        out_specs=(placed, placed),
        check_vma=False,
    )
```

time: 271 us -> 178 us (0.66)
  waiting for transfers between devices: 125 us -> 64.2 us
  Pallas kernels: 0 us -> 41.5 us
  other arithmetic: 41.2 us -> 0.09 us
  local copies, waits for them, and re-layouts: 43.8 us -> 5.38 us
  starting transfers between devices: 34.6 us -> 64.7 us
  matrix products: 19.6 us -> 0 us
  between operations: 5.26 us -> 1.25 us
    ppermute x12 -> x24, waiting for transfers between devices: 93.4 us -> 29.1 us  [along_columns(): return lax.ppermute(value, 'freq', team_pairs(pairs))]
    pallas_call x0 -> x38, Pallas kernels: none -> 41.5 us  [__call__(): pl.pallas_call(run, in_specs=[SMEM] + [ANY] * len(token) + [VMEM] * len(o...]
    ppermute x12 -> x24, starting transfers between devices: 23.1 us -> 47.1 us  [along_columns(): return lax.ppermute(value, 'freq', team_pairs(pairs))]
    dot_general x6 -> x0, matrix products: 19.6 us -> none  [the longest x2 10.1 us: adjoint_product(): lax.dot_general(left, matrix, (((2, 3), (0, 2)), ((), ())), preferred_ele...]
    dot_general x3 -> x0, local copies, waits for them, and re-layouts: 18.5 us -> none  [forward_product(): lax.dot_general(left, matrix, (((2, 3), (0, 1)), ((), ())), preferred_ele...]
    convert_element_type x14 -> x0, other arithmetic: 13.3 us -> none  [the longest x2 5.65 us: body(): lifted = (descent * own_scales[f]).astype(bf16)]
    slice x11 -> x0, local copies, waits for them, and re-layouts: 7.65 us -> none  [the longest x6 3.76 us: adjoint_product(): real, imag = (field[0], field[1])]
    unnamed x35 -> x12, local copies, waits for them, and re-layouts: 12.9 us -> 5.38 us
  transfers between devices with their start and end apart: 28 -> 57, of which waited for: 19 -> 25; matrix products, arithmetic and copies ran while one was open for 28% -> 0% of each run, Pallas kernels for 0% -> 20%
where the time goes in v2:
time: 178 us; the launch traced here: 177 us
  starting transfers between devices  64.7 us (36%)
  waiting for transfers between devices  64.2 us (36%)
  Pallas kernels  41.5 us (23%)
  local copies, waits for them, and re-layouts  5.38 us (3%)
    ppermute x24, starting transfers between devices, along_columns(): return lax.ppermute(value, 'freq', team_pairs(pairs))  47.1 us
    pallas_call x38, Pallas kernels, __call__(): pl.pallas_call(run, in_specs=[SMEM] + [ANY] * len(token) + [VMEM] * len(o...  41.5 us
    ppermute x33, waiting for transfers between devices, swap(): lax.ppermute(value, 'freq', team_pairs([(d, d ^ 1 << bit) for d in range(...  35 us
    ppermute x24, waiting for transfers between devices, along_columns(): return lax.ppermute(value, 'freq', team_pairs(pairs))  29.1 us
    ppermute x33, starting transfers between devices, swap(): lax.ppermute(value, 'freq', team_pairs([(d, d ^ 1 << bit) for d in range(...  17.6 us
    unnamed x12, local copies, waits for them, and re-layouts  5.38 us
  transfers between devices with their start and end apart: 57, of which 25 were waited for; matrix products, arithmetic and copies ran while one was open for 0% of the time, Pallas kernels for 20%

profile of v2, /device:TPU:0, one launch (start us, length us, event | category | flops | bytes accessed | tf_op | source)
XLA Modules:
  0.0 177.1 jit_solution(12376200120815438296)
XLA Ops:
  0.6 3.0 %collective-permute-start.6 = (f32[2,2,256,256]{3,2,1,0:T(8,128)}, f32[2,2,256,256]{3,2,1,0:T(8,128)S(1)}, u32[]{:S(2)}, u32[]{:S(2)}) collective-permute-start(f32[2,2,256,256]{3,2,1,0:T(8,128)} %bitcast.19), channel_id=1, source_target_pairs={{0,2},{1,3},{2,0},{3,1},{4,6},{5,7},{6,4},{7,5},{8,10},{9,11},{10,... | collective-permute-start | bytes 3145736 | tf_op jit(solution)/shard_map/ppermute | solution.py:35
  8.0 2.6 %collective-permute-start.1 = (bf16[2,32,1024]{2,1,0:T(8,128)(2,1)S(1)}, bf16[2,32,1024]{2,1,0:T(8,128)(2,1)S(1)}, u32[]{:S(2)}, u32[]{:S(2)}) collective-permute-start(bf16[2,32,1024]{2,1,0:T(8,128)(2,1)S(1)} %get-tuple-element.60.refs_1_), channel_id=1, source_target_pairs={{0,8},{1,9},{2,10},{3,11},{4,12},{5,13},{6,14},{7,15},{8,0},{9,1},... | collective-permute-start | bytes 393224 | tf_op jit(solution)/shard_map/ppermute | solution.py:31
  11.9 2.8 %collective-permute-done.refs_2_ = bf16[2,32,1024]{2,1,0:T(8,128)(2,1)S(1)} collective-permute-done((bf16[2,32,1024]{2,1,0:T(8,128)(2,1)S(1)}, bf16[2,32,1024]{2,1,0:T(8,128)(2,1)S(1)}, u32[]{:S(2)}, u32[]{:S(2)}) %collective-permute-start) | collective-permute-done | bytes 131104 | tf_op jit(solution)/shard_map/ppermute | solution.py:31
  14.7 4.3 %collective-permute-done.1.refs_3_ = bf16[2,32,1024]{2,1,0:T(8,128)(2,1)S(1)} collective-permute-done((bf16[2,32,1024]{2,1,0:T(8,128)(2,1)S(1)}, bf16[2,32,1024]{2,1,0:T(8,128)(2,1)S(1)}, u32[]{:S(2)}, u32[]{:S(2)}) %collective-permute-start.1) | collective-permute-done | bytes 131104 | tf_op jit(solution)/shard_map/ppermute | solution.py:31
  19.0 3.4 %copy-done = bf16[1,2,2,1024,1024]{4,3,2,1,0:T(8,128)(2,1)S(1)} copy-done((bf16[1,2,2,1024,1024]{4,3,2,1,0:T(8,128)(2,1)S(1)}, bf16[1,2,2,1024,1024]{4,3,2,1,0:T(8,128)(2,1)}, u32[]{:S(2)}) %copy-start) | copy-done | bytes 8388632
  27.4 3.3 %collective-permute-start.7 = (bf16[2,32,1024]{2,1,0:T(8,128)(2,1)S(1)}, bf16[2,32,1024]{2,1,0:T(8,128)(2,1)S(1)}, u32[]{:S(2)}, u32[]{:S(2)}) collective-permute-start(bf16[2,32,1024]{2,1,0:T(8,128)(2,1)S(1)} %get-tuple-element.65.refs_1_), channel_id=1, source_target_pairs={{0,4},{1,5},{2,6},{3,7},{4,8},{5,9},{6,10},{7,11},{8,12},{9,13},{1... | collective-permute-start | bytes 393224 | tf_op jit(solution)/shard_map/ppermute | solution.py:31
  33.0 2.2 %collective-permute-done.5.refs_4_ = bf16[2,2,128,256]{3,2,1,0:T(8,128)(2,1)S(1)} collective-permute-done((bf16[2,2,128,256]{3,2,1,0:T(8,128)(2,1)S(1)}, bf16[2,2,128,256]{3,2,1,0:T(8,128)(2,1)S(1)}, u32[]{:S(2)}, u32[]{:S(2)}) %collective-permute-start.5) | collective-permute-done | bytes 262176 | tf_op jit(solution)/shard_map/ppermute | solution.py:35
  36.1 4.8 %collective-permute-done.8.refs_3_ = bf16[2,32,1024]{2,1,0:T(8,128)(2,1)S(1)} collective-permute-done((bf16[2,32,1024]{2,1,0:T(8,128)(2,1)S(1)}, bf16[2,32,1024]{2,1,0:T(8,128)(2,1)S(1)}, u32[]{:S(2)}, u32[]{:S(2)}) %collective-permute-start.8) | collective-permute-done | bytes 131104 | tf_op jit(solution)/shard_map/ppermute | solution.py:31
  41.0 1.9 %image.5 = (f32[2,2,128,256]{3,2,1,0:T(8,128)S(1)}, f32[2,128,256]{2,1,0:T(8,128)S(1)}, f32[2,128,256]{2,1,0:T(8,128)S(1)}) custom-call(s32[4]{0:T(128)S(1)} %pad_add_fusion.where, bf16[2,2,128,256]{3,2,1,0:T(8,128)(2,1)S(1)} %get-tuple-element.64.refs_0_.refs_1_, bf16[2,32,1024]{2,1,0:T(8,128)(2,1)S(1)} %get-tuple-element.65.refs_1_, ...), custom_call_target="tpu_custom_call" | custom-call | bytes 1024 | tf_op jit(solution)/shard_map/image/pallas_call | solution.py:217
  47.5 3.3 %collective-permute-start.14 = (bf16[2,32,1024]{2,1,0:T(8,128)(2,1)S(1)}, bf16[2,32,1024]{2,1,0:T(8,128)(2,1)S(1)}, u32[]{:S(2)}, u32[]{:S(2)}) collective-permute-start(bf16[2,32,1024]{2,1,0:T(8,128)(2,1)S(1)} %get-tuple-element.71.refs_1_), channel_id=1, source_target_pairs={{0,4},{1,5},{2,6},{3,7},{4,8},{5,9},{6,10},{7,11},{8,12},{9,13},{1... | collective-permute-start | bytes 393224 | tf_op jit(solution)/shard_map/ppermute | solution.py:31
  53.2 2.9 %collective-permute-start.20 = (bf16[2,128,1024]{2,1,0:T(8,128)(2,1)S(1)}, bf16[2,128,1024]{2,1,0:T(8,128)(2,1)S(1)}, u32[]{:S(2)}, u32[]{:S(2)}) collective-permute-start(bf16[2,128,1024]{2,1,0:T(8,128)(2,1)S(1)} %get-tuple-element.67.refs_0_), channel_id=1, source_target_pairs={{0,4},{1,5},{2,6},{3,7},{12,8},{13,9},{14,10},{15,11},{16,20},{17,... | collective-permute-start | bytes 1572872 | tf_op jit(solution)/shard_map/ppermute | solution.py:31
  56.9 3.9 %collective-permute-done.15.refs_3_ = bf16[2,32,1024]{2,1,0:T(8,128)(2,1)S(1)} collective-permute-done((bf16[2,32,1024]{2,1,0:T(8,128)(2,1)S(1)}, bf16[2,32,1024]{2,1,0:T(8,128)(2,1)S(1)}, u32[]{:S(2)}, u32[]{:S(2)}) %collective-permute-start.15) | collective-permute-done | bytes 131104 | tf_op jit(solution)/shard_map/ppermute | solution.py:31
  66.2 3.3 %collective-permute-start.22 = (bf16[2,32,1024]{2,1,0:T(8,128)(2,1)S(1)}, bf16[2,32,1024]{2,1,0:T(8,128)(2,1)S(1)}, u32[]{:S(2)}, u32[]{:S(2)}) collective-permute-start(bf16[2,32,1024]{2,1,0:T(8,128)(2,1)S(1)} %get-tuple-element.78.refs_1_), channel_id=1, source_target_pairs={{0,4},{1,5},{2,6},{3,7},{4,8},{5,9},{6,10},{7,11},{8,12},{9,13},{1... | collective-permute-start | bytes 393224 | tf_op jit(solution)/shard_map/ppermute | solution.py:31
  71.9 3.9 %collective-permute-start.28 = (bf16[2,128,1024]{2,1,0:T(8,128)(2,1)S(1)}, bf16[2,128,1024]{2,1,0:T(8,128)(2,1)S(1)}, u32[]{:S(2)}, u32[]{:S(2)}) collective-permute-start(bf16[2,128,1024]{2,1,0:T(8,128)(2,1)S(1)} %get-tuple-element.73.refs_0_), channel_id=1, source_target_pairs={{0,4},{1,5},{2,6},{3,7},{12,8},{13,9},{14,10},{15,11},{16,20},{17,... | collective-permute-start | bytes 1572872 | tf_op jit(solution)/shard_map/ppermute | solution.py:31
  77.9 2.6 %collective-permute-done.23.refs_3_ = bf16[2,32,1024]{2,1,0:T(8,128)(2,1)S(1)} collective-permute-done((bf16[2,32,1024]{2,1,0:T(8,128)(2,1)S(1)}, bf16[2,32,1024]{2,1,0:T(8,128)(2,1)S(1)}, u32[]{:S(2)}, u32[]{:S(2)}) %collective-permute-start.23) | collective-permute-done | bytes 131104 | tf_op jit(solution)/shard_map/ppermute | solution.py:31
  86.3 5.3 %collective-permute-start.32 = (bf16[2,128,1024]{2,1,0:T(8,128)(2,1)S(1)}, bf16[2,128,1024]{2,1,0:T(8,128)(2,1)S(1)}, u32[]{:S(2)}, u32[]{:S(2)}) collective-permute-start(bf16[2,128,1024]{2,1,0:T(8,128)(2,1)S(1)} %get-tuple-element.80.refs_0_), channel_id=1, source_target_pairs={{0,4},{1,5},{2,6},{3,7},{12,8},{13,9},{14,10},{15,11},{16,20},{17,... | collective-permute-start | bytes 1572872 | tf_op jit(solution)/shard_map/ppermute | solution.py:31
  99.3 4.6 %collective-permute-start.37 = (bf16[2,128,1024]{2,1,0:T(8,128)(2,1)S(1)}, bf16[2,128,1024]{2,1,0:T(8,128)(2,1)S(1)}, u32[]{:S(2)}, u32[]{:S(2)}) collective-permute-start(bf16[2,128,1024]{2,1,0:T(8,128)(2,1)S(1)} %get-tuple-element.85.refs_0_), channel_id=1, source_target_pairs={{0,4},{1,5},{2,6},{3,7},{12,8},{13,9},{14,10},{15,11},{16,20},{17,... | collective-permute-start | bytes 1572872 | tf_op jit(solution)/shard_map/ppermute | solution.py:31
  109.0 2.0 %curvature.4 = (f32[2,2,128,256]{3,2,1,0:T(8,128)S(1)}, f32[2,128,256]{2,1,0:T(8,128)S(1)}, f32[2,128,256]{2,1,0:T(8,128)S(1)}, f32[2,32,1024]{2,1,0:T(8,128)S(1)}) custom-call(s32[4]{0:T(128)S(1)} %pad_add_fusion.where, bf16[2,128,1024]{2,1,0:T(8,128)(2,1)S(1)} %add.50.refs_0_, f32[2,128,1024]{2,1,0:T(8,128)S(1)} %get-tuple-element.76.refs_1_, ...), custom_call_target="tpu_custom_call" | custom-call | bytes 1024 | tf_op jit(solution)/shard_map/curvature/pallas_call | solution.py:217
  118.7 2.9 %collective-permute-done.39.refs_4_ = bf16[2,128,1024]{2,1,0:T(8,128)(2,1)S(1)} collective-permute-done((bf16[2,128,1024]{2,1,0:T(8,128)(2,1)S(1)}, bf16[2,128,1024]{2,1,0:T(8,128)(2,1)S(1)}, u32[]{:S(2)}, u32[]{:S(2)}) %collective-permute-start.39) | collective-permute-done | bytes 524320 | tf_op jit(solution)/shard_map/ppermute | solution.py:31
  121.5 2.0 %curvature.5 = (f32[2,2,128,256]{3,2,1,0:T(8,128)S(1)}, f32[2,128,256]{2,1,0:T(8,128)S(1)}, f32[2,128,256]{2,1,0:T(8,128)S(1)}, f32[2,32,1024]{2,1,0:T(8,128)S(1)}) custom-call(s32[4]{0:T(128)S(1)} %pad_add_fusion.where, bf16[2,128,1024]{2,1,0:T(8,128)(2,1)S(1)} %add.52.refs_0_, f32[2,128,1024]{2,1,0:T(8,128)S(1)} %get-tuple-element.83.refs_1_, ...), custom_call_target="tpu_custom_call" | custom-call | bytes 1024 | tf_op jit(solution)/shard_map/curvature/pallas_call | solution.py:217
  125.3 4.3 %collective-permute-done.40.refs_4_ = bf16[2,128,256]{2,1,0:T(8,128)(2,1)S(1)} collective-permute-done((bf16[2,128,256]{2,1,0:T(8,128)(2,1)S(1)}, bf16[2,128,256]{2,1,0:T(8,128)(2,1)S(1)}, u32[]{:S(2)}, u32[]{:S(2)}) %collective-permute-start.40) | collective-permute-done | bytes 131104 | tf_op jit(solution)/shard_map/ppermute | solution.py:35
  132.9 2.1 %collective-permute-done.44.refs_4_ = bf16[2,128,1024]{2,1,0:T(8,128)(2,1)S(1)} collective-permute-done((bf16[2,128,1024]{2,1,0:T(8,128)(2,1)S(1)}, bf16[2,128,1024]{2,1,0:T(8,128)(2,1)S(1)}, u32[]{:S(2)}, u32[]{:S(2)}) %collective-permute-start.44) | collective-permute-done | bytes 524320 | tf_op jit(solution)/shard_map/ppermute | solution.py:31
  135.0 2.0 %curvature.6 = (f32[2,2,128,256]{3,2,1,0:T(8,128)S(1)}, f32[2,128,256]{2,1,0:T(8,128)S(1)}, f32[2,128,256]{2,1,0:T(8,128)S(1)}, f32[2,32,1024]{2,1,0:T(8,128)S(1)}) custom-call(s32[4]{0:T(128)S(1)} %pad_add_fusion.where, bf16[2,128,1024]{2,1,0:T(8,128)(2,1)S(1)} %add.53.refs_0_, f32[2,128,1024]{2,1,0:T(8,128)S(1)} %get-tuple-element.86.refs_1_, ...), custom_call_target="tpu_custom_call" | custom-call | bytes 1024 | tf_op jit(solution)/shard_map/curvature/pallas_call | solution.py:217
  138.2 4.9 %collective-permute-done.45.refs_4_ = bf16[2,128,256]{2,1,0:T(8,128)(2,1)S(1)} collective-permute-done((bf16[2,128,256]{2,1,0:T(8,128)(2,1)S(1)}, bf16[2,128,256]{2,1,0:T(8,128)(2,1)S(1)}, u32[]{:S(2)}, u32[]{:S(2)}) %collective-permute-start.45) | collective-permute-done | bytes 131104 | tf_op jit(solution)/shard_map/ppermute | solution.py:35
  144.4 2.2 %collective-permute-done.48.refs_4_ = bf16[2,128,1024]{2,1,0:T(8,128)(2,1)S(1)} collective-permute-done((bf16[2,128,1024]{2,1,0:T(8,128)(2,1)S(1)}, bf16[2,128,1024]{2,1,0:T(8,128)(2,1)S(1)}, u32[]{:S(2)}, u32[]{:S(2)}) %collective-permute-start.48) | collective-permute-done | bytes 524320 | tf_op jit(solution)/shard_map/ppermute | solution.py:31
  146.6 2.0 %curvature.7 = (f32[2,2,128,256]{3,2,1,0:T(8,128)S(1)}, f32[2,128,256]{2,1,0:T(8,128)S(1)}, f32[2,128,256]{2,1,0:T(8,128)S(1)}, f32[2,32,1024]{2,1,0:T(8,128)S(1)}) custom-call(s32[4]{0:T(128)S(1)} %pad_add_fusion.where, bf16[2,128,256]{2,1,0:T(8,128)(2,1)S(1)} %bend_half.6.refs_0_, f32[2,128,1024]{2,1,0:T(8,128)S(1)} %get-tuple-element.90.refs_1_, ...), custom_call_target="tpu_custom_call" | custom-call | bytes 1024 | tf_op jit(solution)/shard_map/curvature/pallas_call | solution.py:217
  150.4 4.4 %collective-permute-done.49.refs_4_ = bf16[2,128,256]{2,1,0:T(8,128)(2,1)S(1)} collective-permute-done((bf16[2,128,256]{2,1,0:T(8,128)(2,1)S(1)}, bf16[2,128,256]{2,1,0:T(8,128)(2,1)S(1)}, u32[]{:S(2)}, u32[]{:S(2)}) %collective-permute-start.49) | collective-permute-done | bytes 131104 | tf_op jit(solution)/shard_map/ppermute | solution.py:35
  157.2 3.9 %collective-permute-done.52.refs_4_ = bf16[2,128,256]{2,1,0:T(8,128)(2,1)S(1)} collective-permute-done((bf16[2,128,256]{2,1,0:T(8,128)(2,1)S(1)}, bf16[2,128,256]{2,1,0:T(8,128)(2,1)S(1)}, u32[]{:S(2)}, u32[]{:S(2)}) %collective-permute-start.52) | collective-permute-done | bytes 131104 | tf_op jit(solution)/shard_map/ppermute | solution.py:35
  164.2 2.5 %collective-permute-done.54 = f32[2,8,128]{2,1,0:T(8,128)S(1)} collective-permute-done((f32[2,8,128]{2,1,0:T(8,128)S(1)}, f32[2,8,128]{2,1,0:T(8,128)S(1)}, u32[]{:S(2)}, u32[]{:S(2)}) %collective-permute-start.54) | collective-permute-done | bytes 8224 | tf_op jit(solution)/shard_map/ppermute | solution.py:35
  166.7 3.6 %collective-permute-done.55 = f32[2,8,128]{2,1,0:T(8,128)S(1)} collective-permute-done((f32[2,8,128]{2,1,0:T(8,128)S(1)}, f32[2,8,128]{2,1,0:T(8,128)S(1)}, u32[]{:S(2)}, u32[]{:S(2)}) %collective-permute-start.55) | collective-permute-done | bytes 8224 | tf_op jit(solution)/shard_map/ppermute | solution.py:35
  171.3 3.6 %collective-permute-done.56 = f32[2,8,128]{2,1,0:T(8,128)S(1)} collective-permute-done((f32[2,8,128]{2,1,0:T(8,128)S(1)}, f32[2,8,128]{2,1,0:T(8,128)S(1)}, u32[]{:S(2)}, u32[]{:S(2)}) %collective-permute-start.56) | collective-permute-done | bytes 8224 | tf_op jit(solution)/shard_map/ppermute | solution.py:35
  174.9 2.2 %update.1 = (f32[1,2,2,64,1024]{4,3,2,1,0:T(8,128)}, f32[1,2,2,256,256]{4,3,2,1,0:T(8,128)}) custom-call(s32[4]{0:T(128)S(1)} %pad_add_fusion.where, f32[2,8,128]{2,1,0:T(8,128)S(1)} %get-tuple-element.107.refs_0_, f32[2,8,128]{2,1,0:T(8,128)S(1)} %add.39.refs_1_, f32[2,2,64,1024]{3,2,1,0:T(8,128)S(1)} %bitcast.25, ...), custom_call_target="tpu_custom_call" | custom-call | bytes 1024 | tf_op jit(solution)/shard_map/update/pallas_call | solution.py:217
  (138 shorter events, 73.2 us)
Async XLA Ops:
  0.6 34.6 %collective-permute-start.6 = (f32[2,2,256,256]{3,2,1,0:T(8,128)}, f32[2,2,256,256]{3,2,1,0:T(8,128)S(1)}, u32[]{:S(2)}, u32[]{:S(2)}) collective-permute-start(f32[2,2,256,256]{3,2,1,0:T(8,128)} %bitcast.19), channel_id=1, source_target_pairs={{0,2},{1,3},{2,0},{3,1},{4,6},{5,7},{6,4},{7,5},{8,10},{9,11},{10,... | collective-permute-start | bytes 3145736 | tf_op jit(solution)/shard_map/ppermute | solution.py:35
  6.4 8.4 %collective-permute-start = (bf16[2,32,1024]{2,1,0:T(8,128)(2,1)S(1)}, bf16[2,32,1024]{2,1,0:T(8,128)(2,1)S(1)}, u32[]{:S(2)}, u32[]{:S(2)}) collective-permute-start(bf16[2,32,1024]{2,1,0:T(8,128)(2,1)S(1)} %get-tuple-element.60.refs_1_), channel_id=1, source_target_pairs={{0,4},{1,5},{2,6},{3,7},{4,8},{5,9},{6,10},{7,11},{8,12},{9,13},{1... | collective-permute-start | bytes 393224 | tf_op jit(solution)/shard_map/ppermute | solution.py:31
  8.0 11.0 %collective-permute-start.1 = (bf16[2,32,1024]{2,1,0:T(8,128)(2,1)S(1)}, bf16[2,32,1024]{2,1,0:T(8,128)(2,1)S(1)}, u32[]{:S(2)}, u32[]{:S(2)}) collective-permute-start(bf16[2,32,1024]{2,1,0:T(8,128)(2,1)S(1)} %get-tuple-element.60.refs_1_), channel_id=1, source_target_pairs={{0,8},{1,9},{2,10},{3,11},{4,12},{5,13},{6,14},{7,15},{8,0},{9,1},... | collective-permute-start | bytes 393224 | tf_op jit(solution)/shard_map/ppermute | solution.py:31
  10.6 8.4 %collective-permute-start.2 = (bf16[2,32,1024]{2,1,0:T(8,128)(2,1)S(1)}, bf16[2,32,1024]{2,1,0:T(8,128)(2,1)S(1)}, u32[]{:S(2)}, u32[]{:S(2)}) collective-permute-start(bf16[2,32,1024]{2,1,0:T(8,128)(2,1)S(1)} %get-tuple-element.60.refs_1_), channel_id=1, source_target_pairs={{0,12},{1,13},{2,14},{3,15},{4,0},{5,1},{6,2},{7,3},{8,4},{9,5},{1... | collective-permute-start | bytes 393224 | tf_op jit(solution)/shard_map/ppermute | solution.py:31
  26.9 8.4 %collective-permute-start.5 = (bf16[2,2,128,256]{3,2,1,0:T(8,128)(2,1)S(1)}, bf16[2,2,128,256]{3,2,1,0:T(8,128)(2,1)S(1)}, u32[]{:S(2)}, u32[]{:S(2)}) collective-permute-start(bf16[2,2,128,256]{3,2,1,0:T(8,128)(2,1)S(1)} %half.4.refs_0_), channel_id=1, source_target_pairs={{0,2},{1,3},{2,0},{3,1},{4,6},{5,7},{6,4},{7,5},{8,10},{9,11},{10,... | collective-permute-start | bytes 786440 | tf_op jit(solution)/shard_map/ppermute | solution.py:35
  27.4 8.8 %collective-permute-start.7 = (bf16[2,32,1024]{2,1,0:T(8,128)(2,1)S(1)}, bf16[2,32,1024]{2,1,0:T(8,128)(2,1)S(1)}, u32[]{:S(2)}, u32[]{:S(2)}) collective-permute-start(bf16[2,32,1024]{2,1,0:T(8,128)(2,1)S(1)} %get-tuple-element.65.refs_1_), channel_id=1, source_target_pairs={{0,4},{1,5},{2,6},{3,7},{4,8},{5,9},{6,10},{7,11},{8,12},{9,13},{1... | collective-permute-start | bytes 393224 | tf_op jit(solution)/shard_map/ppermute | solution.py:31
  30.7 10.3 %collective-permute-start.8 = (bf16[2,32,1024]{2,1,0:T(8,128)(2,1)S(1)}, bf16[2,32,1024]{2,1,0:T(8,128)(2,1)S(1)}, u32[]{:S(2)}, u32[]{:S(2)}) collective-permute-start(bf16[2,32,1024]{2,1,0:T(8,128)(2,1)S(1)} %get-tuple-element.65.refs_1_), channel_id=1, source_target_pairs={{0,8},{1,9},{2,10},{3,11},{4,12},{5,13},{6,14},{7,15},{8,0},{9,1},... | collective-permute-start | bytes 393224 | tf_op jit(solution)/shard_map/ppermute | solution.py:31
  32.3 8.7 %collective-permute-start.9 = (bf16[2,32,1024]{2,1,0:T(8,128)(2,1)S(1)}, bf16[2,32,1024]{2,1,0:T(8,128)(2,1)S(1)}, u32[]{:S(2)}, u32[]{:S(2)}) collective-permute-start(bf16[2,32,1024]{2,1,0:T(8,128)(2,1)S(1)} %get-tuple-element.65.refs_1_), channel_id=1, source_target_pairs={{0,12},{1,13},{2,14},{3,15},{4,0},{5,1},{6,2},{7,3},{8,4},{9,5},{1... | collective-permute-start | bytes 393224 | tf_op jit(solution)/shard_map/ppermute | solution.py:31
  36.0 7.5 %collective-permute-start.10 = (bf16[2,2,128,256]{3,2,1,0:T(8,128)(2,1)S(1)}, bf16[2,2,128,256]{3,2,1,0:T(8,128)(2,1)S(1)}, u32[]{:S(2)}, u32[]{:S(2)}) collective-permute-start(bf16[2,2,128,256]{3,2,1,0:T(8,128)(2,1)S(1)} %get-tuple-element.64.refs_0_.refs_1_), channel_id=1, source_target_pairs={{0,1},{1,0},{2,3},{3,2},{4,5},{5,4},{6,7},{7,6},{8,9},{9,8},{10,11... | collective-permute-start | bytes 786440 | tf_op jit(solution)/shard_map/ppermute | solution.py:35
  45.9 10.2 %collective-permute-start.13 = (bf16[2,2,128,256]{3,2,1,0:T(8,128)(2,1)S(1)}, bf16[2,2,128,256]{3,2,1,0:T(8,128)(2,1)S(1)}, u32[]{:S(2)}, u32[]{:S(2)}) collective-permute-start(bf16[2,2,128,256]{3,2,1,0:T(8,128)(2,1)S(1)} %half.5.refs_0_), channel_id=1, source_target_pairs={{0,2},{1,3},{2,0},{3,1},{4,6},{5,7},{6,4},{7,5},{8,10},{9,11},{10,... | collective-permute-start | bytes 786440 | tf_op jit(solution)/shard_map/ppermute | solution.py:35
  47.5 9.3 %collective-permute-start.14 = (bf16[2,32,1024]{2,1,0:T(8,128)(2,1)S(1)}, bf16[2,32,1024]{2,1,0:T(8,128)(2,1)S(1)}, u32[]{:S(2)}, u32[]{:S(2)}) collective-permute-start(bf16[2,32,1024]{2,1,0:T(8,128)(2,1)S(1)} %get-tuple-element.71.refs_1_), channel_id=1, source_target_pairs={{0,4},{1,5},{2,6},{3,7},{4,8},{5,9},{6,10},{7,11},{8,12},{9,13},{1... | collective-permute-start | bytes 393224 | tf_op jit(solution)/shard_map/ppermute | solution.py:31
  50.8 9.9 %collective-permute-start.15 = (bf16[2,32,1024]{2,1,0:T(8,128)(2,1)S(1)}, bf16[2,32,1024]{2,1,0:T(8,128)(2,1)S(1)}, u32[]{:S(2)}, u32[]{:S(2)}) collective-permute-start(bf16[2,32,1024]{2,1,0:T(8,128)(2,1)S(1)} %get-tuple-element.71.refs_1_), channel_id=1, source_target_pairs={{0,8},{1,9},{2,10},{3,11},{4,12},{5,13},{6,14},{7,15},{8,0},{9,1},... | collective-permute-start | bytes 393224 | tf_op jit(solution)/shard_map/ppermute | solution.py:31
  52.1 8.6 %collective-permute-start.16 = (bf16[2,32,1024]{2,1,0:T(8,128)(2,1)S(1)}, bf16[2,32,1024]{2,1,0:T(8,128)(2,1)S(1)}, u32[]{:S(2)}, u32[]{:S(2)}) collective-permute-start(bf16[2,32,1024]{2,1,0:T(8,128)(2,1)S(1)} %get-tuple-element.71.refs_1_), channel_id=1, source_target_pairs={{0,12},{1,13},{2,14},{3,15},{4,0},{5,1},{6,2},{7,3},{8,4},{9,5},{1... | collective-permute-start | bytes 393224 | tf_op jit(solution)/shard_map/ppermute | solution.py:31
  53.2 18.7 %collective-permute-start.20 = (bf16[2,128,1024]{2,1,0:T(8,128)(2,1)S(1)}, bf16[2,128,1024]{2,1,0:T(8,128)(2,1)S(1)}, u32[]{:S(2)}, u32[]{:S(2)}) collective-permute-start(bf16[2,128,1024]{2,1,0:T(8,128)(2,1)S(1)} %get-tuple-element.67.refs_0_), channel_id=1, source_target_pairs={{0,4},{1,5},{2,6},{3,7},{12,8},{13,9},{14,10},{15,11},{16,20},{17,... | collective-permute-start | bytes 1572872 | tf_op jit(solution)/shard_map/ppermute | solution.py:31
  65.7 10.7 %collective-permute-start.21 = (bf16[2,2,128,256]{3,2,1,0:T(8,128)(2,1)S(1)}, bf16[2,2,128,256]{3,2,1,0:T(8,128)(2,1)S(1)}, u32[]{:S(2)}, u32[]{:S(2)}) collective-permute-start(bf16[2,2,128,256]{3,2,1,0:T(8,128)(2,1)S(1)} %half.6.refs_0_), channel_id=1, source_target_pairs={{0,2},{1,3},{2,0},{3,1},{4,6},{5,7},{6,4},{7,5},{8,10},{9,11},{10,... | collective-permute-start | bytes 786440 | tf_op jit(solution)/shard_map/ppermute | solution.py:35
  66.2 11.6 %collective-permute-start.22 = (bf16[2,32,1024]{2,1,0:T(8,128)(2,1)S(1)}, bf16[2,32,1024]{2,1,0:T(8,128)(2,1)S(1)}, u32[]{:S(2)}, u32[]{:S(2)}) collective-permute-start(bf16[2,32,1024]{2,1,0:T(8,128)(2,1)S(1)} %get-tuple-element.78.refs_1_), channel_id=1, source_target_pairs={{0,4},{1,5},{2,6},{3,7},{4,8},{5,9},{6,10},{7,11},{8,12},{9,13},{1... | collective-permute-start | bytes 393224 | tf_op jit(solution)/shard_map/ppermute | solution.py:31
  69.5 10.9 %collective-permute-start.23 = (bf16[2,32,1024]{2,1,0:T(8,128)(2,1)S(1)}, bf16[2,32,1024]{2,1,0:T(8,128)(2,1)S(1)}, u32[]{:S(2)}, u32[]{:S(2)}) collective-permute-start(bf16[2,32,1024]{2,1,0:T(8,128)(2,1)S(1)} %get-tuple-element.78.refs_1_), channel_id=1, source_target_pairs={{0,8},{1,9},{2,10},{3,11},{4,12},{5,13},{6,14},{7,15},{8,0},{9,1},... | collective-permute-start | bytes 393224 | tf_op jit(solution)/shard_map/ppermute | solution.py:31
  71.1 9.3 %collective-permute-start.24 = (bf16[2,32,1024]{2,1,0:T(8,128)(2,1)S(1)}, bf16[2,32,1024]{2,1,0:T(8,128)(2,1)S(1)}, u32[]{:S(2)}, u32[]{:S(2)}) collective-permute-start(bf16[2,32,1024]{2,1,0:T(8,128)(2,1)S(1)} %get-tuple-element.78.refs_1_), channel_id=1, source_target_pairs={{0,12},{1,13},{2,14},{3,15},{4,0},{5,1},{6,2},{7,3},{8,4},{9,5},{1... | collective-permute-start | bytes 393224 | tf_op jit(solution)/shard_map/ppermute | solution.py:31
  71.9 19.7 %collective-permute-start.28 = (bf16[2,128,1024]{2,1,0:T(8,128)(2,1)S(1)}, bf16[2,128,1024]{2,1,0:T(8,128)(2,1)S(1)}, u32[]{:S(2)}, u32[]{:S(2)}) collective-permute-start(bf16[2,128,1024]{2,1,0:T(8,128)(2,1)S(1)} %get-tuple-element.73.refs_0_), channel_id=1, source_target_pairs={{0,4},{1,5},{2,6},{3,7},{12,8},{13,9},{14,10},{15,11},{16,20},{17,... | collective-permute-start | bytes 1572872 | tf_op jit(solution)/shard_map/ppermute | solution.py:31
  76.4 16.6 %collective-permute-start.29 = (bf16[2,128,1024]{2,1,0:T(8,128)(2,1)S(1)}, bf16[2,128,1024]{2,1,0:T(8,128)(2,1)S(1)}, u32[]{:S(2)}, u32[]{:S(2)}) collective-permute-start(bf16[2,128,1024]{2,1,0:T(8,128)(2,1)S(1)} %add.46.refs_0_), channel_id=1, source_target_pairs={{4,8},{5,9},{6,10},{7,11},{8,4},{9,5},{10,6},{11,7},{20,24},{21,25... | collective-permute-start | bytes 1572872 | tf_op jit(solution)/shard_map/ppermute | solution.py:31
  85.4 9.5 %collective-permute-start.30 = (bf16[2,2,128,256]{3,2,1,0:T(8,128)(2,1)S(1)}, bf16[2,2,128,256]{3,2,1,0:T(8,128)(2,1)S(1)}, u32[]{:S(2)}, u32[]{:S(2)}) collective-permute-start(bf16[2,2,128,256]{3,2,1,0:T(8,128)(2,1)S(1)} %half.7.refs_0_), channel_id=1, source_target_pairs={{0,2},{1,3},{2,0},{3,1},{4,6},{5,7},{6,4},{7,5},{8,10},{9,11},{10,... | collective-permute-start | bytes 786440 | tf_op jit(solution)/shard_map/ppermute | solution.py:35
  86.3 17.6 %collective-permute-start.32 = (bf16[2,128,1024]{2,1,0:T(8,128)(2,1)S(1)}, bf16[2,128,1024]{2,1,0:T(8,128)(2,1)S(1)}, u32[]{:S(2)}, u32[]{:S(2)}) collective-permute-start(bf16[2,128,1024]{2,1,0:T(8,128)(2,1)S(1)} %get-tuple-element.80.refs_0_), channel_id=1, source_target_pairs={{0,4},{1,5},{2,6},{3,7},{12,8},{13,9},{14,10},{15,11},{16,20},{17,... | collective-permute-start | bytes 1572872 | tf_op jit(solution)/shard_map/ppermute | solution.py:31
  92.3 13.0 %collective-permute-start.33 = (bf16[2,128,1024]{2,1,0:T(8,128)(2,1)S(1)}, bf16[2,128,1024]{2,1,0:T(8,128)(2,1)S(1)}, u32[]{:S(2)}, u32[]{:S(2)}) collective-permute-start(bf16[2,128,1024]{2,1,0:T(8,128)(2,1)S(1)} %add.47.refs_0_), channel_id=1, source_target_pairs={{4,8},{5,9},{6,10},{7,11},{8,4},{9,5},{10,6},{11,7},{20,24},{21,25... | collective-permute-start | bytes 1572872 | tf_op jit(solution)/shard_map/ppermute | solution.py:31
  93.6 15.3 %collective-permute-start.34 = (bf16[2,128,1024]{2,1,0:T(8,128)(2,1)S(1)}, bf16[2,128,1024]{2,1,0:T(8,128)(2,1)S(1)}, u32[]{:S(2)}, u32[]{:S(2)}) collective-permute-start(bf16[2,128,1024]{2,1,0:T(8,128)(2,1)S(1)} %add.48.refs_0_), channel_id=1, source_target_pairs={{4,0},{5,1},{6,2},{7,3},{8,12},{9,13},{10,14},{11,15},{20,16},{21,... | collective-permute-start | bytes 1572872 | tf_op jit(solution)/shard_map/ppermute | solution.py:31
  99.3 16.1 %collective-permute-start.37 = (bf16[2,128,1024]{2,1,0:T(8,128)(2,1)S(1)}, bf16[2,128,1024]{2,1,0:T(8,128)(2,1)S(1)}, u32[]{:S(2)}, u32[]{:S(2)}) collective-permute-start(bf16[2,128,1024]{2,1,0:T(8,128)(2,1)S(1)} %get-tuple-element.85.refs_0_), channel_id=1, source_target_pairs={{0,4},{1,5},{2,6},{3,7},{12,8},{13,9},{14,10},{15,11},{16,20},{17,... | collective-permute-start | bytes 1572872 | tf_op jit(solution)/shard_map/ppermute | solution.py:31
  104.6 12.1 %collective-permute-start.38 = (bf16[2,128,1024]{2,1,0:T(8,128)(2,1)S(1)}, bf16[2,128,1024]{2,1,0:T(8,128)(2,1)S(1)}, u32[]{:S(2)}, u32[]{:S(2)}) collective-permute-start(bf16[2,128,1024]{2,1,0:T(8,128)(2,1)S(1)} %add.49.refs_0_), channel_id=1, source_target_pairs={{4,8},{5,9},{6,10},{7,11},{8,4},{9,5},{10,6},{11,7},{20,24},{21,25... | collective-permute-start | bytes 1572872 | tf_op jit(solution)/shard_map/ppermute | solution.py:31
  105.9 15.6 %collective-permute-start.39 = (bf16[2,128,1024]{2,1,0:T(8,128)(2,1)S(1)}, bf16[2,128,1024]{2,1,0:T(8,128)(2,1)S(1)}, u32[]{:S(2)}, u32[]{:S(2)}) collective-permute-start(bf16[2,128,1024]{2,1,0:T(8,128)(2,1)S(1)} %add.50.refs_0_), channel_id=1, source_target_pairs={{4,0},{5,1},{6,2},{7,3},{8,12},{9,13},{10,14},{11,15},{20,16},{21,... | collective-permute-start | bytes 1572872 | tf_op jit(solution)/shard_map/ppermute | solution.py:31
  116.0 14.9 %collective-permute-start.43 = (bf16[2,128,1024]{2,1,0:T(8,128)(2,1)S(1)}, bf16[2,128,1024]{2,1,0:T(8,128)(2,1)S(1)}, u32[]{:S(2)}, u32[]{:S(2)}) collective-permute-start(bf16[2,128,1024]{2,1,0:T(8,128)(2,1)S(1)} %add.51.refs_0_), channel_id=1, source_target_pairs={{4,8},{5,9},{6,10},{7,11},{8,4},{9,5},{10,6},{11,7},{20,24},{21,25... | collective-permute-start | bytes 1572872 | tf_op jit(solution)/shard_map/ppermute | solution.py:31
  117.4 17.7 %collective-permute-start.44 = (bf16[2,128,1024]{2,1,0:T(8,128)(2,1)S(1)}, bf16[2,128,1024]{2,1,0:T(8,128)(2,1)S(1)}, u32[]{:S(2)}, u32[]{:S(2)}) collective-permute-start(bf16[2,128,1024]{2,1,0:T(8,128)(2,1)S(1)} %add.52.refs_0_), channel_id=1, source_target_pairs={{4,0},{5,1},{6,2},{7,3},{8,12},{9,13},{10,14},{11,15},{20,16},{21,... | collective-permute-start | bytes 1572872 | tf_op jit(solution)/shard_map/ppermute | solution.py:31
  123.5 6.8 %collective-permute-start.41 = (f32[2,128,256]{2,1,0:T(8,128)S(1)}, f32[2,128,256]{2,1,0:T(8,128)S(1)}, u32[]{:S(2)}, u32[]{:S(2)}) collective-permute-start(f32[2,128,256]{2,1,0:T(8,128)S(1)} %get-tuple-element.94), channel_id=1, source_target_pairs={{0,1},{1,0},{2,3},{3,2},{4,5},{5,4},{6,7},{7,6},{8,9},{9,8},{10,11... | collective-permute-start | bytes 786440 | tf_op jit(solution)/shard_map/ppermute | solution.py:35
  131.6 15.1 %collective-permute-start.48 = (bf16[2,128,1024]{2,1,0:T(8,128)(2,1)S(1)}, bf16[2,128,1024]{2,1,0:T(8,128)(2,1)S(1)}, u32[]{:S(2)}, u32[]{:S(2)}) collective-permute-start(bf16[2,128,1024]{2,1,0:T(8,128)(2,1)S(1)} %add.53.refs_0_), channel_id=1, source_target_pairs={{4,0},{5,1},{6,2},{7,3},{8,12},{9,13},{10,14},{11,15},{20,16},{21,... | collective-permute-start | bytes 1572872 | tf_op jit(solution)/shard_map/ppermute | solution.py:31
  148.7 6.8 %collective-permute-start.50 = (f32[2,128,256]{2,1,0:T(8,128)S(1)}, f32[2,128,256]{2,1,0:T(8,128)S(1)}, u32[]{:S(2)}, u32[]{:S(2)}) collective-permute-start(f32[2,128,256]{2,1,0:T(8,128)S(1)} %get-tuple-element.104), channel_id=1, source_target_pairs={{0,1},{1,0},{2,3},{3,2},{4,5},{5,4},{6,7},{7,6},{8,9},{9,8},{10,11... | collective-permute-start | bytes 786440 | tf_op jit(solution)/shard_map/ppermute | solution.py:35
  (31 other events, 185.8 us)

commit v3 on v2

v3 whole, which is shorter than its diff:
```python
import functools

import jax
import jax.numpy as jnp
from jax import lax
from jax.experimental import pallas as pl
from jax.experimental.pallas import tpu as pltpu
from jax.sharding import PartitionSpec as P

ROWS = 4
COLS = 4
TEAM = ROWS * COLS
SIZES = ((2, 2), (2, 2))
GROUPS = ((0,), (1,), (2,), (3,))
LAG = {"I": 1, "R": 2, "H": 1, "D": 2, "A": 3, "B": 4, "C": 5, "J": 5, "K": 7}

CORE = 2

f32, bf16 = jnp.float32, jnp.bfloat16
VMEM = pl.BlockSpec(memory_space=pltpu.VMEM)
SMEM = pl.BlockSpec(memory_space=pltpu.SMEM)
ANY = pl.BlockSpec(memory_space=pl.ANY)
HBM = pl.BlockSpec(memory_space=pltpu.HBM)
shape = jax.ShapeDtypeStruct


def team_pairs(pairs):
    groups = lax.axis_size("freq") // TEAM
    return [(TEAM * g + a, TEAM * g + b) for g in range(groups) for a, b in pairs]


def along_columns(value, moves):
    pairs = [(ROWS * a + r, ROWS * b + r) for a, b in moves for r in range(ROWS)]
    return lax.ppermute(value, "freq", team_pairs(pairs))


def swap(value, bit):
    return lax.ppermute(value, "freq", team_pairs([(d, d ^ (1 << bit)) for d in range(TEAM)]))


INWARD = [(0, 1), (3, 2)]
MIDDLE = [(1, 2), (2, 1)]
OUTWARD = [(1, 0), (2, 3)]
SHIFTS = [[(a, (a + k) % COLS) for a in range(COLS)] for k in range(1, COLS)]


def product(left, right):
    return lax.dot_general(left, right, (((1,), (0,)), ((), ())), preferred_element_type=f32)


def product_transposed(left, right):
    return lax.dot_general(left, right, (((1,), (1,)), ((), ())), preferred_element_type=f32)


def slab_of(refs, n):
    each = 4 // len(refs)
    return refs[n // each].at[n % each]


def multiply_columns(core, left, matrix, keep, *sends):
    count = left.shape[0] // 2
    width = keep.shape[3]
    away = [slab_of(sends, n) for n in range(4)]
    for which, outs in ((1 - core, away), (core, [keep.at[n // 2, n % 2] for n in range(4)])):
        for half in range(2):
            real, imag = outs[2 * half : 2 * half + 2]
            cols = pl.ds(pl.multiple_of((2 * half + which) * width, width), width)
            with_real = product(left, matrix[0, :, cols])
            with_imag = product(left, matrix[1, :, cols])
            real[...] = with_real[:count] - with_imag[count:]
            imag[...] = with_imag[:count] + with_real[count:]


def load_kernel(where, matrix_hbm, data_hbm, *refs):
    freqs = matrix_hbm.shape[0]
    datas, matrices, sems = refs[-1 - 2 * freqs : -1 - freqs], refs[-1 - freqs : -1], refs[-1]
    pairs = [(data_hbm.at[f], data) for f, data in enumerate(datas)]
    pairs += [(matrix_hbm.at[f], matrix) for f, matrix in enumerate(matrices)]
    copies = [
        pltpu.make_async_copy(source, target, sems.at[n]) for n, (source, target) in enumerate(pairs)
    ]
    for copy in copies:
        copy.start()
    for copy in copies:
        copy.wait()


def image_kernel(start, where, *refs):
    core, col = where[0], where[2]
    fields, (matrix, keep, *sends, left) = refs[:COLS], refs[COLS:]
    for k, field in enumerate(fields):
        left[:, lax.rem(col + COLS - k, COLS)] = field[:, start : start + left.shape[2]]
    rows = 2 * COLS * left.shape[2]
    multiply_columns(core, left[...].reshape(rows, left.shape[3]), matrix, keep, *sends)


def half_kernel(where, keep, *refs):
    *got, low = refs
    for n in range(4):
        low[n // 2, n % 2] = (keep[n // 2, n % 2] + slab_of(got, n)[...]).astype(bf16)


def residual_kernel(start, size, where, keep, *refs):
    *got, far, data, other_data, low, residual = refs
    y = where[1]
    slab = data.shape[1] // COLS
    for half in range(2):
        for source, mine in ((data, True), (other_data, False)):

            @pl.when((y == half) == mine)
            def _(half=half, source=source, mine=mine):
                for c in range(2):
                    for s in range(COLS):
                        rows = pl.ds(s * size, size)
                        image = (keep[half, c, rows] + slab_of(got, 2 * half + c)[rows]) + far[half, c, rows].astype(f32)
                        value = source[c, pl.ds(s * slab + start, size)] - image
                        low[half, c, rows] = value.astype(bf16)
                        if mine:
                            residual[c, rows] = value


def descent_kernel(where, own, other, matrix, low, part, left):
    core = where[0]
    count, width = own.shape[2], own.shape[3]
    for half in range(2):
        for which, ref in ((core, own), (1 - core, other)):
            cols = pl.ds(pl.multiple_of((2 * half + which) * width, width), width)
            left[:, cols] = ref[half].reshape(2 * count, width)
    depth = matrix.shape[1]
    tile = depth // 4
    for k in range(4):
        rows = pl.ds(k * tile, tile)
        with_real = product_transposed(left[...], matrix[0, rows, :])
        with_imag = product_transposed(left[...], matrix[1, rows, :])
        real = with_real[:count] + with_imag[count:]
        imag = with_real[count:] - with_imag[:count]
        part[0, :, rows], part[1, :, rows] = real, imag
        low[0, :, rows], low[1, :, rows] = real.astype(bf16), imag.astype(bf16)


def add_kernel(where, part, got, out):
    out[...] = (part[...] + got[...].astype(f32)).astype(bf16)


def curvature_kernel(f, where, part, first, second, third, scale, matrix, keep, *refs):
    core, col = where[0], where[2]
    *sends, own, left = refs
    count, depth = part.shape[1], part.shape[2]
    piece = own.shape[1]
    row_scale = scale[f : f + 1, :]

    def descent(c, rows):
        inner = part[c, rows] + first[c, rows].astype(f32)
        outer = second[c, rows].astype(f32) + third[c, rows].astype(f32)
        return (inner + outer) * row_scale

    for c in range(2):
        left[c] = (descent(c, pl.ds(0, count)) * row_scale).astype(bf16)
        own[c] = descent(c, pl.ds(pl.multiple_of(col * piece, piece), piece))
    multiply_columns(core, left[...].reshape(2 * count, depth), matrix, keep, *sends)


def bend_half_kernel(where, keep, *refs):
    *got, low = refs
    for half in range(2):

        @pl.when(where[1] != half)
        def _(half=half):
            for c in range(2):
                low[c] = (keep[half, c] + slab_of(got, 2 * half + c)[...]).astype(bf16)


def squares(value):
    return jnp.sum((value * value).reshape(-1, 8, 128), axis=0)


def bend_kernel(where, keep, *refs):
    *got, far, own, sums, out_sums, curvature = refs
    for half in range(2):

        @pl.when(where[1] == half)
        def _(half=half):
            for c in range(2):
                curvature[c] = (keep[half, c] + slab_of(got, 2 * half + c)[...]) + far[c].astype(f32)

    value = curvature[...]
    out_sums[0] = sums[0] + squares(own[...])
    out_sums[1] = sums[1] + squares(value)


def spread_kernel(where, sums, out):
    rows = [jnp.sum(sums[n], axis=0, keepdims=True) for n in range(2)]
    out[...] = jnp.broadcast_to(jnp.concatenate(rows * 4, axis=0)[None], out.shape)


def update_kernel(chunks, where, sums, current, *refs):
    n = len(chunks)
    descents, residuals, curvatures = refs[:n], refs[n : 2 * n], refs[2 * n : 3 * n]
    new_iterate, new_residual = refs[3 * n :]
    total = jnp.sum(sums[...], axis=0)
    step = jnp.sum(total[:1], keepdims=True) / jnp.sum(total[1:2], keepdims=True)
    slab = new_residual.shape[3] // COLS
    for (f, start, size), descent, residual, curvature in zip(
        chunks, descents, residuals, curvatures
    ):
        for c in range(2):
            rows = pl.ds(start, size)
            new_iterate[0, f, c, rows] = current[f, c, rows] + step * descent[c]
            for s in range(COLS):
                rows = pl.ds(s * size, size)
                new_residual[0, f, c, pl.ds(s * slab + start, size)] = (
                    residual[c, rows] - step * curvature[c, rows]
                )


class Chain:
    def __init__(self, where):
        self.where = where
        self.last = None

    def __call__(self, kernel, name, out_shape, *operands, scratch=(), flops=0, specs=None):
        token = [] if self.last is None else [self.last]

        def run(where, *refs):
            return kernel(where, *refs[len(token) :])

        results = pl.pallas_call(
            run,
            in_specs=[SMEM] + [ANY] * len(token) + (specs or [VMEM] * len(operands)),
            out_specs=[VMEM] * len(out_shape),
            out_shape=out_shape,
            scratch_shapes=list(scratch),
            name=name,
            cost_estimate=pl.CostEstimate(
                flops=0, bytes_accessed=1024, transcendentals=0
            ),
            compiler_params=pltpu.CompilerParams(vmem_limit_bytes=32 << 20),
        )(self.where, *token, *operands)
        self.last = results[0]
        return results


def body(spectrum, blocks, scales, iterate):
    index = lax.axis_index("freq")
    where = jnp.stack([index % 2, index // 2 % 2, index // ROWS % COLS, index // TEAM])
    matrix, current, data = blocks[0], iterate[0], spectrum[0]
    freqs, _, row_len, col_len = matrix.shape
    slab, width = current.shape[2], data.shape[3]
    chunks = []
    for f in range(freqs):
        sizes = [slab // 4 * part for part in SIZES[f]]
        chunks += [(f, sum(sizes[:h]), size) for h, size in enumerate(sizes)]
    sent = [[chunks[n] for n in members] for members in GROUPS]
    chain = Chain(where.astype(jnp.int32))

    own_scales = lax.dynamic_slice(
        scales, (index // TEAM * freqs, index % ROWS * row_len), (freqs, row_len)
    )
    owns = [
        jnp.concatenate(
            [current[f, :, start : start + rows] * own_scales[f] for f, start, rows in members], 1
        ).astype(bf16)
        for members in sent
    ]
    staged = chain(
        load_kernel,
        "load",
        [shape(data.shape[1:], f32)] * freqs + [shape(matrix.shape[1:], bf16)] * freqs,
        matrix,
        data,
        *owns,
        specs=[HBM] * 2 + [ANY] * len(owns),
        scratch=[pltpu.SemaphoreType.DMA((2 * freqs,))],
    )
    data, matrices = staged[:freqs], staged[freqs:]
    other_data = [swap(rows, 1) for rows in data]
    values = [{} for _ in chunks]
    totals = [jnp.zeros((2, 8, 128), f32)]

    for members, own in zip(GROUPS, owns):
        gathered = (own, *(along_columns(own, moves) for moves in SHIFTS))
        place = 0
        for n in members:
            values[n]["x"], values[n]["start"] = gathered, place
            place += chunks[n][2]

    def step(kind, n):
        f, start, rows = chunks[n]
        v = values[n]
        count = COLS * rows
        flops = 8 * count * row_len * col_len
        forward = [shape((2, 2, count, width), f32)] + [shape((4 // CORE, count, width), f32)] * CORE
        if kind == "I":
            v["keep"], *sends = chain(
                functools.partial(image_kernel, v["start"]),
                "image",
                forward,
                *v["x"],
                matrices[f],
                scratch=[pltpu.VMEM((2, COLS, rows, row_len), bf16)],
                flops=flops,
            )
            v["got"] = [swap(send, 0) for send in sends]
        elif kind == "H":
            (low,) = chain(half_kernel, "half", [shape((2, 2, count, width), bf16)], v["keep"], *v["got"])
            v["far"] = swap(low, 1)
        elif kind == "R":
            v["low"], v["residual"] = chain(
                functools.partial(residual_kernel, start, rows),
                "residual",
                [shape((2, 2, count, width), bf16), shape((2, count, width), f32)],
                v["keep"],
                *v["got"],
                v["far"],
                data[f],
                other_data[f],
            )
            v["other_low"] = swap(v["low"], 0)
        elif kind == "D":
            low, v["part"] = chain(
                descent_kernel,
                "descent",
                [shape((2, count, row_len), bf16), shape((2, count, row_len), f32)],
                v["low"],
                v["other_low"],
                matrices[f],
                scratch=[pltpu.VMEM((2 * count, col_len), bf16)],
                flops=flops,
            )
            v["first"] = along_columns(low, INWARD)
        elif kind in "AB":
            name, source, moves = (
                ("second", "first", MIDDLE) if kind == "A" else ("third", "second", OUTWARD)
            )
            (low,) = chain(add_kernel, "add", [shape((2, count, row_len), bf16)], v["part"], v[source])
            v[name] = along_columns(low, moves)
        elif kind == "C":
            v["keep"], *sends, v["own"] = chain(
                functools.partial(curvature_kernel, f),
                "curvature",
                forward + [shape((2, rows, row_len), f32)],
                v["part"],
                v["first"],
                v["second"],
                v["third"],
                own_scales,
                matrices[f],
                scratch=[pltpu.VMEM((2, count, row_len), bf16)],
                flops=flops,
            )
            v["got"] = [swap(send, 0) for send in sends]
        elif kind == "J":
            (low,) = chain(
                bend_half_kernel, "bend_half", [shape((2, count, width), bf16)], v["keep"], *v["got"]
            )
            v["far"] = swap(low, 1)
        elif kind == "K":
            totals[0], v["curvature"] = chain(
                bend_kernel,
                "bend",
                [shape((2, 8, 128), f32), shape((2, count, width), f32)],
                v["keep"],
                *v["got"],
                v["far"],
                v["own"],
                totals[0],
            )

    for turn in range(max(LAG.values()) + len(chunks)):
        for kind, lag in LAG.items():
            if 0 <= turn - lag < len(chunks):
                step(kind, turn - lag)

    (sums,) = chain(spread_kernel, "spread", [shape((TEAM, 8, 128), f32)], totals[0])
    teams = lax.axis_size("freq") // TEAM
    members = [[TEAM * g + d for d in range(TEAM)] for g in range(teams)]
    sums = lax.all_to_all(sums, "freq", 0, 0, axis_index_groups=members)
    return chain(
        functools.partial(update_kernel, chunks),
        "update",
        [shape(iterate.shape, f32), shape(spectrum.shape, f32)],
        sums,
        current,
        *(v[name] for name in ("own", "residual", "curvature") for v in values),
    )


def solution(mesh):
    placed = P(("parts", "freq"), None, None, None, None)
    return jax.shard_map(
        body,
        mesh=mesh,
        in_specs=(placed, P("freq", None, None, None, None), P(), placed),
        out_specs=(placed, placed),
        check_vma=False,
    )
```

time: 178 us -> 170 us (0.955)
  waiting for transfers between devices: 64.2 us -> 45.1 us
  blocking collectives: 0 us -> 10.5 us
  starting transfers between devices: 64.7 us -> 62.6 us
    ppermute x33 -> x30, waiting for transfers between devices: 35 us -> 15.4 us  [swap(): lax.ppermute(value, 'freq', team_pairs([(d, d ^ 1 << bit) for d in range(...]
    all_to_all x0 -> x1, blocking collectives: none -> 10.5 us  [body(): sums = lax.all_to_all(sums, 'freq', 0, 0, axis_index_groups=members)]
    ppermute x33 -> x30, starting transfers between devices: 17.6 us -> 15.1 us  [swap(): lax.ppermute(value, 'freq', team_pairs([(d, d ^ 1 << bit) for d in range(...]
    pallas_call x38 -> x39, Pallas kernels: 41.5 us -> 42.5 us  [__call__(): pl.pallas_call(run, in_specs=[SMEM] + [ANY] * len(token) + (specs or [VME...]
    unnamed x12 -> x6, local copies, waits for them, and re-layouts: 5.38 us -> 4.61 us
  transfers between devices with their start and end apart: 57 -> 54, of which waited for: 25 -> 27; matrix products, arithmetic and copies ran while one was open for 0% -> 0% of each run, Pallas kernels for 20% -> 21%
where the time goes in v3:
time: 170 us; the launch traced here: 169 us
  starting transfers between devices  62.6 us (37%)
  waiting for transfers between devices  45.1 us (27%)
  Pallas kernels  42.5 us (25%)
  blocking collectives  10.5 us (6%)
  local copies, waits for them, and re-layouts  6.17 us (4%)
    ppermute x24, starting transfers between devices, along_columns(): return lax.ppermute(value, 'freq', team_pairs(pairs))  47.4 us
    pallas_call x39, Pallas kernels, __call__(): pl.pallas_call(run, in_specs=[SMEM] + [ANY] * len(token) + (specs or [VME...  42.5 us
    ppermute x24, waiting for transfers between devices, along_columns(): return lax.ppermute(value, 'freq', team_pairs(pairs))  29.7 us
    ppermute x30, waiting for transfers between devices, swap(): lax.ppermute(value, 'freq', team_pairs([(d, d ^ 1 << bit) for d in range(...  15.4 us
    ppermute x30, starting transfers between devices, swap(): lax.ppermute(value, 'freq', team_pairs([(d, d ^ 1 << bit) for d in range(...  15.1 us
    all_to_all x1, blocking collectives, body(): sums = lax.all_to_all(sums, 'freq', 0, 0, axis_index_groups=members)  10.5 us
    unnamed x6, local copies, waits for them, and re-layouts  4.61 us
  transfers between devices with their start and end apart: 54, of which 27 were waited for; matrix products, arithmetic and copies ran while one was open for 0% of the time, Pallas kernels for 21%

profile of v3, /device:TPU:0, one launch (start us, length us, event | category | flops | bytes accessed | tf_op | source)
XLA Modules:
  0.0 169.4 jit_solution(14984132621465576985)
XLA Ops:
  2.8 3.1 %collective-permute-start = (bf16[2,32,1024]{2,1,0:T(8,128)(2,1)S(1)}, bf16[2,32,1024]{2,1,0:T(8,128)(2,1)S(1)}, u32[]{:S(2)}, u32[]{:S(2)}) collective-permute-start(bf16[2,32,1024]{2,1,0:T(8,128)(2,1)S(1)} %get-tuple-element.118.refs_2_.refs_1_), channel_id=1, source_target_pairs={{0,4},{1,5},{2,6},{3,7},{4,8},{5,9},{6,10},{7,11},{8,12},{9,13},{1... | collective-permute-start | bytes 393224 | tf_op jit(solution)/shard_map/ppermute | solution.py:34
  5.9 2.6 %collective-permute-start.1 = (bf16[2,32,1024]{2,1,0:T(8,128)(2,1)S(1)}, bf16[2,32,1024]{2,1,0:T(8,128)(2,1)S(1)}, u32[]{:S(2)}, u32[]{:S(2)}) collective-permute-start(bf16[2,32,1024]{2,1,0:T(8,128)(2,1)S(1)} %get-tuple-element.118.refs_2_.refs_1_), channel_id=1, source_target_pairs={{0,8},{1,9},{2,10},{3,11},{4,12},{5,13},{6,14},{7,15},{8,0},{9,1},... | collective-permute-start | bytes 393224 | tf_op jit(solution)/shard_map/ppermute | solution.py:34
  9.9 3.4 %copy-done = bf16[1,2,2,1024,1024]{4,3,2,1,0:T(8,128)(2,1)S(1)} copy-done((bf16[1,2,2,1024,1024]{4,3,2,1,0:T(8,128)(2,1)S(1)}, bf16[1,2,2,1024,1024]{4,3,2,1,0:T(8,128)(2,1)}, u32[]{:S(2)}) %copy-start) | copy-done | bytes 8388632
  17.1 1.9 %image.4 = (f32[2,2,128,256]{3,2,1,0:T(8,128)S(1)}, f32[2,128,256]{2,1,0:T(8,128)S(1)}, f32[2,128,256]{2,1,0:T(8,128)S(1)}) custom-call(s32[4]{0:T(128)S(1)} %pad_add_fusion.where, f32[2,256,256]{2,1,0:T(8,128)S(1)} %get-tuple-element.58.refs_0_.refs_5_, bf16[2,32,1024]{2,1,0:T(8,128)(2,1)S(1)} %get-tuple-element.118.refs_2_.refs_1_, ...), custom_call_target="tpu_custom_call" | custom-call | bytes 1024 | tf_op jit(solution)/shard_map/image/pallas_call | solution.py:227
  23.1 3.3 %collective-permute-start.5 = (bf16[2,32,1024]{2,1,0:T(8,128)(2,1)S(1)}, bf16[2,32,1024]{2,1,0:T(8,128)(2,1)S(1)}, u32[]{:S(2)}, u32[]{:S(2)}) collective-permute-start(bf16[2,32,1024]{2,1,0:T(8,128)(2,1)S(1)} %get-tuple-element.119.refs_3_.refs_1_), channel_id=1, source_target_pairs={{0,4},{1,5},{2,6},{3,7},{4,8},{5,9},{6,10},{7,11},{8,12},{9,13},{1... | collective-permute-start | bytes 393224 | tf_op jit(solution)/shard_map/ppermute | solution.py:34
  28.8 3.1 %collective-permute-done.5.refs_2_ = bf16[2,32,1024]{2,1,0:T(8,128)(2,1)S(1)} collective-permute-done((bf16[2,32,1024]{2,1,0:T(8,128)(2,1)S(1)}, bf16[2,32,1024]{2,1,0:T(8,128)(2,1)S(1)}, u32[]{:S(2)}, u32[]{:S(2)}) %collective-permute-start.5) | collective-permute-done | bytes 131104 | tf_op jit(solution)/shard_map/ppermute | solution.py:34
  31.9 4.8 %collective-permute-done.6.refs_3_ = bf16[2,32,1024]{2,1,0:T(8,128)(2,1)S(1)} collective-permute-done((bf16[2,32,1024]{2,1,0:T(8,128)(2,1)S(1)}, bf16[2,32,1024]{2,1,0:T(8,128)(2,1)S(1)}, u32[]{:S(2)}, u32[]{:S(2)}) %collective-permute-start.6) | collective-permute-done | bytes 131104 | tf_op jit(solution)/shard_map/ppermute | solution.py:34
  36.7 1.9 %image.5 = (f32[2,2,128,256]{3,2,1,0:T(8,128)S(1)}, f32[2,128,256]{2,1,0:T(8,128)S(1)}, f32[2,128,256]{2,1,0:T(8,128)S(1)}) custom-call(s32[4]{0:T(128)S(1)} %pad_add_fusion.where, bf16[2,2,128,256]{3,2,1,0:T(8,128)(2,1)S(1)} %half.4.refs_0_, bf16[2,32,1024]{2,1,0:T(8,128)(2,1)S(1)} %get-tuple-element.119.refs_3_.refs_1_, ...), custom_call_target="tpu_custom_call" | custom-call | bytes 1024 | tf_op jit(solution)/shard_map/image/pallas_call | solution.py:227
  42.1 3.3 %collective-permute-start.13 = (bf16[2,32,1024]{2,1,0:T(8,128)(2,1)S(1)}, bf16[2,32,1024]{2,1,0:T(8,128)(2,1)S(1)}, u32[]{:S(2)}, u32[]{:S(2)}) collective-permute-start(bf16[2,32,1024]{2,1,0:T(8,128)(2,1)S(1)} %get-tuple-element.115.refs_4_.refs_1_), channel_id=1, source_target_pairs={{0,4},{1,5},{2,6},{3,7},{4,8},{5,9},{6,10},{7,11},{8,12},{9,13},{1... | collective-permute-start | bytes 393224 | tf_op jit(solution)/shard_map/ppermute | solution.py:34
  47.7 1.9 %descent.4 = (bf16[2,128,1024]{2,1,0:T(8,128)(2,1)S(1)}, f32[2,128,1024]{2,1,0:T(8,128)S(1)}) custom-call(s32[4]{0:T(128)S(1)} %pad_add_fusion.where, bf16[2,2,128,256]{3,2,1,0:T(8,128)(2,1)S(1)} %half.5.refs_0_, bf16[2,2,128,256]{3,2,1,0:T(8,128)(2,1)S(1)} %get-tuple-element.64.refs_0_.refs_1_, ...), custom_call_target="tpu_custom_call" | custom-call | bytes 1024 | tf_op jit(solution)/shard_map/descent/pallas_call | solution.py:227
  49.6 3.2 %collective-permute-start.20 = (bf16[2,128,1024]{2,1,0:T(8,128)(2,1)S(1)}, bf16[2,128,1024]{2,1,0:T(8,128)(2,1)S(1)}, u32[]{:S(2)}, u32[]{:S(2)}) collective-permute-start(bf16[2,128,1024]{2,1,0:T(8,128)(2,1)S(1)} %get-tuple-element.67.refs_0_), channel_id=1, source_target_pairs={{0,4},{1,5},{2,6},{3,7},{12,8},{13,9},{14,10},{15,11},{16,20},{17,... | collective-permute-start | bytes 1572872 | tf_op jit(solution)/shard_map/ppermute | solution.py:34
  53.8 2.2 %collective-permute-done.14.refs_3_ = bf16[2,32,1024]{2,1,0:T(8,128)(2,1)S(1)} collective-permute-done((bf16[2,32,1024]{2,1,0:T(8,128)(2,1)S(1)}, bf16[2,32,1024]{2,1,0:T(8,128)(2,1)S(1)}, u32[]{:S(2)}, u32[]{:S(2)}) %collective-permute-start.14) | collective-permute-done | bytes 131104 | tf_op jit(solution)/shard_map/ppermute | solution.py:34
  56.0 1.9 %image.6 = (f32[2,2,128,256]{3,2,1,0:T(8,128)S(1)}, f32[2,128,256]{2,1,0:T(8,128)S(1)}, f32[2,128,256]{2,1,0:T(8,128)S(1)}) custom-call(s32[4]{0:T(128)S(1)} %pad_add_fusion.where, bf16[2,128,1024]{2,1,0:T(8,128)(2,1)S(1)} %get-tuple-element.67.refs_0_, bf16[2,32,1024]{2,1,0:T(8,128)(2,1)S(1)} %get-tuple-element.115.refs_4_.refs_1_, ...), custom_call_target="tpu_custom_call" | custom-call | bytes 1024 | tf_op jit(solution)/shard_map/image/pallas_call | solution.py:227
  59.5 3.3 %collective-permute-start.21 = (bf16[2,32,1024]{2,1,0:T(8,128)(2,1)S(1)}, bf16[2,32,1024]{2,1,0:T(8,128)(2,1)S(1)}, u32[]{:S(2)}, u32[]{:S(2)}) collective-permute-start(bf16[2,32,1024]{2,1,0:T(8,128)(2,1)S(1)} %get-tuple-element.114.refs_5_.refs_1_), channel_id=1, source_target_pairs={{0,4},{1,5},{2,6},{3,7},{4,8},{5,9},{6,10},{7,11},{8,12},{9,13},{1... | collective-permute-start | bytes 393224 | tf_op jit(solution)/shard_map/ppermute | solution.py:34
  66.1 1.9 %descent.5 = (bf16[2,128,1024]{2,1,0:T(8,128)(2,1)S(1)}, f32[2,128,1024]{2,1,0:T(8,128)S(1)}) custom-call(s32[4]{0:T(128)S(1)} %pad_add_fusion.where, bf16[2,2,128,256]{3,2,1,0:T(8,128)(2,1)S(1)} %half.6.refs_0_, bf16[2,2,128,256]{3,2,1,0:T(8,128)(2,1)S(1)} %get-tuple-element.70.refs_0_.refs_1_, ...), custom_call_target="tpu_custom_call" | custom-call | bytes 1024 | tf_op jit(solution)/shard_map/descent/pallas_call | solution.py:227
  70.5 2.8 %collective-permute-start.29 = (bf16[2,128,1024]{2,1,0:T(8,128)(2,1)S(1)}, bf16[2,128,1024]{2,1,0:T(8,128)(2,1)S(1)}, u32[]{:S(2)}, u32[]{:S(2)}) collective-permute-start(bf16[2,128,1024]{2,1,0:T(8,128)(2,1)S(1)} %get-tuple-element.73.refs_0_), channel_id=1, source_target_pairs={{0,4},{1,5},{2,6},{3,7},{12,8},{13,9},{14,10},{15,11},{16,20},{17,... | collective-permute-start | bytes 1572872 | tf_op jit(solution)/shard_map/ppermute | solution.py:34
  73.3 2.1 %collective-permute-done.22.refs_3_ = bf16[2,32,1024]{2,1,0:T(8,128)(2,1)S(1)} collective-permute-done((bf16[2,32,1024]{2,1,0:T(8,128)(2,1)S(1)}, bf16[2,32,1024]{2,1,0:T(8,128)(2,1)S(1)}, u32[]{:S(2)}, u32[]{:S(2)}) %collective-permute-start.22) | collective-permute-done | bytes 131104 | tf_op jit(solution)/shard_map/ppermute | solution.py:34
  76.1 1.9 %image.7 = (f32[2,2,128,256]{3,2,1,0:T(8,128)S(1)}, f32[2,128,256]{2,1,0:T(8,128)S(1)}, f32[2,128,256]{2,1,0:T(8,128)S(1)}) custom-call(s32[4]{0:T(128)S(1)} %pad_add_fusion.where, bf16[2,128,1024]{2,1,0:T(8,128)(2,1)S(1)} %add.40.refs_0_, bf16[2,32,1024]{2,1,0:T(8,128)(2,1)S(1)} %get-tuple-element.114.refs_5_.refs_1_, ...), custom_call_target="tpu_custom_call" | custom-call | bytes 1024 | tf_op jit(solution)/shard_map/image/pallas_call | solution.py:227
  82.8 4.6 %collective-permute-start.33 = (bf16[2,128,1024]{2,1,0:T(8,128)(2,1)S(1)}, bf16[2,128,1024]{2,1,0:T(8,128)(2,1)S(1)}, u32[]{:S(2)}, u32[]{:S(2)}) collective-permute-start(bf16[2,128,1024]{2,1,0:T(8,128)(2,1)S(1)} %get-tuple-element.80.refs_0_), channel_id=1, source_target_pairs={{0,4},{1,5},{2,6},{3,7},{12,8},{13,9},{14,10},{15,11},{16,20},{17,... | collective-permute-start | bytes 1572872 | tf_op jit(solution)/shard_map/ppermute | solution.py:34
  95.1 4.6 %collective-permute-start.38 = (bf16[2,128,1024]{2,1,0:T(8,128)(2,1)S(1)}, bf16[2,128,1024]{2,1,0:T(8,128)(2,1)S(1)}, u32[]{:S(2)}, u32[]{:S(2)}) collective-permute-start(bf16[2,128,1024]{2,1,0:T(8,128)(2,1)S(1)} %get-tuple-element.83.refs_0_), channel_id=1, source_target_pairs={{0,4},{1,5},{2,6},{3,7},{12,8},{13,9},{14,10},{15,11},{16,20},{17,... | collective-permute-start | bytes 1572872 | tf_op jit(solution)/shard_map/ppermute | solution.py:34
  104.8 2.0 %curvature.4 = (f32[2,2,128,256]{3,2,1,0:T(8,128)S(1)}, f32[2,128,256]{2,1,0:T(8,128)S(1)}, f32[2,128,256]{2,1,0:T(8,128)S(1)}, f32[2,32,1024]{2,1,0:T(8,128)S(1)}) custom-call(s32[4]{0:T(128)S(1)} %pad_add_fusion.where, bf16[2,128,1024]{2,1,0:T(8,128)(2,1)S(1)} %add.44.refs_0_, f32[2,128,1024]{2,1,0:T(8,128)S(1)} %get-tuple-element.74.refs_1_, ...), custom_call_target="tpu_custom_call" | custom-call | bytes 1024 | tf_op jit(solution)/shard_map/curvature/pallas_call | solution.py:227
  114.4 3.6 %collective-permute-done.40.refs_4_ = bf16[2,128,1024]{2,1,0:T(8,128)(2,1)S(1)} collective-permute-done((bf16[2,128,1024]{2,1,0:T(8,128)(2,1)S(1)}, bf16[2,128,1024]{2,1,0:T(8,128)(2,1)S(1)}, u32[]{:S(2)}, u32[]{:S(2)}) %collective-permute-start.40) | collective-permute-done | bytes 524320 | tf_op jit(solution)/shard_map/ppermute | solution.py:34
  118.0 2.0 %curvature.5 = (f32[2,2,128,256]{3,2,1,0:T(8,128)S(1)}, f32[2,128,256]{2,1,0:T(8,128)S(1)}, f32[2,128,256]{2,1,0:T(8,128)S(1)}, f32[2,32,1024]{2,1,0:T(8,128)S(1)}) custom-call(s32[4]{0:T(128)S(1)} %pad_add_fusion.where, bf16[2,128,1024]{2,1,0:T(8,128)(2,1)S(1)} %add.46.refs_0_, f32[2,128,1024]{2,1,0:T(8,128)S(1)} %get-tuple-element.81.refs_1_, ...), custom_call_target="tpu_custom_call" | custom-call | bytes 1024 | tf_op jit(solution)/shard_map/curvature/pallas_call | solution.py:227
  124.6 5.3 %collective-permute-done.44.refs_4_ = bf16[2,128,1024]{2,1,0:T(8,128)(2,1)S(1)} collective-permute-done((bf16[2,128,1024]{2,1,0:T(8,128)(2,1)S(1)}, bf16[2,128,1024]{2,1,0:T(8,128)(2,1)S(1)}, u32[]{:S(2)}, u32[]{:S(2)}) %collective-permute-start.44) | collective-permute-done | bytes 524320 | tf_op jit(solution)/shard_map/ppermute | solution.py:34
  129.9 2.0 %curvature.6 = (f32[2,2,128,256]{3,2,1,0:T(8,128)S(1)}, f32[2,128,256]{2,1,0:T(8,128)S(1)}, f32[2,128,256]{2,1,0:T(8,128)S(1)}, f32[2,32,1024]{2,1,0:T(8,128)S(1)}) custom-call(s32[4]{0:T(128)S(1)} %pad_add_fusion.where, bf16[2,128,1024]{2,1,0:T(8,128)(2,1)S(1)} %add.47.refs_0_, f32[2,128,1024]{2,1,0:T(8,128)S(1)} %get-tuple-element.84.refs_1_, ...), custom_call_target="tpu_custom_call" | custom-call | bytes 1024 | tf_op jit(solution)/shard_map/curvature/pallas_call | solution.py:227
  134.5 3.5 %collective-permute-done.47.refs_4_ = bf16[2,128,256]{2,1,0:T(8,128)(2,1)S(1)} collective-permute-done((bf16[2,128,256]{2,1,0:T(8,128)(2,1)S(1)}, bf16[2,128,256]{2,1,0:T(8,128)(2,1)S(1)}, u32[]{:S(2)}, u32[]{:S(2)}) %collective-permute-start.47) | collective-permute-done | bytes 131104 | tf_op jit(solution)/shard_map/ppermute | solution.py:38
  138.7 3.0 %collective-permute-done.48.refs_4_ = bf16[2,128,1024]{2,1,0:T(8,128)(2,1)S(1)} collective-permute-done((bf16[2,128,1024]{2,1,0:T(8,128)(2,1)S(1)}, bf16[2,128,1024]{2,1,0:T(8,128)(2,1)S(1)}, u32[]{:S(2)}, u32[]{:S(2)}) %collective-permute-start.48) | collective-permute-done | bytes 524320 | tf_op jit(solution)/shard_map/ppermute | solution.py:34
  141.7 2.0 %curvature.7 = (f32[2,2,128,256]{3,2,1,0:T(8,128)S(1)}, f32[2,128,256]{2,1,0:T(8,128)S(1)}, f32[2,128,256]{2,1,0:T(8,128)S(1)}, f32[2,32,1024]{2,1,0:T(8,128)S(1)}) custom-call(s32[4]{0:T(128)S(1)} %pad_add_fusion.where, f32[2,8,128]{2,1,0:T(8,128)S(1)} %get-tuple-element.96.refs_0_.refs_6_, f32[2,128,1024]{2,1,0:T(8,128)S(1)} %get-tuple-element.88.refs_1_, ...), custom_call_target="tpu_custom_call" | custom-call | bytes 1024 | tf_op jit(solution)/shard_map/curvature/pallas_call | solution.py:227
  148.3 2.4 %collective-permute-done.51.refs_4_ = bf16[2,128,256]{2,1,0:T(8,128)(2,1)S(1)} collective-permute-done((bf16[2,128,256]{2,1,0:T(8,128)(2,1)S(1)}, bf16[2,128,256]{2,1,0:T(8,128)(2,1)S(1)}, u32[]{:S(2)}, u32[]{:S(2)}) %collective-permute-start.51) | collective-permute-done | bytes 131104 | tf_op jit(solution)/shard_map/ppermute | solution.py:38
  151.4 2.1 %collective-permute-done.52.refs_4_ = bf16[2,128,256]{2,1,0:T(8,128)(2,1)S(1)} collective-permute-done((bf16[2,128,256]{2,1,0:T(8,128)(2,1)S(1)}, bf16[2,128,256]{2,1,0:T(8,128)(2,1)S(1)}, u32[]{:S(2)}, u32[]{:S(2)}) %collective-permute-start.52) | collective-permute-done | bytes 131104 | tf_op jit(solution)/shard_map/ppermute | solution.py:38
  156.7 10.5 %all_to_all.5.refs_1_ = f32[16,8,128]{2,1,0:T(8,128)S(1)} all-to-all(f32[16,8,128]{2,1,0:T(8,128)S(1)} %spread.1.refs_0_), channel_id=1, replica_groups={{0,1,2,3,4,5,6,7,8,9,10,11,12,13,14,15},{16,17,18,19,20,21,22,23,24,25,..., dimensions={0} | all-to-all | bytes 131072 | tf_op jit(solution)/shard_map/all_to_all | solution.py:377
  167.2 2.2 %update.1 = (f32[1,2,2,64,1024]{4,3,2,1,0:T(8,128)}, f32[1,2,2,256,256]{4,3,2,1,0:T(8,128)}) custom-call(s32[4]{0:T(128)S(1)} %pad_add_fusion.where, f32[16,8,128]{2,1,0:T(8,128)S(1)} %spread.1.refs_0_, f32[16,8,128]{2,1,0:T(8,128)S(1)} %all_to_all.5.refs_1_, f32[2,2,64,1024]{3,2,1,0:T(8,128)S(1)} %bitcast.35, ...), custom_call_target="tpu_custom_call" | custom-call | bytes 1024 | tf_op jit(solution)/shard_map/update/pallas_call | solution.py:227
  (127 shorter events, 70.0 us)
Async XLA Ops:
  2.8 12.9 %collective-permute-start = (bf16[2,32,1024]{2,1,0:T(8,128)(2,1)S(1)}, bf16[2,32,1024]{2,1,0:T(8,128)(2,1)S(1)}, u32[]{:S(2)}, u32[]{:S(2)}) collective-permute-start(bf16[2,32,1024]{2,1,0:T(8,128)(2,1)S(1)} %get-tuple-element.118.refs_2_.refs_1_), channel_id=1, source_target_pairs={{0,4},{1,5},{2,6},{3,7},{4,8},{5,9},{6,10},{7,11},{8,12},{9,13},{1... | collective-permute-start | bytes 393224 | tf_op jit(solution)/shard_map/ppermute | solution.py:34
  5.9 11.2 %collective-permute-start.1 = (bf16[2,32,1024]{2,1,0:T(8,128)(2,1)S(1)}, bf16[2,32,1024]{2,1,0:T(8,128)(2,1)S(1)}, u32[]{:S(2)}, u32[]{:S(2)}) collective-permute-start(bf16[2,32,1024]{2,1,0:T(8,128)(2,1)S(1)} %get-tuple-element.118.refs_2_.refs_1_), channel_id=1, source_target_pairs={{0,8},{1,9},{2,10},{3,11},{4,12},{5,13},{6,14},{7,15},{8,0},{9,1},... | collective-permute-start | bytes 393224 | tf_op jit(solution)/shard_map/ppermute | solution.py:34
  8.5 8.6 %collective-permute-start.2 = (bf16[2,32,1024]{2,1,0:T(8,128)(2,1)S(1)}, bf16[2,32,1024]{2,1,0:T(8,128)(2,1)S(1)}, u32[]{:S(2)}, u32[]{:S(2)}) collective-permute-start(bf16[2,32,1024]{2,1,0:T(8,128)(2,1)S(1)} %get-tuple-element.118.refs_2_.refs_1_), channel_id=1, source_target_pairs={{0,12},{1,13},{2,14},{3,15},{4,0},{5,1},{6,2},{7,3},{8,4},{9,5},{1... | collective-permute-start | bytes 393224 | tf_op jit(solution)/shard_map/ppermute | solution.py:34
  19.6 19.6 %collective-permute-start.9 = (f32[2,256,256]{2,1,0:T(8,128)S(1)}, f32[2,256,256]{2,1,0:T(8,128)S(1)}, u32[]{:S(2)}, u32[]{:S(2)}) collective-permute-start(f32[2,256,256]{2,1,0:T(8,128)S(1)} %get-tuple-element.58.refs_0_.refs_5_), channel_id=1, source_target_pairs={{0,2},{1,3},{2,0},{3,1},{4,6},{5,7},{6,4},{7,5},{8,10},{9,11},{10,... | collective-permute-start | bytes 1572872 | tf_op jit(solution)/shard_map/ppermute | solution.py:38
  21.7 17.5 %collective-permute-start.8 = (bf16[2,2,128,256]{3,2,1,0:T(8,128)(2,1)S(1)}, bf16[2,2,128,256]{3,2,1,0:T(8,128)(2,1)S(1)}, u32[]{:S(2)}, u32[]{:S(2)}) collective-permute-start(bf16[2,2,128,256]{3,2,1,0:T(8,128)(2,1)S(1)} %half.4.refs_0_), channel_id=1, source_target_pairs={{0,2},{1,3},{2,0},{3,1},{4,6},{5,7},{6,4},{7,5},{8,10},{9,11},{10,... | collective-permute-start | bytes 786440 | tf_op jit(solution)/shard_map/ppermute | solution.py:38
  23.1 8.8 %collective-permute-start.5 = (bf16[2,32,1024]{2,1,0:T(8,128)(2,1)S(1)}, bf16[2,32,1024]{2,1,0:T(8,128)(2,1)S(1)}, u32[]{:S(2)}, u32[]{:S(2)}) collective-permute-start(bf16[2,32,1024]{2,1,0:T(8,128)(2,1)S(1)} %get-tuple-element.119.refs_3_.refs_1_), channel_id=1, source_target_pairs={{0,4},{1,5},{2,6},{3,7},{4,8},{5,9},{6,10},{7,11},{8,12},{9,13},{1... | collective-permute-start | bytes 393224 | tf_op jit(solution)/shard_map/ppermute | solution.py:34
  26.4 10.3 %collective-permute-start.6 = (bf16[2,32,1024]{2,1,0:T(8,128)(2,1)S(1)}, bf16[2,32,1024]{2,1,0:T(8,128)(2,1)S(1)}, u32[]{:S(2)}, u32[]{:S(2)}) collective-permute-start(bf16[2,32,1024]{2,1,0:T(8,128)(2,1)S(1)} %get-tuple-element.119.refs_3_.refs_1_), channel_id=1, source_target_pairs={{0,8},{1,9},{2,10},{3,11},{4,12},{5,13},{6,14},{7,15},{8,0},{9,1},... | collective-permute-start | bytes 393224 | tf_op jit(solution)/shard_map/ppermute | solution.py:34
  28.0 8.7 %collective-permute-start.7 = (bf16[2,32,1024]{2,1,0:T(8,128)(2,1)S(1)}, bf16[2,32,1024]{2,1,0:T(8,128)(2,1)S(1)}, u32[]{:S(2)}, u32[]{:S(2)}) collective-permute-start(bf16[2,32,1024]{2,1,0:T(8,128)(2,1)S(1)} %get-tuple-element.119.refs_3_.refs_1_), channel_id=1, source_target_pairs={{0,12},{1,13},{2,14},{3,15},{4,0},{5,1},{6,2},{7,3},{8,4},{9,5},{1... | collective-permute-start | bytes 393224 | tf_op jit(solution)/shard_map/ppermute | solution.py:34
  41.2 17.2 %collective-permute-start.16 = (bf16[2,2,128,256]{3,2,1,0:T(8,128)(2,1)S(1)}, bf16[2,2,128,256]{3,2,1,0:T(8,128)(2,1)S(1)}, u32[]{:S(2)}, u32[]{:S(2)}) collective-permute-start(bf16[2,2,128,256]{3,2,1,0:T(8,128)(2,1)S(1)} %half.5.refs_0_), channel_id=1, source_target_pairs={{0,2},{1,3},{2,0},{3,1},{4,6},{5,7},{6,4},{7,5},{8,10},{9,11},{10,... | collective-permute-start | bytes 786440 | tf_op jit(solution)/shard_map/ppermute | solution.py:38
  42.1 10.7 %collective-permute-start.13 = (bf16[2,32,1024]{2,1,0:T(8,128)(2,1)S(1)}, bf16[2,32,1024]{2,1,0:T(8,128)(2,1)S(1)}, u32[]{:S(2)}, u32[]{:S(2)}) collective-permute-start(bf16[2,32,1024]{2,1,0:T(8,128)(2,1)S(1)} %get-tuple-element.115.refs_4_.refs_1_), channel_id=1, source_target_pairs={{0,4},{1,5},{2,6},{3,7},{4,8},{5,9},{6,10},{7,11},{8,12},{9,13},{1... | collective-permute-start | bytes 393224 | tf_op jit(solution)/shard_map/ppermute | solution.py:34
  45.3 10.6 %collective-permute-start.14 = (bf16[2,32,1024]{2,1,0:T(8,128)(2,1)S(1)}, bf16[2,32,1024]{2,1,0:T(8,128)(2,1)S(1)}, u32[]{:S(2)}, u32[]{:S(2)}) collective-permute-start(bf16[2,32,1024]{2,1,0:T(8,128)(2,1)S(1)} %get-tuple-element.115.refs_4_.refs_1_), channel_id=1, source_target_pairs={{0,8},{1,9},{2,10},{3,11},{4,12},{5,13},{6,14},{7,15},{8,0},{9,1},... | collective-permute-start | bytes 393224 | tf_op jit(solution)/shard_map/ppermute | solution.py:34
  47.0 9.0 %collective-permute-start.15 = (bf16[2,32,1024]{2,1,0:T(8,128)(2,1)S(1)}, bf16[2,32,1024]{2,1,0:T(8,128)(2,1)S(1)}, u32[]{:S(2)}, u32[]{:S(2)}) collective-permute-start(bf16[2,32,1024]{2,1,0:T(8,128)(2,1)S(1)} %get-tuple-element.115.refs_4_.refs_1_), channel_id=1, source_target_pairs={{0,12},{1,13},{2,14},{3,15},{4,0},{5,1},{6,2},{7,3},{8,4},{9,5},{1... | collective-permute-start | bytes 393224 | tf_op jit(solution)/shard_map/ppermute | solution.py:34
  49.6 18.4 %collective-permute-start.20 = (bf16[2,128,1024]{2,1,0:T(8,128)(2,1)S(1)}, bf16[2,128,1024]{2,1,0:T(8,128)(2,1)S(1)}, u32[]{:S(2)}, u32[]{:S(2)}) collective-permute-start(bf16[2,128,1024]{2,1,0:T(8,128)(2,1)S(1)} %get-tuple-element.67.refs_0_), channel_id=1, source_target_pairs={{0,4},{1,5},{2,6},{3,7},{12,8},{13,9},{14,10},{15,11},{16,20},{17,... | collective-permute-start | bytes 1572872 | tf_op jit(solution)/shard_map/ppermute | solution.py:34
  52.8 25.3 %collective-permute-start.25 = (f32[2,256,256]{2,1,0:T(8,128)S(1)}, f32[2,256,256]{2,1,0:T(8,128)S(1)}, u32[]{:S(2)}, u32[]{:S(2)}) collective-permute-start(f32[2,256,256]{2,1,0:T(8,128)S(1)} %get-tuple-element.76.refs_5_), channel_id=1, source_target_pairs={{0,2},{1,3},{2,0},{3,1},{4,6},{5,7},{6,4},{7,5},{8,10},{9,11},{10,... | collective-permute-start | bytes 1572872 | tf_op jit(solution)/shard_map/ppermute | solution.py:38
  59.5 11.1 %collective-permute-start.21 = (bf16[2,32,1024]{2,1,0:T(8,128)(2,1)S(1)}, bf16[2,32,1024]{2,1,0:T(8,128)(2,1)S(1)}, u32[]{:S(2)}, u32[]{:S(2)}) collective-permute-start(bf16[2,32,1024]{2,1,0:T(8,128)(2,1)S(1)} %get-tuple-element.114.refs_5_.refs_1_), channel_id=1, source_target_pairs={{0,4},{1,5},{2,6},{3,7},{4,8},{5,9},{6,10},{7,11},{8,12},{9,13},{1... | collective-permute-start | bytes 393224 | tf_op jit(solution)/shard_map/ppermute | solution.py:34
  62.7 12.7 %collective-permute-start.22 = (bf16[2,32,1024]{2,1,0:T(8,128)(2,1)S(1)}, bf16[2,32,1024]{2,1,0:T(8,128)(2,1)S(1)}, u32[]{:S(2)}, u32[]{:S(2)}) collective-permute-start(bf16[2,32,1024]{2,1,0:T(8,128)(2,1)S(1)} %get-tuple-element.114.refs_5_.refs_1_), channel_id=1, source_target_pairs={{0,8},{1,9},{2,10},{3,11},{4,12},{5,13},{6,14},{7,15},{8,0},{9,1},... | collective-permute-start | bytes 393224 | tf_op jit(solution)/shard_map/ppermute | solution.py:34
  64.0 12.1 %collective-permute-start.23 = (bf16[2,32,1024]{2,1,0:T(8,128)(2,1)S(1)}, bf16[2,32,1024]{2,1,0:T(8,128)(2,1)S(1)}, u32[]{:S(2)}, u32[]{:S(2)}) collective-permute-start(bf16[2,32,1024]{2,1,0:T(8,128)(2,1)S(1)} %get-tuple-element.114.refs_5_.refs_1_), channel_id=1, source_target_pairs={{0,12},{1,13},{2,14},{3,15},{4,0},{5,1},{6,2},{7,3},{8,4},{9,5},{1... | collective-permute-start | bytes 393224 | tf_op jit(solution)/shard_map/ppermute | solution.py:34
  67.9 10.7 %collective-permute-start.24 = (bf16[2,2,128,256]{3,2,1,0:T(8,128)(2,1)S(1)}, bf16[2,2,128,256]{3,2,1,0:T(8,128)(2,1)S(1)}, u32[]{:S(2)}, u32[]{:S(2)}) collective-permute-start(bf16[2,2,128,256]{3,2,1,0:T(8,128)(2,1)S(1)} %half.6.refs_0_), channel_id=1, source_target_pairs={{0,2},{1,3},{2,0},{3,1},{4,6},{5,7},{6,4},{7,5},{8,10},{9,11},{10,... | collective-permute-start | bytes 786440 | tf_op jit(solution)/shard_map/ppermute | solution.py:38
  70.5 16.9 %collective-permute-start.29 = (bf16[2,128,1024]{2,1,0:T(8,128)(2,1)S(1)}, bf16[2,128,1024]{2,1,0:T(8,128)(2,1)S(1)}, u32[]{:S(2)}, u32[]{:S(2)}) collective-permute-start(bf16[2,128,1024]{2,1,0:T(8,128)(2,1)S(1)} %get-tuple-element.73.refs_0_), channel_id=1, source_target_pairs={{0,4},{1,5},{2,6},{3,7},{12,8},{13,9},{14,10},{15,11},{16,20},{17,... | collective-permute-start | bytes 1572872 | tf_op jit(solution)/shard_map/ppermute | solution.py:34
  75.4 13.4 %collective-permute-start.30 = (bf16[2,128,1024]{2,1,0:T(8,128)(2,1)S(1)}, bf16[2,128,1024]{2,1,0:T(8,128)(2,1)S(1)}, u32[]{:S(2)}, u32[]{:S(2)}) collective-permute-start(bf16[2,128,1024]{2,1,0:T(8,128)(2,1)S(1)} %add.40.refs_0_), channel_id=1, source_target_pairs={{4,8},{5,9},{6,10},{7,11},{8,4},{9,5},{10,6},{11,7},{20,24},{21,25... | collective-permute-start | bytes 1572872 | tf_op jit(solution)/shard_map/ppermute | solution.py:34
  80.6 10.2 %collective-permute-start.31 = (bf16[2,2,128,256]{3,2,1,0:T(8,128)(2,1)S(1)}, bf16[2,2,128,256]{3,2,1,0:T(8,128)(2,1)S(1)}, u32[]{:S(2)}, u32[]{:S(2)}) collective-permute-start(bf16[2,2,128,256]{3,2,1,0:T(8,128)(2,1)S(1)} %half.7.refs_0_), channel_id=1, source_target_pairs={{0,2},{1,3},{2,0},{3,1},{4,6},{5,7},{6,4},{7,5},{8,10},{9,11},{10,... | collective-permute-start | bytes 786440 | tf_op jit(solution)/shard_map/ppermute | solution.py:38
  82.8 17.6 %collective-permute-start.33 = (bf16[2,128,1024]{2,1,0:T(8,128)(2,1)S(1)}, bf16[2,128,1024]{2,1,0:T(8,128)(2,1)S(1)}, u32[]{:S(2)}, u32[]{:S(2)}) collective-permute-start(bf16[2,128,1024]{2,1,0:T(8,128)(2,1)S(1)} %get-tuple-element.80.refs_0_), channel_id=1, source_target_pairs={{0,4},{1,5},{2,6},{3,7},{12,8},{13,9},{14,10},{15,11},{16,20},{17,... | collective-permute-start | bytes 1572872 | tf_op jit(solution)/shard_map/ppermute | solution.py:34
  88.1 13.6 %collective-permute-start.34 = (bf16[2,128,1024]{2,1,0:T(8,128)(2,1)S(1)}, bf16[2,128,1024]{2,1,0:T(8,128)(2,1)S(1)}, u32[]{:S(2)}, u32[]{:S(2)}) collective-permute-start(bf16[2,128,1024]{2,1,0:T(8,128)(2,1)S(1)} %add.41.refs_0_), channel_id=1, source_target_pairs={{4,8},{5,9},{6,10},{7,11},{8,4},{9,5},{10,6},{11,7},{20,24},{21,25... | collective-permute-start | bytes 1572872 | tf_op jit(solution)/shard_map/ppermute | solution.py:34
  89.5 15.3 %collective-permute-start.35 = (bf16[2,128,1024]{2,1,0:T(8,128)(2,1)S(1)}, bf16[2,128,1024]{2,1,0:T(8,128)(2,1)S(1)}, u32[]{:S(2)}, u32[]{:S(2)}) collective-permute-start(bf16[2,128,1024]{2,1,0:T(8,128)(2,1)S(1)} %add.42.refs_0_), channel_id=1, source_target_pairs={{4,0},{5,1},{6,2},{7,3},{8,12},{9,13},{10,14},{11,15},{20,16},{21,... | collective-permute-start | bytes 1572872 | tf_op jit(solution)/shard_map/ppermute | solution.py:34
  95.1 16.1 %collective-permute-start.38 = (bf16[2,128,1024]{2,1,0:T(8,128)(2,1)S(1)}, bf16[2,128,1024]{2,1,0:T(8,128)(2,1)S(1)}, u32[]{:S(2)}, u32[]{:S(2)}) collective-permute-start(bf16[2,128,1024]{2,1,0:T(8,128)(2,1)S(1)} %get-tuple-element.83.refs_0_), channel_id=1, source_target_pairs={{0,4},{1,5},{2,6},{3,7},{12,8},{13,9},{14,10},{15,11},{16,20},{17,... | collective-permute-start | bytes 1572872 | tf_op jit(solution)/shard_map/ppermute | solution.py:34
  101.1 11.4 %collective-permute-start.39 = (bf16[2,128,1024]{2,1,0:T(8,128)(2,1)S(1)}, bf16[2,128,1024]{2,1,0:T(8,128)(2,1)S(1)}, u32[]{:S(2)}, u32[]{:S(2)}) collective-permute-start(bf16[2,128,1024]{2,1,0:T(8,128)(2,1)S(1)} %add.43.refs_0_), channel_id=1, source_target_pairs={{4,8},{5,9},{6,10},{7,11},{8,4},{9,5},{10,6},{11,7},{20,24},{21,25... | collective-permute-start | bytes 1572872 | tf_op jit(solution)/shard_map/ppermute | solution.py:34
  102.4 15.6 %collective-permute-start.40 = (bf16[2,128,1024]{2,1,0:T(8,128)(2,1)S(1)}, bf16[2,128,1024]{2,1,0:T(8,128)(2,1)S(1)}, u32[]{:S(2)}, u32[]{:S(2)}) collective-permute-start(bf16[2,128,1024]{2,1,0:T(8,128)(2,1)S(1)} %add.44.refs_0_), channel_id=1, source_target_pairs={{4,0},{5,1},{6,2},{7,3},{8,12},{9,13},{10,14},{11,15},{20,16},{21,... | collective-permute-start | bytes 1572872 | tf_op jit(solution)/shard_map/ppermute | solution.py:34
  111.8 10.8 %collective-permute-start.43 = (bf16[2,128,1024]{2,1,0:T(8,128)(2,1)S(1)}, bf16[2,128,1024]{2,1,0:T(8,128)(2,1)S(1)}, u32[]{:S(2)}, u32[]{:S(2)}) collective-permute-start(bf16[2,128,1024]{2,1,0:T(8,128)(2,1)S(1)} %add.45.refs_0_), channel_id=1, source_target_pairs={{4,8},{5,9},{6,10},{7,11},{8,4},{9,5},{10,6},{11,7},{20,24},{21,25... | collective-permute-start | bytes 1572872 | tf_op jit(solution)/shard_map/ppermute | solution.py:34
  113.1 16.7 %collective-permute-start.44 = (bf16[2,128,1024]{2,1,0:T(8,128)(2,1)S(1)}, bf16[2,128,1024]{2,1,0:T(8,128)(2,1)S(1)}, u32[]{:S(2)}, u32[]{:S(2)}) collective-permute-start(bf16[2,128,1024]{2,1,0:T(8,128)(2,1)S(1)} %add.46.refs_0_), channel_id=1, source_target_pairs={{4,0},{5,1},{6,2},{7,3},{8,12},{9,13},{10,14},{11,15},{20,16},{21,... | collective-permute-start | bytes 1572872 | tf_op jit(solution)/shard_map/ppermute | solution.py:34
  123.3 18.4 %collective-permute-start.48 = (bf16[2,128,1024]{2,1,0:T(8,128)(2,1)S(1)}, bf16[2,128,1024]{2,1,0:T(8,128)(2,1)S(1)}, u32[]{:S(2)}, u32[]{:S(2)}) collective-permute-start(bf16[2,128,1024]{2,1,0:T(8,128)(2,1)S(1)} %add.47.refs_0_), channel_id=1, source_target_pairs={{4,0},{5,1},{6,2},{7,3},{8,12},{9,13},{10,14},{11,15},{20,16},{21,... | collective-permute-start | bytes 1572872 | tf_op jit(solution)/shard_map/ppermute | solution.py:34
  145.6 7.9 %collective-permute-start.52 = (bf16[2,128,256]{2,1,0:T(8,128)(2,1)S(1)}, bf16[2,128,256]{2,1,0:T(8,128)(2,1)S(1)}, u32[]{:S(2)}, u32[]{:S(2)}) collective-permute-start(bf16[2,128,256]{2,1,0:T(8,128)(2,1)S(1)} %bend_half.6.refs_0_), channel_id=1, source_target_pairs={{0,2},{1,3},{2,0},{3,1},{4,6},{5,7},{6,4},{7,5},{8,10},{9,11},{10,... | collective-permute-start | bytes 393224 | tf_op jit(solution)/shard_map/ppermute | solution.py:38
  147.0 8.5 %collective-permute-start.53 = (bf16[2,128,256]{2,1,0:T(8,128)(2,1)S(1)}, bf16[2,128,256]{2,1,0:T(8,128)(2,1)S(1)}, u32[]{:S(2)}, u32[]{:S(2)}) collective-permute-start(bf16[2,128,256]{2,1,0:T(8,128)(2,1)S(1)} %bend_half.7.refs_0_), channel_id=1, source_target_pairs={{0,2},{1,3},{2,0},{3,1},{4,6},{5,7},{6,4},{7,5},{8,10},{9,11},{10,... | collective-permute-start | bytes 393224 | tf_op jit(solution)/shard_map/ppermute | solution.py:38
  (25 other events, 89.1 us)

commit v4 on v3

--- a/solution.py
+++ b/solution.py
@@ -12,7 +12,7 @@
 TEAM = ROWS * COLS
 SIZES = ((2, 2), (2, 2))
 GROUPS = ((0,), (1,), (2,), (3,))
-LAG = {"I": 1, "R": 2, "H": 1, "D": 2, "A": 3, "B": 4, "C": 5, "J": 5, "K": 7}
+LAG = {"I": 1, "R": 2, "H": 1, "D": 2, "A": 3, "B": 4, "K": 7, "C": 5, "J": 5}
 
 CORE = 2
 
@@ -71,9 +71,9 @@
             imag[...] = with_imag[:count] + with_real[count:]
 
 
-def load_kernel(where, matrix_hbm, data_hbm, *refs):
+def load_kernel(groups, where, matrix_hbm, data_hbm, _, current, scale, *refs):
     freqs = matrix_hbm.shape[0]
-    datas, matrices, sems = refs[-1 - 2 * freqs : -1 - freqs], refs[-1 - freqs : -1], refs[-1]
+    datas, matrices, sems = refs[:freqs], refs[freqs : 2 * freqs], refs[-1]
     pairs = [(data_hbm.at[f], data) for f, data in enumerate(datas)]
     pairs += [(matrix_hbm.at[f], matrix) for f, matrix in enumerate(matrices)]
     copies = [
@@ -81,6 +81,13 @@
     ]
     for copy in copies:
         copy.start()
+    for members, out in zip(groups, refs[2 * freqs : -1]):
+        place = 0
+        for f, start, size in members:
+            for c in range(2):
+                rows = current[f, c, start : start + size, :]
+                out[c, place : place + size] = (rows * scale[f : f + 1, :]).astype(bf16)
+            place += size
     for copy in copies:
         copy.wait()
 
@@ -188,17 +195,21 @@
     out_sums[1] = sums[1] + squares(value)
 
 
-def spread_kernel(where, sums, out):
-    rows = [jnp.sum(sums[n], axis=0, keepdims=True) for n in range(2)]
-    out[...] = jnp.broadcast_to(jnp.concatenate(rows * 4, axis=0)[None], out.shape)
+def spread_kernel(where, *refs):
+    *refs, out = refs
+    bend_kernel(where, *refs)
+    gamma, bent = (jnp.sum(refs[-2][n], keepdims=True) for n in range(2))
+    lane = lax.broadcasted_iota(jnp.int32, out.shape, 1)
+    out[...] = jnp.where(lane < out.shape[1] // 2, gamma, bent)
 
 
 def update_kernel(chunks, where, sums, current, *refs):
     n = len(chunks)
     descents, residuals, curvatures = refs[:n], refs[n : 2 * n], refs[2 * n : 3 * n]
     new_iterate, new_residual = refs[3 * n :]
-    total = jnp.sum(sums[...], axis=0)
-    step = jnp.sum(total[:1], keepdims=True) / jnp.sum(total[1:2], keepdims=True)
+    total = jnp.sum(sums[...], axis=0, keepdims=True)
+    middle = total.shape[1] // 2
+    step = total[:, :1] / total[:, middle : middle + 1]
     slab = new_residual.shape[3] // COLS
     for (f, start, size), descent, residual, curvature in zip(
         chunks, descents, residuals, curvatures
@@ -256,26 +267,27 @@
     own_scales = lax.dynamic_slice(
         scales, (index // TEAM * freqs, index % ROWS * row_len), (freqs, row_len)
     )
-    owns = [
-        jnp.concatenate(
-            [current[f, :, start : start + rows] * own_scales[f] for f, start, rows in members], 1
-        ).astype(bf16)
-        for members in sent
-    ]
+    f, start, rows = sent[0][0]
+    owns = [(current[f, :, start : start + rows] * own_scales[f]).astype(bf16)]
     staged = chain(
-        load_kernel,
+        functools.partial(load_kernel, sent[1:]),
         "load",
-        [shape(data.shape[1:], f32)] * freqs + [shape(matrix.shape[1:], bf16)] * freqs,
+        [shape(data.shape[1:], f32)] * freqs
+        + [shape(matrix.shape[1:], bf16)] * freqs
+        + [shape((2, sum(c[2] for c in members), row_len), bf16) for members in sent[1:]],
         matrix,
         data,
-        *owns,
-        specs=[HBM] * 2 + [ANY] * len(owns),
+        owns[0],
+        current,
+        own_scales,
+        specs=[HBM] * 2 + [ANY] + [VMEM] * 2,
         scratch=[pltpu.SemaphoreType.DMA((2 * freqs,))],
     )
-    data, matrices = staged[:freqs], staged[freqs:]
+    data, matrices = staged[:freqs], staged[freqs : 2 * freqs]
+    owns += staged[2 * freqs :]
     other_data = [swap(rows, 1) for rows in data]
     values = [{} for _ in chunks]
-    totals = [jnp.zeros((2, 8, 128), f32)]
+    totals, spread = [jnp.zeros((2, 8, 128), f32)], []
 
     for members, own in zip(GROUPS, owns):
         gathered = (own, *(along_columns(own, moves) for moves in SHIFTS))
@@ -355,10 +367,12 @@
             )
             v["far"] = swap(low, 1)
         elif kind == "K":
-            totals[0], v["curvature"] = chain(
-                bend_kernel,
+            last = n == len(chunks) - 1
+            totals[0], v["curvature"], *spread[:] = chain(
+                spread_kernel if last else bend_kernel,
                 "bend",
-                [shape((2, 8, 128), f32), shape((2, count, width), f32)],
+                [shape((2, 8, 128), f32), shape((2, count, width), f32)]
+                + [shape((TEAM, 128), f32)] * last,
                 v["keep"],
                 *v["got"],
                 v["far"],
@@ -371,10 +385,9 @@
             if 0 <= turn - lag < len(chunks):
                 step(kind, turn - lag)
 
-    (sums,) = chain(spread_kernel, "spread", [shape((TEAM, 8, 128), f32)], totals[0])
     teams = lax.axis_size("freq") // TEAM
     members = [[TEAM * g + d for d in range(TEAM)] for g in range(teams)]
-    sums = lax.all_to_all(sums, "freq", 0, 0, axis_index_groups=members)
+    sums = lax.all_to_all(spread[0], "freq", 0, 0, axis_index_groups=members)
     return chain(
         functools.partial(update_kernel, chunks),
         "update",

time: 170 us -> 168 us (0.988)
  waiting for transfers between devices: 45.1 us -> 40.7 us
  blocking collectives: 10.5 us -> 12.4 us
    ppermute x24, waiting for transfers between devices: 29.7 us -> 22.8 us  [along_columns(): return lax.ppermute(value, 'freq', team_pairs(pairs))]
    ppermute x30, waiting for transfers between devices: 15.4 us -> 17.9 us  [swap(): lax.ppermute(value, 'freq', team_pairs([(d, d ^ 1 << bit) for d in range(...]
    all_to_all x1, blocking collectives: 10.5 us -> 12.4 us  [body(): sums = lax.all_to_all(spread[0], 'freq', 0, 0, axis_index_groups=members)]
    unnamed x6 -> x10, local copies, waits for them, and re-layouts: 4.61 us -> 6.57 us
    pallas_call x39 -> x38, Pallas kernels: 42.5 us -> 42.2 us  [__call__(): pl.pallas_call(run, in_specs=[SMEM] + [ANY] * len(token) + (specs or [VME...]
  transfers between devices with their start and end apart: 54 -> 54, of which waited for: 27 -> 26; matrix products, arithmetic and copies ran while one was open for 0% -> 0% of each run, Pallas kernels for 21% -> 21%
where the time goes in v4:
time: 168 us
  starting transfers between devices  63.6 us (38%)
  Pallas kernels  42.2 us (25%)
  waiting for transfers between devices  40.7 us (24%)
  blocking collectives  12.4 us (7%)
  local copies, waits for them, and re-layouts  6.58 us (4%)
    ppermute x24, starting transfers between devices, along_columns(): return lax.ppermute(value, 'freq', team_pairs(pairs))  47.5 us
    pallas_call x38, Pallas kernels, __call__(): pl.pallas_call(run, in_specs=[SMEM] + [ANY] * len(token) + (specs or [VME...  42.2 us
    ppermute x24, waiting for transfers between devices, along_columns(): return lax.ppermute(value, 'freq', team_pairs(pairs))  22.8 us
    ppermute x30, waiting for transfers between devices, swap(): lax.ppermute(value, 'freq', team_pairs([(d, d ^ 1 << bit) for d in range(...  17.9 us
    ppermute x30, starting transfers between devices, swap(): lax.ppermute(value, 'freq', team_pairs([(d, d ^ 1 << bit) for d in range(...  16.1 us
    all_to_all x1, blocking collectives, body(): sums = lax.all_to_all(spread[0], 'freq', 0, 0, axis_index_groups=members)  12.4 us
    unnamed x10, local copies, waits for them, and re-layouts  6.57 us
  transfers between devices with their start and end apart: 54, of which 26 were waited for; matrix products, arithmetic and copies ran while one was open for 0% of the time, Pallas kernels for 21%

profile of v4, /device:TPU:0, one launch (start us, length us, event | category | flops | bytes accessed | tf_op | source)
XLA Modules:
  0.0 167.8 jit_solution(6849976804763829892)
XLA Ops:
  2.4 3.1 %collective-permute-start = (bf16[2,32,1024]{2,1,0:T(8,128)(2,1)S(1)}, bf16[2,32,1024]{2,1,0:T(8,128)(2,1)S(1)}, u32[]{:S(2)}, u32[]{:S(2)}) collective-permute-start(bf16[2,32,1024]{2,1,0:T(8,128)(2,1)S(1)} %fusion.1.refs_2_.refs_1_), channel_id=1, source_target_pairs={{0,4},{1,5},{2,6},{3,7},{4,8},{5,9},{6,10},{7,11},{8,12},{9,13},{1... | collective-permute-start | bytes 393224 | tf_op jit(solution)/shard_map/ppermute | solution.py:34
  5.4 2.6 %collective-permute-start.1 = (bf16[2,32,1024]{2,1,0:T(8,128)(2,1)S(1)}, bf16[2,32,1024]{2,1,0:T(8,128)(2,1)S(1)}, u32[]{:S(2)}, u32[]{:S(2)}) collective-permute-start(bf16[2,32,1024]{2,1,0:T(8,128)(2,1)S(1)} %fusion.1.refs_2_.refs_1_), channel_id=1, source_target_pairs={{0,8},{1,9},{2,10},{3,11},{4,12},{5,13},{6,14},{7,15},{8,0},{9,1},... | collective-permute-start | bytes 393224 | tf_op jit(solution)/shard_map/ppermute | solution.py:34
  9.5 3.4 %copy-done.1 = bf16[1,2,2,1024,1024]{4,3,2,1,0:T(8,128)(2,1)S(1)} copy-done((bf16[1,2,2,1024,1024]{4,3,2,1,0:T(8,128)(2,1)S(1)}, bf16[1,2,2,1024,1024]{4,3,2,1,0:T(8,128)(2,1)}, u32[]{:S(2)}) %copy-start.1) | copy-done | bytes 8388632
  22.7 3.3 %collective-permute-start.5 = (bf16[2,32,1024]{2,1,0:T(8,128)(2,1)S(1)}, bf16[2,32,1024]{2,1,0:T(8,128)(2,1)S(1)}, u32[]{:S(2)}, u32[]{:S(2)}) collective-permute-start(bf16[2,32,1024]{2,1,0:T(8,128)(2,1)S(1)} %get-tuple-element.67.refs_1_), channel_id=1, source_target_pairs={{0,4},{1,5},{2,6},{3,7},{4,8},{5,9},{6,10},{7,11},{8,12},{9,13},{1... | collective-permute-start | bytes 393224 | tf_op jit(solution)/shard_map/ppermute | solution.py:34
  28.4 3.1 %collective-permute-done.5.refs_2_ = bf16[2,32,1024]{2,1,0:T(8,128)(2,1)S(1)} collective-permute-done((bf16[2,32,1024]{2,1,0:T(8,128)(2,1)S(1)}, bf16[2,32,1024]{2,1,0:T(8,128)(2,1)S(1)}, u32[]{:S(2)}, u32[]{:S(2)}) %collective-permute-start.5) | collective-permute-done | bytes 131104 | tf_op jit(solution)/shard_map/ppermute | solution.py:34
  31.5 4.8 %collective-permute-done.6.refs_3_ = bf16[2,32,1024]{2,1,0:T(8,128)(2,1)S(1)} collective-permute-done((bf16[2,32,1024]{2,1,0:T(8,128)(2,1)S(1)}, bf16[2,32,1024]{2,1,0:T(8,128)(2,1)S(1)}, u32[]{:S(2)}, u32[]{:S(2)}) %collective-permute-start.6) | collective-permute-done | bytes 131104 | tf_op jit(solution)/shard_map/ppermute | solution.py:34
  36.3 1.9 %image.5 = (f32[2,2,128,256]{3,2,1,0:T(8,128)S(1)}, f32[2,128,256]{2,1,0:T(8,128)S(1)}, f32[2,128,256]{2,1,0:T(8,128)S(1)}) custom-call(s32[4]{0:T(128)S(1)} %pad_add_fusion.where, bf16[2,2,128,256]{3,2,1,0:T(8,128)(2,1)S(1)} %half.4.refs_0_, bf16[2,32,1024]{2,1,0:T(8,128)(2,1)S(1)} %get-tuple-element.67.refs_1_, ...), custom_call_target="tpu_custom_call" | custom-call | bytes 1024 | tf_op jit(solution)/shard_map/image/pallas_call | solution.py:238
  41.7 3.3 %collective-permute-start.13 = (bf16[2,32,1024]{2,1,0:T(8,128)(2,1)S(1)}, bf16[2,32,1024]{2,1,0:T(8,128)(2,1)S(1)}, u32[]{:S(2)}, u32[]{:S(2)}) collective-permute-start(bf16[2,32,1024]{2,1,0:T(8,128)(2,1)S(1)} %get-tuple-element.73.refs_1_), channel_id=1, source_target_pairs={{0,4},{1,5},{2,6},{3,7},{4,8},{5,9},{6,10},{7,11},{8,12},{9,13},{1... | collective-permute-start | bytes 393224 | tf_op jit(solution)/shard_map/ppermute | solution.py:34
  47.3 1.9 %descent.4 = (bf16[2,128,1024]{2,1,0:T(8,128)(2,1)S(1)}, f32[2,128,1024]{2,1,0:T(8,128)S(1)}) custom-call(s32[4]{0:T(128)S(1)} %pad_add_fusion.where, bf16[2,2,128,256]{3,2,1,0:T(8,128)(2,1)S(1)} %half.5.refs_0_, bf16[2,2,128,256]{3,2,1,0:T(8,128)(2,1)S(1)} %get-tuple-element.69.refs_0_.refs_1_, ...), custom_call_target="tpu_custom_call" | custom-call | bytes 1024 | tf_op jit(solution)/shard_map/descent/pallas_call | solution.py:238
  49.2 3.2 %collective-permute-start.20 = (bf16[2,128,1024]{2,1,0:T(8,128)(2,1)S(1)}, bf16[2,128,1024]{2,1,0:T(8,128)(2,1)S(1)}, u32[]{:S(2)}, u32[]{:S(2)}) collective-permute-start(bf16[2,128,1024]{2,1,0:T(8,128)(2,1)S(1)} %get-tuple-element.72.refs_0_), channel_id=1, source_target_pairs={{0,4},{1,5},{2,6},{3,7},{12,8},{13,9},{14,10},{15,11},{16,20},{17,... | collective-permute-start | bytes 1572872 | tf_op jit(solution)/shard_map/ppermute | solution.py:34
  53.4 2.2 %collective-permute-done.14.refs_3_ = bf16[2,32,1024]{2,1,0:T(8,128)(2,1)S(1)} collective-permute-done((bf16[2,32,1024]{2,1,0:T(8,128)(2,1)S(1)}, bf16[2,32,1024]{2,1,0:T(8,128)(2,1)S(1)}, u32[]{:S(2)}, u32[]{:S(2)}) %collective-permute-start.14) | collective-permute-done | bytes 131104 | tf_op jit(solution)/shard_map/ppermute | solution.py:34
  55.6 1.9 %image.6 = (f32[2,2,128,256]{3,2,1,0:T(8,128)S(1)}, f32[2,128,256]{2,1,0:T(8,128)S(1)}, f32[2,128,256]{2,1,0:T(8,128)S(1)}) custom-call(s32[4]{0:T(128)S(1)} %pad_add_fusion.where, bf16[2,128,1024]{2,1,0:T(8,128)(2,1)S(1)} %get-tuple-element.72.refs_0_, bf16[2,32,1024]{2,1,0:T(8,128)(2,1)S(1)} %get-tuple-element.73.refs_1_, ...), custom_call_target="tpu_custom_call" | custom-call | bytes 1024 | tf_op jit(solution)/shard_map/image/pallas_call | solution.py:238
  59.1 3.3 %collective-permute-start.21 = (bf16[2,32,1024]{2,1,0:T(8,128)(2,1)S(1)}, bf16[2,32,1024]{2,1,0:T(8,128)(2,1)S(1)}, u32[]{:S(2)}, u32[]{:S(2)}) collective-permute-start(bf16[2,32,1024]{2,1,0:T(8,128)(2,1)S(1)} %get-tuple-element.81.refs_1_), channel_id=1, source_target_pairs={{0,4},{1,5},{2,6},{3,7},{4,8},{5,9},{6,10},{7,11},{8,12},{9,13},{1... | collective-permute-start | bytes 393224 | tf_op jit(solution)/shard_map/ppermute | solution.py:34
  65.7 1.9 %descent.5 = (bf16[2,128,1024]{2,1,0:T(8,128)(2,1)S(1)}, f32[2,128,1024]{2,1,0:T(8,128)S(1)}) custom-call(s32[4]{0:T(128)S(1)} %pad_add_fusion.where, bf16[2,2,128,256]{3,2,1,0:T(8,128)(2,1)S(1)} %half.6.refs_0_, bf16[2,2,128,256]{3,2,1,0:T(8,128)(2,1)S(1)} %get-tuple-element.76.refs_0_.refs_1_, ...), custom_call_target="tpu_custom_call" | custom-call | bytes 1024 | tf_op jit(solution)/shard_map/descent/pallas_call | solution.py:238
  70.1 2.8 %collective-permute-start.29 = (bf16[2,128,1024]{2,1,0:T(8,128)(2,1)S(1)}, bf16[2,128,1024]{2,1,0:T(8,128)(2,1)S(1)}, u32[]{:S(2)}, u32[]{:S(2)}) collective-permute-start(bf16[2,128,1024]{2,1,0:T(8,128)(2,1)S(1)} %get-tuple-element.79.refs_0_), channel_id=1, source_target_pairs={{0,4},{1,5},{2,6},{3,7},{12,8},{13,9},{14,10},{15,11},{16,20},{17,... | collective-permute-start | bytes 1572872 | tf_op jit(solution)/shard_map/ppermute | solution.py:34
  72.9 2.1 %collective-permute-done.22.refs_3_ = bf16[2,32,1024]{2,1,0:T(8,128)(2,1)S(1)} collective-permute-done((bf16[2,32,1024]{2,1,0:T(8,128)(2,1)S(1)}, bf16[2,32,1024]{2,1,0:T(8,128)(2,1)S(1)}, u32[]{:S(2)}, u32[]{:S(2)}) %collective-permute-start.22) | collective-permute-done | bytes 131104 | tf_op jit(solution)/shard_map/ppermute | solution.py:34
  75.8 1.9 %image.7 = (f32[2,2,128,256]{3,2,1,0:T(8,128)S(1)}, f32[2,128,256]{2,1,0:T(8,128)S(1)}, f32[2,128,256]{2,1,0:T(8,128)S(1)}) custom-call(s32[4]{0:T(128)S(1)} %pad_add_fusion.where, bf16[2,128,1024]{2,1,0:T(8,128)(2,1)S(1)} %add.39.refs_0_, bf16[2,32,1024]{2,1,0:T(8,128)(2,1)S(1)} %get-tuple-element.81.refs_1_, ...), custom_call_target="tpu_custom_call" | custom-call | bytes 1024 | tf_op jit(solution)/shard_map/image/pallas_call | solution.py:238
  80.7 1.9 %descent.6 = (bf16[2,128,1024]{2,1,0:T(8,128)(2,1)S(1)}, f32[2,128,1024]{2,1,0:T(8,128)S(1)}) custom-call(s32[4]{0:T(128)S(1)} %pad_add_fusion.where, bf16[2,2,128,256]{3,2,1,0:T(8,128)(2,1)S(1)} %half.7.refs_0_, bf16[2,2,128,256]{3,2,1,0:T(8,128)(2,1)S(1)} %get-tuple-element.84.refs_0_.refs_1_, ...), custom_call_target="tpu_custom_call" | custom-call | bytes 1024 | tf_op jit(solution)/shard_map/descent/pallas_call | solution.py:238
  82.5 4.6 %collective-permute-start.33 = (bf16[2,128,1024]{2,1,0:T(8,128)(2,1)S(1)}, bf16[2,128,1024]{2,1,0:T(8,128)(2,1)S(1)}, u32[]{:S(2)}, u32[]{:S(2)}) collective-permute-start(bf16[2,128,1024]{2,1,0:T(8,128)(2,1)S(1)} %get-tuple-element.87.refs_0_), channel_id=1, source_target_pairs={{0,4},{1,5},{2,6},{3,7},{12,8},{13,9},{14,10},{15,11},{16,20},{17,... | collective-permute-start | bytes 1572872 | tf_op jit(solution)/shard_map/ppermute | solution.py:34
  92.9 1.9 %descent.7 = (bf16[2,128,1024]{2,1,0:T(8,128)(2,1)S(1)}, f32[2,128,1024]{2,1,0:T(8,128)S(1)}) custom-call(s32[4]{0:T(128)S(1)} %pad_add_fusion.where, bf16[2,2,128,256]{3,2,1,0:T(8,128)(2,1)S(1)} %get-tuple-element.89.refs_0_.refs_1_, bf16[2,2,128,256]{3,2,1,0:T(8,128)(2,1)S(1)} %get-tuple-element.89.refs_0_.refs_1_, ...), custom_call_target="tpu_custom_call" | custom-call | bytes 1024 | tf_op jit(solution)/shard_map/descent/pallas_call | solution.py:238
  94.8 4.6 %collective-permute-start.38 = (bf16[2,128,1024]{2,1,0:T(8,128)(2,1)S(1)}, bf16[2,128,1024]{2,1,0:T(8,128)(2,1)S(1)}, u32[]{:S(2)}, u32[]{:S(2)}) collective-permute-start(bf16[2,128,1024]{2,1,0:T(8,128)(2,1)S(1)} %get-tuple-element.90.refs_0_), channel_id=1, source_target_pairs={{0,4},{1,5},{2,6},{3,7},{12,8},{13,9},{14,10},{15,11},{16,20},{17,... | collective-permute-start | bytes 1572872 | tf_op jit(solution)/shard_map/ppermute | solution.py:34
  104.4 2.0 %curvature.4 = (f32[2,2,128,256]{3,2,1,0:T(8,128)S(1)}, f32[2,128,256]{2,1,0:T(8,128)S(1)}, f32[2,128,256]{2,1,0:T(8,128)S(1)}, f32[2,32,1024]{2,1,0:T(8,128)S(1)}) custom-call(s32[4]{0:T(128)S(1)} %pad_add_fusion.where, bf16[2,128,1024]{2,1,0:T(8,128)(2,1)S(1)} %add.43.refs_0_, f32[2,128,1024]{2,1,0:T(8,128)S(1)} %get-tuple-element.80.refs_1_, ...), custom_call_target="tpu_custom_call" | custom-call | bytes 1024 | tf_op jit(solution)/shard_map/curvature/pallas_call | solution.py:238
  114.1 2.9 %collective-permute-done.40.refs_4_ = bf16[2,128,1024]{2,1,0:T(8,128)(2,1)S(1)} collective-permute-done((bf16[2,128,1024]{2,1,0:T(8,128)(2,1)S(1)}, bf16[2,128,1024]{2,1,0:T(8,128)(2,1)S(1)}, u32[]{:S(2)}, u32[]{:S(2)}) %collective-permute-start.40) | collective-permute-done | bytes 524320 | tf_op jit(solution)/shard_map/ppermute | solution.py:34
  117.0 2.0 %curvature.5 = (f32[2,2,128,256]{3,2,1,0:T(8,128)S(1)}, f32[2,128,256]{2,1,0:T(8,128)S(1)}, f32[2,128,256]{2,1,0:T(8,128)S(1)}, f32[2,32,1024]{2,1,0:T(8,128)S(1)}) custom-call(s32[4]{0:T(128)S(1)} %pad_add_fusion.where, bf16[2,128,1024]{2,1,0:T(8,128)(2,1)S(1)} %add.45.refs_0_, f32[2,128,1024]{2,1,0:T(8,128)S(1)} %get-tuple-element.88.refs_1_, ...), custom_call_target="tpu_custom_call" | custom-call | bytes 1024 | tf_op jit(solution)/shard_map/curvature/pallas_call | solution.py:238
  124.9 4.3 %collective-permute-done.44.refs_4_ = bf16[2,128,256]{2,1,0:T(8,128)(2,1)S(1)} collective-permute-done((bf16[2,128,256]{2,1,0:T(8,128)(2,1)S(1)}, bf16[2,128,256]{2,1,0:T(8,128)(2,1)S(1)}, u32[]{:S(2)}, u32[]{:S(2)}) %collective-permute-start.44) | collective-permute-done | bytes 131104 | tf_op jit(solution)/shard_map/ppermute | solution.py:38
  129.9 2.0 %curvature.6 = (f32[2,2,128,256]{3,2,1,0:T(8,128)S(1)}, f32[2,128,256]{2,1,0:T(8,128)S(1)}, f32[2,128,256]{2,1,0:T(8,128)S(1)}, f32[2,32,1024]{2,1,0:T(8,128)S(1)}) custom-call(s32[4]{0:T(128)S(1)} %pad_add_fusion.where, f32[2,8,128]{2,1,0:T(8,128)S(1)} %get-tuple-element.100.refs_0_.refs_6_, f32[2,128,1024]{2,1,0:T(8,128)S(1)} %get-tuple-element.91.refs_1_, ...), custom_call_target="tpu_custom_call" | custom-call | bytes 1024 | tf_op jit(solution)/shard_map/curvature/pallas_call | solution.py:238
  134.5 3.5 %collective-permute-done.48.refs_4_ = bf16[2,128,256]{2,1,0:T(8,128)(2,1)S(1)} collective-permute-done((bf16[2,128,256]{2,1,0:T(8,128)(2,1)S(1)}, bf16[2,128,256]{2,1,0:T(8,128)(2,1)S(1)}, u32[]{:S(2)}, u32[]{:S(2)}) %collective-permute-start.48) | collective-permute-done | bytes 131104 | tf_op jit(solution)/shard_map/ppermute | solution.py:38
  138.7 2.7 %collective-permute-done.49.refs_4_ = bf16[2,128,1024]{2,1,0:T(8,128)(2,1)S(1)} collective-permute-done((bf16[2,128,1024]{2,1,0:T(8,128)(2,1)S(1)}, bf16[2,128,1024]{2,1,0:T(8,128)(2,1)S(1)}, u32[]{:S(2)}, u32[]{:S(2)}) %collective-permute-start.49) | collective-permute-done | bytes 524320 | tf_op jit(solution)/shard_map/ppermute | solution.py:34
  141.4 2.0 %curvature.7 = (f32[2,2,128,256]{3,2,1,0:T(8,128)S(1)}, f32[2,128,256]{2,1,0:T(8,128)S(1)}, f32[2,128,256]{2,1,0:T(8,128)S(1)}, f32[2,32,1024]{2,1,0:T(8,128)S(1)}) custom-call(s32[4]{0:T(128)S(1)} %pad_add_fusion.where, f32[2,8,128]{2,1,0:T(8,128)S(1)} %get-tuple-element.105.refs_0_.refs_6_, f32[2,128,1024]{2,1,0:T(8,128)S(1)} %get-tuple-element.95.refs_1_, ...), custom_call_target="tpu_custom_call" | custom-call | bytes 1024 | tf_op jit(solution)/shard_map/curvature/pallas_call | solution.py:238
  147.3 2.8 %collective-permute-done.52.refs_4_ = bf16[2,128,256]{2,1,0:T(8,128)(2,1)S(1)} collective-permute-done((bf16[2,128,256]{2,1,0:T(8,128)(2,1)S(1)}, bf16[2,128,256]{2,1,0:T(8,128)(2,1)S(1)}, u32[]{:S(2)}, u32[]{:S(2)}) %collective-permute-start.52) | collective-permute-done | bytes 131104 | tf_op jit(solution)/shard_map/ppermute | solution.py:38
  153.1 12.4 %all_to_all.11 = f32[16,1,128]{2,1,0:T(1,128)S(1)} all-to-all(f32[16,1,128]{2,1,0:T(1,128)S(1)} %bitcast.24), channel_id=1, replica_groups={{0,1,2,3,4,5,6,7,8,9,10,11,12,13,14,15},{16,17,18,19,20,21,22,23,24,25,..., dimensions={0} | all-to-all | bytes 16384 | tf_op jit(solution)/shard_map/all_to_all | solution.py:390
  165.6 2.2 %update.1 = (f32[1,2,2,64,1024]{4,3,2,1,0:T(8,128)}, f32[1,2,2,256,256]{4,3,2,1,0:T(8,128)}) custom-call(s32[4]{0:T(128)S(1)} %pad_add_fusion.where, f32[2,8,128]{2,1,0:T(8,128)S(1)} %get-tuple-element.112.refs_0_, f32[16,128]{1,0:T(8,128)S(1)} %bitcast.23, f32[2,2,64,1024]{3,2,1,0:T(8,128)S(1)} %bitcast.21, ...), custom_call_target="tpu_custom_call" | custom-call | bytes 1024 | tf_op jit(solution)/shard_map/update/pallas_call | solution.py:238
  (130 shorter events, 68.2 us)
Async XLA Ops:
  2.4 14.2 %collective-permute-start = (bf16[2,32,1024]{2,1,0:T(8,128)(2,1)S(1)}, bf16[2,32,1024]{2,1,0:T(8,128)(2,1)S(1)}, u32[]{:S(2)}, u32[]{:S(2)}) collective-permute-start(bf16[2,32,1024]{2,1,0:T(8,128)(2,1)S(1)} %fusion.1.refs_2_.refs_1_), channel_id=1, source_target_pairs={{0,4},{1,5},{2,6},{3,7},{4,8},{5,9},{6,10},{7,11},{8,12},{9,13},{1... | collective-permute-start | bytes 393224 | tf_op jit(solution)/shard_map/ppermute | solution.py:34
  5.4 11.2 %collective-permute-start.1 = (bf16[2,32,1024]{2,1,0:T(8,128)(2,1)S(1)}, bf16[2,32,1024]{2,1,0:T(8,128)(2,1)S(1)}, u32[]{:S(2)}, u32[]{:S(2)}) collective-permute-start(bf16[2,32,1024]{2,1,0:T(8,128)(2,1)S(1)} %fusion.1.refs_2_.refs_1_), channel_id=1, source_target_pairs={{0,8},{1,9},{2,10},{3,11},{4,12},{5,13},{6,14},{7,15},{8,0},{9,1},... | collective-permute-start | bytes 393224 | tf_op jit(solution)/shard_map/ppermute | solution.py:34
  8.0 8.6 %collective-permute-start.2 = (bf16[2,32,1024]{2,1,0:T(8,128)(2,1)S(1)}, bf16[2,32,1024]{2,1,0:T(8,128)(2,1)S(1)}, u32[]{:S(2)}, u32[]{:S(2)}) collective-permute-start(bf16[2,32,1024]{2,1,0:T(8,128)(2,1)S(1)} %fusion.1.refs_2_.refs_1_), channel_id=1, source_target_pairs={{0,12},{1,13},{2,14},{3,15},{4,0},{5,1},{6,2},{7,3},{8,4},{9,5},{1... | collective-permute-start | bytes 393224 | tf_op jit(solution)/shard_map/ppermute | solution.py:34
  19.1 19.6 %collective-permute-start.9 = (f32[2,256,256]{2,1,0:T(8,128)S(1)}, f32[2,256,256]{2,1,0:T(8,128)S(1)}, u32[]{:S(2)}, u32[]{:S(2)}) collective-permute-start(f32[2,256,256]{2,1,0:T(8,128)S(1)} %get-tuple-element.62.refs_0_.refs_5_), channel_id=1, source_target_pairs={{0,2},{1,3},{2,0},{3,1},{4,6},{5,7},{6,4},{7,5},{8,10},{9,11},{10,... | collective-permute-start | bytes 1572872 | tf_op jit(solution)/shard_map/ppermute | solution.py:38
  21.3 17.5 %collective-permute-start.8 = (bf16[2,2,128,256]{3,2,1,0:T(8,128)(2,1)S(1)}, bf16[2,2,128,256]{3,2,1,0:T(8,128)(2,1)S(1)}, u32[]{:S(2)}, u32[]{:S(2)}) collective-permute-start(bf16[2,2,128,256]{3,2,1,0:T(8,128)(2,1)S(1)} %half.4.refs_0_), channel_id=1, source_target_pairs={{0,2},{1,3},{2,0},{3,1},{4,6},{5,7},{6,4},{7,5},{8,10},{9,11},{10,... | collective-permute-start | bytes 786440 | tf_op jit(solution)/shard_map/ppermute | solution.py:38
  22.7 8.8 %collective-permute-start.5 = (bf16[2,32,1024]{2,1,0:T(8,128)(2,1)S(1)}, bf16[2,32,1024]{2,1,0:T(8,128)(2,1)S(1)}, u32[]{:S(2)}, u32[]{:S(2)}) collective-permute-start(bf16[2,32,1024]{2,1,0:T(8,128)(2,1)S(1)} %get-tuple-element.67.refs_1_), channel_id=1, source_target_pairs={{0,4},{1,5},{2,6},{3,7},{4,8},{5,9},{6,10},{7,11},{8,12},{9,13},{1... | collective-permute-start | bytes 393224 | tf_op jit(solution)/shard_map/ppermute | solution.py:34
  26.0 10.3 %collective-permute-start.6 = (bf16[2,32,1024]{2,1,0:T(8,128)(2,1)S(1)}, bf16[2,32,1024]{2,1,0:T(8,128)(2,1)S(1)}, u32[]{:S(2)}, u32[]{:S(2)}) collective-permute-start(bf16[2,32,1024]{2,1,0:T(8,128)(2,1)S(1)} %get-tuple-element.67.refs_1_), channel_id=1, source_target_pairs={{0,8},{1,9},{2,10},{3,11},{4,12},{5,13},{6,14},{7,15},{8,0},{9,1},... | collective-permute-start | bytes 393224 | tf_op jit(solution)/shard_map/ppermute | solution.py:34
  27.6 8.7 %collective-permute-start.7 = (bf16[2,32,1024]{2,1,0:T(8,128)(2,1)S(1)}, bf16[2,32,1024]{2,1,0:T(8,128)(2,1)S(1)}, u32[]{:S(2)}, u32[]{:S(2)}) collective-permute-start(bf16[2,32,1024]{2,1,0:T(8,128)(2,1)S(1)} %get-tuple-element.67.refs_1_), channel_id=1, source_target_pairs={{0,12},{1,13},{2,14},{3,15},{4,0},{5,1},{6,2},{7,3},{8,4},{9,5},{1... | collective-permute-start | bytes 393224 | tf_op jit(solution)/shard_map/ppermute | solution.py:34
  39.5 7.8 %collective-permute-start.12 = (bf16[2,2,128,256]{3,2,1,0:T(8,128)(2,1)S(1)}, bf16[2,2,128,256]{3,2,1,0:T(8,128)(2,1)S(1)}, u32[]{:S(2)}, u32[]{:S(2)}) collective-permute-start(bf16[2,2,128,256]{3,2,1,0:T(8,128)(2,1)S(1)} %get-tuple-element.69.refs_0_.refs_1_), channel_id=1, source_target_pairs={{0,1},{1,0},{2,3},{3,2},{4,5},{5,4},{6,7},{7,6},{8,9},{9,8},{10,11... | collective-permute-start | bytes 786440 | tf_op jit(solution)/shard_map/ppermute | solution.py:38
  40.8 17.2 %collective-permute-start.16 = (bf16[2,2,128,256]{3,2,1,0:T(8,128)(2,1)S(1)}, bf16[2,2,128,256]{3,2,1,0:T(8,128)(2,1)S(1)}, u32[]{:S(2)}, u32[]{:S(2)}) collective-permute-start(bf16[2,2,128,256]{3,2,1,0:T(8,128)(2,1)S(1)} %half.5.refs_0_), channel_id=1, source_target_pairs={{0,2},{1,3},{2,0},{3,1},{4,6},{5,7},{6,4},{7,5},{8,10},{9,11},{10,... | collective-permute-start | bytes 786440 | tf_op jit(solution)/shard_map/ppermute | solution.py:38
  41.7 10.8 %collective-permute-start.13 = (bf16[2,32,1024]{2,1,0:T(8,128)(2,1)S(1)}, bf16[2,32,1024]{2,1,0:T(8,128)(2,1)S(1)}, u32[]{:S(2)}, u32[]{:S(2)}) collective-permute-start(bf16[2,32,1024]{2,1,0:T(8,128)(2,1)S(1)} %get-tuple-element.73.refs_1_), channel_id=1, source_target_pairs={{0,4},{1,5},{2,6},{3,7},{4,8},{5,9},{6,10},{7,11},{8,12},{9,13},{1... | collective-permute-start | bytes 393224 | tf_op jit(solution)/shard_map/ppermute | solution.py:34
  44.9 10.6 %collective-permute-start.14 = (bf16[2,32,1024]{2,1,0:T(8,128)(2,1)S(1)}, bf16[2,32,1024]{2,1,0:T(8,128)(2,1)S(1)}, u32[]{:S(2)}, u32[]{:S(2)}) collective-permute-start(bf16[2,32,1024]{2,1,0:T(8,128)(2,1)S(1)} %get-tuple-element.73.refs_1_), channel_id=1, source_target_pairs={{0,8},{1,9},{2,10},{3,11},{4,12},{5,13},{6,14},{7,15},{8,0},{9,1},... | collective-permute-start | bytes 393224 | tf_op jit(solution)/shard_map/ppermute | solution.py:34
  46.6 9.0 %collective-permute-start.15 = (bf16[2,32,1024]{2,1,0:T(8,128)(2,1)S(1)}, bf16[2,32,1024]{2,1,0:T(8,128)(2,1)S(1)}, u32[]{:S(2)}, u32[]{:S(2)}) collective-permute-start(bf16[2,32,1024]{2,1,0:T(8,128)(2,1)S(1)} %get-tuple-element.73.refs_1_), channel_id=1, source_target_pairs={{0,12},{1,13},{2,14},{3,15},{4,0},{5,1},{6,2},{7,3},{8,4},{9,5},{1... | collective-permute-start | bytes 393224 | tf_op jit(solution)/shard_map/ppermute | solution.py:34
  49.2 18.4 %collective-permute-start.20 = (bf16[2,128,1024]{2,1,0:T(8,128)(2,1)S(1)}, bf16[2,128,1024]{2,1,0:T(8,128)(2,1)S(1)}, u32[]{:S(2)}, u32[]{:S(2)}) collective-permute-start(bf16[2,128,1024]{2,1,0:T(8,128)(2,1)S(1)} %get-tuple-element.72.refs_0_), channel_id=1, source_target_pairs={{0,4},{1,5},{2,6},{3,7},{12,8},{13,9},{14,10},{15,11},{16,20},{17,... | collective-permute-start | bytes 1572872 | tf_op jit(solution)/shard_map/ppermute | solution.py:34
  52.4 25.3 %collective-permute-start.25 = (f32[2,256,256]{2,1,0:T(8,128)S(1)}, f32[2,256,256]{2,1,0:T(8,128)S(1)}, u32[]{:S(2)}, u32[]{:S(2)}) collective-permute-start(f32[2,256,256]{2,1,0:T(8,128)S(1)} %get-tuple-element.83.refs_5_), channel_id=1, source_target_pairs={{0,2},{1,3},{2,0},{3,1},{4,6},{5,7},{6,4},{7,5},{8,10},{9,11},{10,... | collective-permute-start | bytes 1572872 | tf_op jit(solution)/shard_map/ppermute | solution.py:38
  59.1 11.1 %collective-permute-start.21 = (bf16[2,32,1024]{2,1,0:T(8,128)(2,1)S(1)}, bf16[2,32,1024]{2,1,0:T(8,128)(2,1)S(1)}, u32[]{:S(2)}, u32[]{:S(2)}) collective-permute-start(bf16[2,32,1024]{2,1,0:T(8,128)(2,1)S(1)} %get-tuple-element.81.refs_1_), channel_id=1, source_target_pairs={{0,4},{1,5},{2,6},{3,7},{4,8},{5,9},{6,10},{7,11},{8,12},{9,13},{1... | collective-permute-start | bytes 393224 | tf_op jit(solution)/shard_map/ppermute | solution.py:34
  62.4 12.7 %collective-permute-start.22 = (bf16[2,32,1024]{2,1,0:T(8,128)(2,1)S(1)}, bf16[2,32,1024]{2,1,0:T(8,128)(2,1)S(1)}, u32[]{:S(2)}, u32[]{:S(2)}) collective-permute-start(bf16[2,32,1024]{2,1,0:T(8,128)(2,1)S(1)} %get-tuple-element.81.refs_1_), channel_id=1, source_target_pairs={{0,8},{1,9},{2,10},{3,11},{4,12},{5,13},{6,14},{7,15},{8,0},{9,1},... | collective-permute-start | bytes 393224 | tf_op jit(solution)/shard_map/ppermute | solution.py:34
  63.7 12.1 %collective-permute-start.23 = (bf16[2,32,1024]{2,1,0:T(8,128)(2,1)S(1)}, bf16[2,32,1024]{2,1,0:T(8,128)(2,1)S(1)}, u32[]{:S(2)}, u32[]{:S(2)}) collective-permute-start(bf16[2,32,1024]{2,1,0:T(8,128)(2,1)S(1)} %get-tuple-element.81.refs_1_), channel_id=1, source_target_pairs={{0,12},{1,13},{2,14},{3,15},{4,0},{5,1},{6,2},{7,3},{8,4},{9,5},{1... | collective-permute-start | bytes 393224 | tf_op jit(solution)/shard_map/ppermute | solution.py:34
  67.6 10.6 %collective-permute-start.24 = (bf16[2,2,128,256]{3,2,1,0:T(8,128)(2,1)S(1)}, bf16[2,2,128,256]{3,2,1,0:T(8,128)(2,1)S(1)}, u32[]{:S(2)}, u32[]{:S(2)}) collective-permute-start(bf16[2,2,128,256]{3,2,1,0:T(8,128)(2,1)S(1)} %half.6.refs_0_), channel_id=1, source_target_pairs={{0,2},{1,3},{2,0},{3,1},{4,6},{5,7},{6,4},{7,5},{8,10},{9,11},{10,... | collective-permute-start | bytes 786440 | tf_op jit(solution)/shard_map/ppermute | solution.py:38
  70.1 17.0 %collective-permute-start.29 = (bf16[2,128,1024]{2,1,0:T(8,128)(2,1)S(1)}, bf16[2,128,1024]{2,1,0:T(8,128)(2,1)S(1)}, u32[]{:S(2)}, u32[]{:S(2)}) collective-permute-start(bf16[2,128,1024]{2,1,0:T(8,128)(2,1)S(1)} %get-tuple-element.79.refs_0_), channel_id=1, source_target_pairs={{0,4},{1,5},{2,6},{3,7},{12,8},{13,9},{14,10},{15,11},{16,20},{17,... | collective-permute-start | bytes 1572872 | tf_op jit(solution)/shard_map/ppermute | solution.py:34
  75.0 13.5 %collective-permute-start.30 = (bf16[2,128,1024]{2,1,0:T(8,128)(2,1)S(1)}, bf16[2,128,1024]{2,1,0:T(8,128)(2,1)S(1)}, u32[]{:S(2)}, u32[]{:S(2)}) collective-permute-start(bf16[2,128,1024]{2,1,0:T(8,128)(2,1)S(1)} %add.39.refs_0_), channel_id=1, source_target_pairs={{4,8},{5,9},{6,10},{7,11},{8,4},{9,5},{10,6},{11,7},{20,24},{21,25... | collective-permute-start | bytes 1572872 | tf_op jit(solution)/shard_map/ppermute | solution.py:34
  80.2 10.2 %collective-permute-start.31 = (bf16[2,2,128,256]{3,2,1,0:T(8,128)(2,1)S(1)}, bf16[2,2,128,256]{3,2,1,0:T(8,128)(2,1)S(1)}, u32[]{:S(2)}, u32[]{:S(2)}) collective-permute-start(bf16[2,2,128,256]{3,2,1,0:T(8,128)(2,1)S(1)} %half.7.refs_0_), channel_id=1, source_target_pairs={{0,2},{1,3},{2,0},{3,1},{4,6},{5,7},{6,4},{7,5},{8,10},{9,11},{10,... | collective-permute-start | bytes 786440 | tf_op jit(solution)/shard_map/ppermute | solution.py:38
  82.5 16.9 %collective-permute-start.33 = (bf16[2,128,1024]{2,1,0:T(8,128)(2,1)S(1)}, bf16[2,128,1024]{2,1,0:T(8,128)(2,1)S(1)}, u32[]{:S(2)}, u32[]{:S(2)}) collective-permute-start(bf16[2,128,1024]{2,1,0:T(8,128)(2,1)S(1)} %get-tuple-element.87.refs_0_), channel_id=1, source_target_pairs={{0,4},{1,5},{2,6},{3,7},{12,8},{13,9},{14,10},{15,11},{16,20},{17,... | collective-permute-start | bytes 1572872 | tf_op jit(solution)/shard_map/ppermute | solution.py:34
  87.8 13.0 %collective-permute-start.34 = (bf16[2,128,1024]{2,1,0:T(8,128)(2,1)S(1)}, bf16[2,128,1024]{2,1,0:T(8,128)(2,1)S(1)}, u32[]{:S(2)}, u32[]{:S(2)}) collective-permute-start(bf16[2,128,1024]{2,1,0:T(8,128)(2,1)S(1)} %add.40.refs_0_), channel_id=1, source_target_pairs={{4,8},{5,9},{6,10},{7,11},{8,4},{9,5},{10,6},{11,7},{20,24},{21,25... | collective-permute-start | bytes 1572872 | tf_op jit(solution)/shard_map/ppermute | solution.py:34
  89.1 15.3 %collective-permute-start.35 = (bf16[2,128,1024]{2,1,0:T(8,128)(2,1)S(1)}, bf16[2,128,1024]{2,1,0:T(8,128)(2,1)S(1)}, u32[]{:S(2)}, u32[]{:S(2)}) collective-permute-start(bf16[2,128,1024]{2,1,0:T(8,128)(2,1)S(1)} %add.41.refs_0_), channel_id=1, source_target_pairs={{4,0},{5,1},{6,2},{7,3},{8,12},{9,13},{10,14},{11,15},{20,16},{21,... | collective-permute-start | bytes 1572872 | tf_op jit(solution)/shard_map/ppermute | solution.py:34
  94.8 16.0 %collective-permute-start.38 = (bf16[2,128,1024]{2,1,0:T(8,128)(2,1)S(1)}, bf16[2,128,1024]{2,1,0:T(8,128)(2,1)S(1)}, u32[]{:S(2)}, u32[]{:S(2)}) collective-permute-start(bf16[2,128,1024]{2,1,0:T(8,128)(2,1)S(1)} %get-tuple-element.90.refs_0_), channel_id=1, source_target_pairs={{0,4},{1,5},{2,6},{3,7},{12,8},{13,9},{14,10},{15,11},{16,20},{17,... | collective-permute-start | bytes 1572872 | tf_op jit(solution)/shard_map/ppermute | solution.py:34
  100.1 12.1 %collective-permute-start.39 = (bf16[2,128,1024]{2,1,0:T(8,128)(2,1)S(1)}, bf16[2,128,1024]{2,1,0:T(8,128)(2,1)S(1)}, u32[]{:S(2)}, u32[]{:S(2)}) collective-permute-start(bf16[2,128,1024]{2,1,0:T(8,128)(2,1)S(1)} %add.42.refs_0_), channel_id=1, source_target_pairs={{4,8},{5,9},{6,10},{7,11},{8,4},{9,5},{10,6},{11,7},{20,24},{21,25... | collective-permute-start | bytes 1572872 | tf_op jit(solution)/shard_map/ppermute | solution.py:34
  101.4 15.6 %collective-permute-start.40 = (bf16[2,128,1024]{2,1,0:T(8,128)(2,1)S(1)}, bf16[2,128,1024]{2,1,0:T(8,128)(2,1)S(1)}, u32[]{:S(2)}, u32[]{:S(2)}) collective-permute-start(bf16[2,128,1024]{2,1,0:T(8,128)(2,1)S(1)} %add.43.refs_0_), channel_id=1, source_target_pairs={{4,0},{5,1},{6,2},{7,3},{8,12},{9,13},{10,14},{11,15},{20,16},{21,... | collective-permute-start | bytes 1572872 | tf_op jit(solution)/shard_map/ppermute | solution.py:34
  111.5 10.1 %collective-permute-start.43 = (bf16[2,128,1024]{2,1,0:T(8,128)(2,1)S(1)}, bf16[2,128,1024]{2,1,0:T(8,128)(2,1)S(1)}, u32[]{:S(2)}, u32[]{:S(2)}) collective-permute-start(bf16[2,128,1024]{2,1,0:T(8,128)(2,1)S(1)} %add.44.refs_0_), channel_id=1, source_target_pairs={{4,8},{5,9},{6,10},{7,11},{8,4},{9,5},{10,6},{11,7},{20,24},{21,25... | collective-permute-start | bytes 1572872 | tf_op jit(solution)/shard_map/ppermute | solution.py:34
  112.8 17.1 %collective-permute-start.45 = (bf16[2,128,1024]{2,1,0:T(8,128)(2,1)S(1)}, bf16[2,128,1024]{2,1,0:T(8,128)(2,1)S(1)}, u32[]{:S(2)}, u32[]{:S(2)}) collective-permute-start(bf16[2,128,1024]{2,1,0:T(8,128)(2,1)S(1)} %add.45.refs_0_), channel_id=1, source_target_pairs={{4,0},{5,1},{6,2},{7,3},{8,12},{9,13},{10,14},{11,15},{20,16},{21,... | collective-permute-start | bytes 1572872 | tf_op jit(solution)/shard_map/ppermute | solution.py:34
  122.3 19.1 %collective-permute-start.49 = (bf16[2,128,1024]{2,1,0:T(8,128)(2,1)S(1)}, bf16[2,128,1024]{2,1,0:T(8,128)(2,1)S(1)}, u32[]{:S(2)}, u32[]{:S(2)}) collective-permute-start(bf16[2,128,1024]{2,1,0:T(8,128)(2,1)S(1)} %add.46.refs_0_), channel_id=1, source_target_pairs={{4,0},{5,1},{6,2},{7,3},{8,12},{9,13},{10,14},{11,15},{20,16},{21,... | collective-permute-start | bytes 1572872 | tf_op jit(solution)/shard_map/ppermute | solution.py:34
  146.0 6.3 %collective-permute-start.53 = (bf16[2,128,256]{2,1,0:T(8,128)(2,1)S(1)}, bf16[2,128,256]{2,1,0:T(8,128)(2,1)S(1)}, u32[]{:S(2)}, u32[]{:S(2)}) collective-permute-start(bf16[2,128,256]{2,1,0:T(8,128)(2,1)S(1)} %bend_half.7.refs_0_), channel_id=1, source_target_pairs={{0,2},{1,3},{2,0},{3,1},{4,6},{5,7},{6,4},{7,5},{8,10},{9,11},{10,... | collective-permute-start | bytes 393224 | tf_op jit(solution)/shard_map/ppermute | solution.py:38
  (27 other events, 88.3 us)

commit v5 on v4

--- a/solution.py
+++ b/solution.py
@@ -12,7 +12,7 @@
 TEAM = ROWS * COLS
 SIZES = ((2, 2), (2, 2))
 GROUPS = ((0,), (1,), (2,), (3,))
-LAG = {"I": 1, "R": 2, "H": 1, "D": 2, "A": 3, "B": 4, "K": 7, "C": 5, "J": 5}
+LAG = {"I": 1, "R": 2, "H": 1, "D": 2, "A": 3, "B": 4, "C": 5, "J": 5, "K": 6}
 
 CORE = 2
 

time: 168 us -> 166 us (0.988)
  blocking collectives: 12.4 us -> 10.3 us
    all_to_all x1, blocking collectives: 12.4 us -> 10.3 us  [body(): sums = lax.all_to_all(spread[0], 'freq', 0, 0, axis_index_groups=members)]
    ppermute x30, waiting for transfers between devices: 17.9 us -> 16.2 us  [swap(): lax.ppermute(value, 'freq', team_pairs([(d, d ^ 1 << bit) for d in range(...]
where the time goes in v5:
time: 166 us
  starting transfers between devices  64.9 us (39%)
  Pallas kernels  42.4 us (26%)
  waiting for transfers between devices  39.4 us (24%)
  blocking collectives  10.3 us (6%)
  local copies, waits for them, and re-layouts  6.58 us (4%)
    ppermute x24, starting transfers between devices, along_columns(): return lax.ppermute(value, 'freq', team_pairs(pairs))  48.5 us
    pallas_call x38, Pallas kernels, __call__(): pl.pallas_call(run, in_specs=[SMEM] + [ANY] * len(token) + (specs or [VME...  42.4 us
    ppermute x24, waiting for transfers between devices, along_columns(): return lax.ppermute(value, 'freq', team_pairs(pairs))  23.2 us
    ppermute x30, starting transfers between devices, swap(): lax.ppermute(value, 'freq', team_pairs([(d, d ^ 1 << bit) for d in range(...  16.4 us
    ppermute x30, waiting for transfers between devices, swap(): lax.ppermute(value, 'freq', team_pairs([(d, d ^ 1 << bit) for d in range(...  16.2 us
    all_to_all x1, blocking collectives, body(): sums = lax.all_to_all(spread[0], 'freq', 0, 0, axis_index_groups=members)  10.3 us
    unnamed x10, local copies, waits for them, and re-layouts  6.57 us
  transfers between devices with their start and end apart: 54, of which 26 were waited for; matrix products, arithmetic and copies ran while one was open for 0% of the time, Pallas kernels for 21%

profile of v5, /device:TPU:0, one launch (start us, length us, event | category | flops | bytes accessed | tf_op | source)
XLA Modules:
  0.0 165.7 jit_solution(14559139780257423711)
XLA Ops:
  2.4 3.1 %collective-permute-start = (bf16[2,32,1024]{2,1,0:T(8,128)(2,1)S(1)}, bf16[2,32,1024]{2,1,0:T(8,128)(2,1)S(1)}, u32[]{:S(2)}, u32[]{:S(2)}) collective-permute-start(bf16[2,32,1024]{2,1,0:T(8,128)(2,1)S(1)} %fusion.1.refs_2_.refs_1_), channel_id=1, source_target_pairs={{0,4},{1,5},{2,6},{3,7},{4,8},{5,9},{6,10},{7,11},{8,12},{9,13},{1... | collective-permute-start | bytes 393224 | tf_op jit(solution)/shard_map/ppermute | solution.py:34
  5.4 2.6 %collective-permute-start.1 = (bf16[2,32,1024]{2,1,0:T(8,128)(2,1)S(1)}, bf16[2,32,1024]{2,1,0:T(8,128)(2,1)S(1)}, u32[]{:S(2)}, u32[]{:S(2)}) collective-permute-start(bf16[2,32,1024]{2,1,0:T(8,128)(2,1)S(1)} %fusion.1.refs_2_.refs_1_), channel_id=1, source_target_pairs={{0,8},{1,9},{2,10},{3,11},{4,12},{5,13},{6,14},{7,15},{8,0},{9,1},... | collective-permute-start | bytes 393224 | tf_op jit(solution)/shard_map/ppermute | solution.py:34
  9.5 3.4 %copy-done.1 = bf16[1,2,2,1024,1024]{4,3,2,1,0:T(8,128)(2,1)S(1)} copy-done((bf16[1,2,2,1024,1024]{4,3,2,1,0:T(8,128)(2,1)S(1)}, bf16[1,2,2,1024,1024]{4,3,2,1,0:T(8,128)(2,1)}, u32[]{:S(2)}) %copy-start.1) | copy-done | bytes 8388632
  16.7 1.9 %image.4 = (f32[2,2,128,256]{3,2,1,0:T(8,128)S(1)}, f32[2,128,256]{2,1,0:T(8,128)S(1)}, f32[2,128,256]{2,1,0:T(8,128)S(1)}) custom-call(s32[4]{0:T(128)S(1)} %pad_add_fusion.where, f32[2,256,256]{2,1,0:T(8,128)S(1)} %get-tuple-element.62.refs_0_.refs_5_, bf16[2,32,1024]{2,1,0:T(8,128)(2,1)S(1)} %fusion.1.refs_2_.refs_1_, ...), custom_call_target="tpu_custom_call" | custom-call | bytes 1024 | tf_op jit(solution)/shard_map/image/pallas_call | solution.py:238
  22.7 3.3 %collective-permute-start.5 = (bf16[2,32,1024]{2,1,0:T(8,128)(2,1)S(1)}, bf16[2,32,1024]{2,1,0:T(8,128)(2,1)S(1)}, u32[]{:S(2)}, u32[]{:S(2)}) collective-permute-start(bf16[2,32,1024]{2,1,0:T(8,128)(2,1)S(1)} %get-tuple-element.67.refs_1_), channel_id=1, source_target_pairs={{0,4},{1,5},{2,6},{3,7},{4,8},{5,9},{6,10},{7,11},{8,12},{9,13},{1... | collective-permute-start | bytes 393224 | tf_op jit(solution)/shard_map/ppermute | solution.py:34
  28.4 3.1 %collective-permute-done.5.refs_2_ = bf16[2,32,1024]{2,1,0:T(8,128)(2,1)S(1)} collective-permute-done((bf16[2,32,1024]{2,1,0:T(8,128)(2,1)S(1)}, bf16[2,32,1024]{2,1,0:T(8,128)(2,1)S(1)}, u32[]{:S(2)}, u32[]{:S(2)}) %collective-permute-start.5) | collective-permute-done | bytes 131104 | tf_op jit(solution)/shard_map/ppermute | solution.py:34
  31.5 4.8 %collective-permute-done.6.refs_3_ = bf16[2,32,1024]{2,1,0:T(8,128)(2,1)S(1)} collective-permute-done((bf16[2,32,1024]{2,1,0:T(8,128)(2,1)S(1)}, bf16[2,32,1024]{2,1,0:T(8,128)(2,1)S(1)}, u32[]{:S(2)}, u32[]{:S(2)}) %collective-permute-start.6) | collective-permute-done | bytes 131104 | tf_op jit(solution)/shard_map/ppermute | solution.py:34
  36.3 1.9 %image.5 = (f32[2,2,128,256]{3,2,1,0:T(8,128)S(1)}, f32[2,128,256]{2,1,0:T(8,128)S(1)}, f32[2,128,256]{2,1,0:T(8,128)S(1)}) custom-call(s32[4]{0:T(128)S(1)} %pad_add_fusion.where, bf16[2,2,128,256]{3,2,1,0:T(8,128)(2,1)S(1)} %half.4.refs_0_, bf16[2,32,1024]{2,1,0:T(8,128)(2,1)S(1)} %get-tuple-element.67.refs_1_, ...), custom_call_target="tpu_custom_call" | custom-call | bytes 1024 | tf_op jit(solution)/shard_map/image/pallas_call | solution.py:238
  41.7 3.3 %collective-permute-start.13 = (bf16[2,32,1024]{2,1,0:T(8,128)(2,1)S(1)}, bf16[2,32,1024]{2,1,0:T(8,128)(2,1)S(1)}, u32[]{:S(2)}, u32[]{:S(2)}) collective-permute-start(bf16[2,32,1024]{2,1,0:T(8,128)(2,1)S(1)} %get-tuple-element.73.refs_1_), channel_id=1, source_target_pairs={{0,4},{1,5},{2,6},{3,7},{4,8},{5,9},{6,10},{7,11},{8,12},{9,13},{1... | collective-permute-start | bytes 393224 | tf_op jit(solution)/shard_map/ppermute | solution.py:34
  47.3 1.9 %descent.4 = (bf16[2,128,1024]{2,1,0:T(8,128)(2,1)S(1)}, f32[2,128,1024]{2,1,0:T(8,128)S(1)}) custom-call(s32[4]{0:T(128)S(1)} %pad_add_fusion.where, bf16[2,2,128,256]{3,2,1,0:T(8,128)(2,1)S(1)} %half.5.refs_0_, bf16[2,2,128,256]{3,2,1,0:T(8,128)(2,1)S(1)} %get-tuple-element.69.refs_0_.refs_1_, ...), custom_call_target="tpu_custom_call" | custom-call | bytes 1024 | tf_op jit(solution)/shard_map/descent/pallas_call | solution.py:238
  49.2 3.2 %collective-permute-start.20 = (bf16[2,128,1024]{2,1,0:T(8,128)(2,1)S(1)}, bf16[2,128,1024]{2,1,0:T(8,128)(2,1)S(1)}, u32[]{:S(2)}, u32[]{:S(2)}) collective-permute-start(bf16[2,128,1024]{2,1,0:T(8,128)(2,1)S(1)} %get-tuple-element.72.refs_0_), channel_id=1, source_target_pairs={{0,4},{1,5},{2,6},{3,7},{12,8},{13,9},{14,10},{15,11},{16,20},{17,... | collective-permute-start | bytes 1572872 | tf_op jit(solution)/shard_map/ppermute | solution.py:34
  53.4 2.2 %collective-permute-done.14.refs_3_ = bf16[2,32,1024]{2,1,0:T(8,128)(2,1)S(1)} collective-permute-done((bf16[2,32,1024]{2,1,0:T(8,128)(2,1)S(1)}, bf16[2,32,1024]{2,1,0:T(8,128)(2,1)S(1)}, u32[]{:S(2)}, u32[]{:S(2)}) %collective-permute-start.14) | collective-permute-done | bytes 131104 | tf_op jit(solution)/shard_map/ppermute | solution.py:34
  55.6 1.9 %image.6 = (f32[2,2,128,256]{3,2,1,0:T(8,128)S(1)}, f32[2,128,256]{2,1,0:T(8,128)S(1)}, f32[2,128,256]{2,1,0:T(8,128)S(1)}) custom-call(s32[4]{0:T(128)S(1)} %pad_add_fusion.where, bf16[2,128,1024]{2,1,0:T(8,128)(2,1)S(1)} %get-tuple-element.72.refs_0_, bf16[2,32,1024]{2,1,0:T(8,128)(2,1)S(1)} %get-tuple-element.73.refs_1_, ...), custom_call_target="tpu_custom_call" | custom-call | bytes 1024 | tf_op jit(solution)/shard_map/image/pallas_call | solution.py:238
  59.1 3.3 %collective-permute-start.21 = (bf16[2,32,1024]{2,1,0:T(8,128)(2,1)S(1)}, bf16[2,32,1024]{2,1,0:T(8,128)(2,1)S(1)}, u32[]{:S(2)}, u32[]{:S(2)}) collective-permute-start(bf16[2,32,1024]{2,1,0:T(8,128)(2,1)S(1)} %get-tuple-element.81.refs_1_), channel_id=1, source_target_pairs={{0,4},{1,5},{2,6},{3,7},{4,8},{5,9},{6,10},{7,11},{8,12},{9,13},{1... | collective-permute-start | bytes 393224 | tf_op jit(solution)/shard_map/ppermute | solution.py:34
  67.0 1.9 %descent.5 = (bf16[2,128,1024]{2,1,0:T(8,128)(2,1)S(1)}, f32[2,128,1024]{2,1,0:T(8,128)S(1)}) custom-call(s32[4]{0:T(128)S(1)} %pad_add_fusion.where, bf16[2,2,128,256]{3,2,1,0:T(8,128)(2,1)S(1)} %half.6.refs_0_, bf16[2,2,128,256]{3,2,1,0:T(8,128)(2,1)S(1)} %get-tuple-element.76.refs_0_.refs_1_, ...), custom_call_target="tpu_custom_call" | custom-call | bytes 1024 | tf_op jit(solution)/shard_map/descent/pallas_call | solution.py:238
  70.1 3.8 %collective-permute-start.29 = (bf16[2,128,1024]{2,1,0:T(8,128)(2,1)S(1)}, bf16[2,128,1024]{2,1,0:T(8,128)(2,1)S(1)}, u32[]{:S(2)}, u32[]{:S(2)}) collective-permute-start(bf16[2,128,1024]{2,1,0:T(8,128)(2,1)S(1)} %get-tuple-element.79.refs_0_), channel_id=1, source_target_pairs={{0,4},{1,5},{2,6},{3,7},{12,8},{13,9},{14,10},{15,11},{16,20},{17,... | collective-permute-start | bytes 1572872 | tf_op jit(solution)/shard_map/ppermute | solution.py:34
  75.8 1.9 %image.7 = (f32[2,2,128,256]{3,2,1,0:T(8,128)S(1)}, f32[2,128,256]{2,1,0:T(8,128)S(1)}, f32[2,128,256]{2,1,0:T(8,128)S(1)}) custom-call(s32[4]{0:T(128)S(1)} %pad_add_fusion.where, bf16[2,128,1024]{2,1,0:T(8,128)(2,1)S(1)} %add.39.refs_0_, bf16[2,32,1024]{2,1,0:T(8,128)(2,1)S(1)} %get-tuple-element.81.refs_1_, ...), custom_call_target="tpu_custom_call" | custom-call | bytes 1024 | tf_op jit(solution)/shard_map/image/pallas_call | solution.py:238
  80.7 1.9 %descent.6 = (bf16[2,128,1024]{2,1,0:T(8,128)(2,1)S(1)}, f32[2,128,1024]{2,1,0:T(8,128)S(1)}) custom-call(s32[4]{0:T(128)S(1)} %pad_add_fusion.where, bf16[2,2,128,256]{3,2,1,0:T(8,128)(2,1)S(1)} %half.7.refs_0_, bf16[2,2,128,256]{3,2,1,0:T(8,128)(2,1)S(1)} %get-tuple-element.84.refs_0_.refs_1_, ...), custom_call_target="tpu_custom_call" | custom-call | bytes 1024 | tf_op jit(solution)/shard_map/descent/pallas_call | solution.py:238
  82.6 4.6 %collective-permute-start.33 = (bf16[2,128,1024]{2,1,0:T(8,128)(2,1)S(1)}, bf16[2,128,1024]{2,1,0:T(8,128)(2,1)S(1)}, u32[]{:S(2)}, u32[]{:S(2)}) collective-permute-start(bf16[2,128,1024]{2,1,0:T(8,128)(2,1)S(1)} %get-tuple-element.87.refs_0_), channel_id=1, source_target_pairs={{0,4},{1,5},{2,6},{3,7},{12,8},{13,9},{14,10},{15,11},{16,20},{17,... | collective-permute-start | bytes 1572872 | tf_op jit(solution)/shard_map/ppermute | solution.py:34
  92.9 1.9 %descent.7 = (bf16[2,128,1024]{2,1,0:T(8,128)(2,1)S(1)}, f32[2,128,1024]{2,1,0:T(8,128)S(1)}) custom-call(s32[4]{0:T(128)S(1)} %pad_add_fusion.where, bf16[2,2,128,256]{3,2,1,0:T(8,128)(2,1)S(1)} %get-tuple-element.89.refs_0_.refs_1_, bf16[2,2,128,256]{3,2,1,0:T(8,128)(2,1)S(1)} %get-tuple-element.89.refs_0_.refs_1_, ...), custom_call_target="tpu_custom_call" | custom-call | bytes 1024 | tf_op jit(solution)/shard_map/descent/pallas_call | solution.py:238
  94.8 4.6 %collective-permute-start.38 = (bf16[2,128,1024]{2,1,0:T(8,128)(2,1)S(1)}, bf16[2,128,1024]{2,1,0:T(8,128)(2,1)S(1)}, u32[]{:S(2)}, u32[]{:S(2)}) collective-permute-start(bf16[2,128,1024]{2,1,0:T(8,128)(2,1)S(1)} %get-tuple-element.90.refs_0_), channel_id=1, source_target_pairs={{0,4},{1,5},{2,6},{3,7},{12,8},{13,9},{14,10},{15,11},{16,20},{17,... | collective-permute-start | bytes 1572872 | tf_op jit(solution)/shard_map/ppermute | solution.py:34
  104.5 2.0 %curvature.4 = (f32[2,2,128,256]{3,2,1,0:T(8,128)S(1)}, f32[2,128,256]{2,1,0:T(8,128)S(1)}, f32[2,128,256]{2,1,0:T(8,128)S(1)}, f32[2,32,1024]{2,1,0:T(8,128)S(1)}) custom-call(s32[4]{0:T(128)S(1)} %pad_add_fusion.where, bf16[2,128,1024]{2,1,0:T(8,128)(2,1)S(1)} %add.43.refs_0_, f32[2,128,1024]{2,1,0:T(8,128)S(1)} %get-tuple-element.80.refs_1_, ...), custom_call_target="tpu_custom_call" | custom-call | bytes 1024 | tf_op jit(solution)/shard_map/curvature/pallas_call | solution.py:238
  114.2 2.9 %collective-permute-done.40.refs_4_ = bf16[2,128,1024]{2,1,0:T(8,128)(2,1)S(1)} collective-permute-done((bf16[2,128,1024]{2,1,0:T(8,128)(2,1)S(1)}, bf16[2,128,1024]{2,1,0:T(8,128)(2,1)S(1)}, u32[]{:S(2)}, u32[]{:S(2)}) %collective-permute-start.40) | collective-permute-done | bytes 524320 | tf_op jit(solution)/shard_map/ppermute | solution.py:34
  117.1 2.0 %curvature.5 = (f32[2,2,128,256]{3,2,1,0:T(8,128)S(1)}, f32[2,128,256]{2,1,0:T(8,128)S(1)}, f32[2,128,256]{2,1,0:T(8,128)S(1)}, f32[2,32,1024]{2,1,0:T(8,128)S(1)}) custom-call(s32[4]{0:T(128)S(1)} %pad_add_fusion.where, bf16[2,128,1024]{2,1,0:T(8,128)(2,1)S(1)} %add.45.refs_0_, f32[2,128,1024]{2,1,0:T(8,128)S(1)} %get-tuple-element.88.refs_1_, ...), custom_call_target="tpu_custom_call" | custom-call | bytes 1024 | tf_op jit(solution)/shard_map/curvature/pallas_call | solution.py:238
  121.7 3.5 %collective-permute-done.43.refs_4_ = bf16[2,128,256]{2,1,0:T(8,128)(2,1)S(1)} collective-permute-done((bf16[2,128,256]{2,1,0:T(8,128)(2,1)S(1)}, bf16[2,128,256]{2,1,0:T(8,128)(2,1)S(1)}, u32[]{:S(2)}, u32[]{:S(2)}) %collective-permute-start.43) | collective-permute-done | bytes 131104 | tf_op jit(solution)/shard_map/ppermute | solution.py:38
  129.5 2.0 %curvature.6 = (f32[2,2,128,256]{3,2,1,0:T(8,128)S(1)}, f32[2,128,256]{2,1,0:T(8,128)S(1)}, f32[2,128,256]{2,1,0:T(8,128)S(1)}, f32[2,32,1024]{2,1,0:T(8,128)S(1)}) custom-call(s32[4]{0:T(128)S(1)} %pad_add_fusion.where, bf16[2,128,1024]{2,1,0:T(8,128)(2,1)S(1)} %add.46.refs_0_, f32[2,128,1024]{2,1,0:T(8,128)S(1)} %get-tuple-element.91.refs_1_, ...), custom_call_target="tpu_custom_call" | custom-call | bytes 1024 | tf_op jit(solution)/shard_map/curvature/pallas_call | solution.py:238
  134.1 3.5 %collective-permute-done.48.refs_4_ = bf16[2,128,256]{2,1,0:T(8,128)(2,1)S(1)} collective-permute-done((bf16[2,128,256]{2,1,0:T(8,128)(2,1)S(1)}, bf16[2,128,256]{2,1,0:T(8,128)(2,1)S(1)}, u32[]{:S(2)}, u32[]{:S(2)}) %collective-permute-start.48) | collective-permute-done | bytes 131104 | tf_op jit(solution)/shard_map/ppermute | solution.py:38
  138.3 3.2 %collective-permute-done.49.refs_4_ = bf16[2,128,1024]{2,1,0:T(8,128)(2,1)S(1)} collective-permute-done((bf16[2,128,1024]{2,1,0:T(8,128)(2,1)S(1)}, bf16[2,128,1024]{2,1,0:T(8,128)(2,1)S(1)}, u32[]{:S(2)}, u32[]{:S(2)}) %collective-permute-start.49) | collective-permute-done | bytes 524320 | tf_op jit(solution)/shard_map/ppermute | solution.py:34
  141.5 2.0 %curvature.7 = (f32[2,2,128,256]{3,2,1,0:T(8,128)S(1)}, f32[2,128,256]{2,1,0:T(8,128)S(1)}, f32[2,128,256]{2,1,0:T(8,128)S(1)}, f32[2,32,1024]{2,1,0:T(8,128)S(1)}) custom-call(s32[4]{0:T(128)S(1)} %pad_add_fusion.where, f32[2,8,128]{2,1,0:T(8,128)S(1)} %get-tuple-element.105.refs_0_.refs_6_, f32[2,128,1024]{2,1,0:T(8,128)S(1)} %get-tuple-element.95.refs_1_, ...), custom_call_target="tpu_custom_call" | custom-call | bytes 1024 | tf_op jit(solution)/shard_map/curvature/pallas_call | solution.py:238
  147.4 2.8 %collective-permute-done.52.refs_4_ = bf16[2,128,256]{2,1,0:T(8,128)(2,1)S(1)} collective-permute-done((bf16[2,128,256]{2,1,0:T(8,128)(2,1)S(1)}, bf16[2,128,256]{2,1,0:T(8,128)(2,1)S(1)}, u32[]{:S(2)}, u32[]{:S(2)}) %collective-permute-start.52) | collective-permute-done | bytes 131104 | tf_op jit(solution)/shard_map/ppermute | solution.py:38
  153.2 10.3 %all_to_all.11 = f32[16,1,128]{2,1,0:T(1,128)S(1)} all-to-all(f32[16,1,128]{2,1,0:T(1,128)S(1)} %bitcast.24), channel_id=1, replica_groups={{0,1,2,3,4,5,6,7,8,9,10,11,12,13,14,15},{16,17,18,19,20,21,22,23,24,25,..., dimensions={0} | all-to-all | bytes 16384 | tf_op jit(solution)/shard_map/all_to_all | solution.py:390
  163.5 2.2 %update.1 = (f32[1,2,2,64,1024]{4,3,2,1,0:T(8,128)}, f32[1,2,2,256,256]{4,3,2,1,0:T(8,128)}) custom-call(s32[4]{0:T(128)S(1)} %pad_add_fusion.where, f32[2,8,128]{2,1,0:T(8,128)S(1)} %get-tuple-element.112.refs_0_, f32[16,128]{1,0:T(8,128)S(1)} %bitcast.23, f32[2,2,64,1024]{3,2,1,0:T(8,128)S(1)} %bitcast.21, ...), custom_call_target="tpu_custom_call" | custom-call | bytes 1024 | tf_op jit(solution)/shard_map/update/pallas_call | solution.py:238
  (130 shorter events, 67.9 us)
Async XLA Ops:
  2.4 14.2 %collective-permute-start = (bf16[2,32,1024]{2,1,0:T(8,128)(2,1)S(1)}, bf16[2,32,1024]{2,1,0:T(8,128)(2,1)S(1)}, u32[]{:S(2)}, u32[]{:S(2)}) collective-permute-start(bf16[2,32,1024]{2,1,0:T(8,128)(2,1)S(1)} %fusion.1.refs_2_.refs_1_), channel_id=1, source_target_pairs={{0,4},{1,5},{2,6},{3,7},{4,8},{5,9},{6,10},{7,11},{8,12},{9,13},{1... | collective-permute-start | bytes 393224 | tf_op jit(solution)/shard_map/ppermute | solution.py:34
  5.4 11.2 %collective-permute-start.1 = (bf16[2,32,1024]{2,1,0:T(8,128)(2,1)S(1)}, bf16[2,32,1024]{2,1,0:T(8,128)(2,1)S(1)}, u32[]{:S(2)}, u32[]{:S(2)}) collective-permute-start(bf16[2,32,1024]{2,1,0:T(8,128)(2,1)S(1)} %fusion.1.refs_2_.refs_1_), channel_id=1, source_target_pairs={{0,8},{1,9},{2,10},{3,11},{4,12},{5,13},{6,14},{7,15},{8,0},{9,1},... | collective-permute-start | bytes 393224 | tf_op jit(solution)/shard_map/ppermute | solution.py:34
  8.0 8.6 %collective-permute-start.2 = (bf16[2,32,1024]{2,1,0:T(8,128)(2,1)S(1)}, bf16[2,32,1024]{2,1,0:T(8,128)(2,1)S(1)}, u32[]{:S(2)}, u32[]{:S(2)}) collective-permute-start(bf16[2,32,1024]{2,1,0:T(8,128)(2,1)S(1)} %fusion.1.refs_2_.refs_1_), channel_id=1, source_target_pairs={{0,12},{1,13},{2,14},{3,15},{4,0},{5,1},{6,2},{7,3},{8,4},{9,5},{1... | collective-permute-start | bytes 393224 | tf_op jit(solution)/shard_map/ppermute | solution.py:34
  19.1 19.6 %collective-permute-start.9 = (f32[2,256,256]{2,1,0:T(8,128)S(1)}, f32[2,256,256]{2,1,0:T(8,128)S(1)}, u32[]{:S(2)}, u32[]{:S(2)}) collective-permute-start(f32[2,256,256]{2,1,0:T(8,128)S(1)} %get-tuple-element.62.refs_0_.refs_5_), channel_id=1, source_target_pairs={{0,2},{1,3},{2,0},{3,1},{4,6},{5,7},{6,4},{7,5},{8,10},{9,11},{10,... | collective-permute-start | bytes 1572872 | tf_op jit(solution)/shard_map/ppermute | solution.py:38
  21.3 17.5 %collective-permute-start.8 = (bf16[2,2,128,256]{3,2,1,0:T(8,128)(2,1)S(1)}, bf16[2,2,128,256]{3,2,1,0:T(8,128)(2,1)S(1)}, u32[]{:S(2)}, u32[]{:S(2)}) collective-permute-start(bf16[2,2,128,256]{3,2,1,0:T(8,128)(2,1)S(1)} %half.4.refs_0_), channel_id=1, source_target_pairs={{0,2},{1,3},{2,0},{3,1},{4,6},{5,7},{6,4},{7,5},{8,10},{9,11},{10,... | collective-permute-start | bytes 786440 | tf_op jit(solution)/shard_map/ppermute | solution.py:38
  22.7 8.8 %collective-permute-start.5 = (bf16[2,32,1024]{2,1,0:T(8,128)(2,1)S(1)}, bf16[2,32,1024]{2,1,0:T(8,128)(2,1)S(1)}, u32[]{:S(2)}, u32[]{:S(2)}) collective-permute-start(bf16[2,32,1024]{2,1,0:T(8,128)(2,1)S(1)} %get-tuple-element.67.refs_1_), channel_id=1, source_target_pairs={{0,4},{1,5},{2,6},{3,7},{4,8},{5,9},{6,10},{7,11},{8,12},{9,13},{1... | collective-permute-start | bytes 393224 | tf_op jit(solution)/shard_map/ppermute | solution.py:34
  26.0 10.3 %collective-permute-start.6 = (bf16[2,32,1024]{2,1,0:T(8,128)(2,1)S(1)}, bf16[2,32,1024]{2,1,0:T(8,128)(2,1)S(1)}, u32[]{:S(2)}, u32[]{:S(2)}) collective-permute-start(bf16[2,32,1024]{2,1,0:T(8,128)(2,1)S(1)} %get-tuple-element.67.refs_1_), channel_id=1, source_target_pairs={{0,8},{1,9},{2,10},{3,11},{4,12},{5,13},{6,14},{7,15},{8,0},{9,1},... | collective-permute-start | bytes 393224 | tf_op jit(solution)/shard_map/ppermute | solution.py:34
  27.6 8.7 %collective-permute-start.7 = (bf16[2,32,1024]{2,1,0:T(8,128)(2,1)S(1)}, bf16[2,32,1024]{2,1,0:T(8,128)(2,1)S(1)}, u32[]{:S(2)}, u32[]{:S(2)}) collective-permute-start(bf16[2,32,1024]{2,1,0:T(8,128)(2,1)S(1)} %get-tuple-element.67.refs_1_), channel_id=1, source_target_pairs={{0,12},{1,13},{2,14},{3,15},{4,0},{5,1},{6,2},{7,3},{8,4},{9,5},{1... | collective-permute-start | bytes 393224 | tf_op jit(solution)/shard_map/ppermute | solution.py:34
  39.5 7.8 %collective-permute-start.12 = (bf16[2,2,128,256]{3,2,1,0:T(8,128)(2,1)S(1)}, bf16[2,2,128,256]{3,2,1,0:T(8,128)(2,1)S(1)}, u32[]{:S(2)}, u32[]{:S(2)}) collective-permute-start(bf16[2,2,128,256]{3,2,1,0:T(8,128)(2,1)S(1)} %get-tuple-element.69.refs_0_.refs_1_), channel_id=1, source_target_pairs={{0,1},{1,0},{2,3},{3,2},{4,5},{5,4},{6,7},{7,6},{8,9},{9,8},{10,11... | collective-permute-start | bytes 786440 | tf_op jit(solution)/shard_map/ppermute | solution.py:38
  40.8 17.2 %collective-permute-start.16 = (bf16[2,2,128,256]{3,2,1,0:T(8,128)(2,1)S(1)}, bf16[2,2,128,256]{3,2,1,0:T(8,128)(2,1)S(1)}, u32[]{:S(2)}, u32[]{:S(2)}) collective-permute-start(bf16[2,2,128,256]{3,2,1,0:T(8,128)(2,1)S(1)} %half.5.refs_0_), channel_id=1, source_target_pairs={{0,2},{1,3},{2,0},{3,1},{4,6},{5,7},{6,4},{7,5},{8,10},{9,11},{10,... | collective-permute-start | bytes 786440 | tf_op jit(solution)/shard_map/ppermute | solution.py:38
  41.7 10.8 %collective-permute-start.13 = (bf16[2,32,1024]{2,1,0:T(8,128)(2,1)S(1)}, bf16[2,32,1024]{2,1,0:T(8,128)(2,1)S(1)}, u32[]{:S(2)}, u32[]{:S(2)}) collective-permute-start(bf16[2,32,1024]{2,1,0:T(8,128)(2,1)S(1)} %get-tuple-element.73.refs_1_), channel_id=1, source_target_pairs={{0,4},{1,5},{2,6},{3,7},{4,8},{5,9},{6,10},{7,11},{8,12},{9,13},{1... | collective-permute-start | bytes 393224 | tf_op jit(solution)/shard_map/ppermute | solution.py:34
  44.9 10.6 %collective-permute-start.14 = (bf16[2,32,1024]{2,1,0:T(8,128)(2,1)S(1)}, bf16[2,32,1024]{2,1,0:T(8,128)(2,1)S(1)}, u32[]{:S(2)}, u32[]{:S(2)}) collective-permute-start(bf16[2,32,1024]{2,1,0:T(8,128)(2,1)S(1)} %get-tuple-element.73.refs_1_), channel_id=1, source_target_pairs={{0,8},{1,9},{2,10},{3,11},{4,12},{5,13},{6,14},{7,15},{8,0},{9,1},... | collective-permute-start | bytes 393224 | tf_op jit(solution)/shard_map/ppermute | solution.py:34
  46.6 9.0 %collective-permute-start.15 = (bf16[2,32,1024]{2,1,0:T(8,128)(2,1)S(1)}, bf16[2,32,1024]{2,1,0:T(8,128)(2,1)S(1)}, u32[]{:S(2)}, u32[]{:S(2)}) collective-permute-start(bf16[2,32,1024]{2,1,0:T(8,128)(2,1)S(1)} %get-tuple-element.73.refs_1_), channel_id=1, source_target_pairs={{0,12},{1,13},{2,14},{3,15},{4,0},{5,1},{6,2},{7,3},{8,4},{9,5},{1... | collective-permute-start | bytes 393224 | tf_op jit(solution)/shard_map/ppermute | solution.py:34
  49.2 16.5 %collective-permute-start.20 = (bf16[2,128,1024]{2,1,0:T(8,128)(2,1)S(1)}, bf16[2,128,1024]{2,1,0:T(8,128)(2,1)S(1)}, u32[]{:S(2)}, u32[]{:S(2)}) collective-permute-start(bf16[2,128,1024]{2,1,0:T(8,128)(2,1)S(1)} %get-tuple-element.72.refs_0_), channel_id=1, source_target_pairs={{0,4},{1,5},{2,6},{3,7},{12,8},{13,9},{14,10},{15,11},{16,20},{17,... | collective-permute-start | bytes 1572872 | tf_op jit(solution)/shard_map/ppermute | solution.py:34
  52.4 25.3 %collective-permute-start.25 = (f32[2,256,256]{2,1,0:T(8,128)S(1)}, f32[2,256,256]{2,1,0:T(8,128)S(1)}, u32[]{:S(2)}, u32[]{:S(2)}) collective-permute-start(f32[2,256,256]{2,1,0:T(8,128)S(1)} %get-tuple-element.83.refs_5_), channel_id=1, source_target_pairs={{0,2},{1,3},{2,0},{3,1},{4,6},{5,7},{6,4},{7,5},{8,10},{9,11},{10,... | collective-permute-start | bytes 1572872 | tf_op jit(solution)/shard_map/ppermute | solution.py:38
  59.1 11.1 %collective-permute-start.21 = (bf16[2,32,1024]{2,1,0:T(8,128)(2,1)S(1)}, bf16[2,32,1024]{2,1,0:T(8,128)(2,1)S(1)}, u32[]{:S(2)}, u32[]{:S(2)}) collective-permute-start(bf16[2,32,1024]{2,1,0:T(8,128)(2,1)S(1)} %get-tuple-element.81.refs_1_), channel_id=1, source_target_pairs={{0,4},{1,5},{2,6},{3,7},{4,8},{5,9},{6,10},{7,11},{8,12},{9,13},{1... | collective-permute-start | bytes 393224 | tf_op jit(solution)/shard_map/ppermute | solution.py:34
  62.4 12.7 %collective-permute-start.22 = (bf16[2,32,1024]{2,1,0:T(8,128)(2,1)S(1)}, bf16[2,32,1024]{2,1,0:T(8,128)(2,1)S(1)}, u32[]{:S(2)}, u32[]{:S(2)}) collective-permute-start(bf16[2,32,1024]{2,1,0:T(8,128)(2,1)S(1)} %get-tuple-element.81.refs_1_), channel_id=1, source_target_pairs={{0,8},{1,9},{2,10},{3,11},{4,12},{5,13},{6,14},{7,15},{8,0},{9,1},... | collective-permute-start | bytes 393224 | tf_op jit(solution)/shard_map/ppermute | solution.py:34
  63.7 12.1 %collective-permute-start.23 = (bf16[2,32,1024]{2,1,0:T(8,128)(2,1)S(1)}, bf16[2,32,1024]{2,1,0:T(8,128)(2,1)S(1)}, u32[]{:S(2)}, u32[]{:S(2)}) collective-permute-start(bf16[2,32,1024]{2,1,0:T(8,128)(2,1)S(1)} %get-tuple-element.81.refs_1_), channel_id=1, source_target_pairs={{0,12},{1,13},{2,14},{3,15},{4,0},{5,1},{6,2},{7,3},{8,4},{9,5},{1... | collective-permute-start | bytes 393224 | tf_op jit(solution)/shard_map/ppermute | solution.py:34
  65.7 12.5 %collective-permute-start.24 = (bf16[2,2,128,256]{3,2,1,0:T(8,128)(2,1)S(1)}, bf16[2,2,128,256]{3,2,1,0:T(8,128)(2,1)S(1)}, u32[]{:S(2)}, u32[]{:S(2)}) collective-permute-start(bf16[2,2,128,256]{3,2,1,0:T(8,128)(2,1)S(1)} %half.6.refs_0_), channel_id=1, source_target_pairs={{0,2},{1,3},{2,0},{3,1},{4,6},{5,7},{6,4},{7,5},{8,10},{9,11},{10,... | collective-permute-start | bytes 786440 | tf_op jit(solution)/shard_map/ppermute | solution.py:38
  70.1 17.0 %collective-permute-start.29 = (bf16[2,128,1024]{2,1,0:T(8,128)(2,1)S(1)}, bf16[2,128,1024]{2,1,0:T(8,128)(2,1)S(1)}, u32[]{:S(2)}, u32[]{:S(2)}) collective-permute-start(bf16[2,128,1024]{2,1,0:T(8,128)(2,1)S(1)} %get-tuple-element.79.refs_0_), channel_id=1, source_target_pairs={{0,4},{1,5},{2,6},{3,7},{12,8},{13,9},{14,10},{15,11},{16,20},{17,... | collective-permute-start | bytes 1572872 | tf_op jit(solution)/shard_map/ppermute | solution.py:34
  75.0 13.5 %collective-permute-start.30 = (bf16[2,128,1024]{2,1,0:T(8,128)(2,1)S(1)}, bf16[2,128,1024]{2,1,0:T(8,128)(2,1)S(1)}, u32[]{:S(2)}, u32[]{:S(2)}) collective-permute-start(bf16[2,128,1024]{2,1,0:T(8,128)(2,1)S(1)} %add.39.refs_0_), channel_id=1, source_target_pairs={{4,8},{5,9},{6,10},{7,11},{8,4},{9,5},{10,6},{11,7},{20,24},{21,25... | collective-permute-start | bytes 1572872 | tf_op jit(solution)/shard_map/ppermute | solution.py:34
  80.2 10.2 %collective-permute-start.31 = (bf16[2,2,128,256]{3,2,1,0:T(8,128)(2,1)S(1)}, bf16[2,2,128,256]{3,2,1,0:T(8,128)(2,1)S(1)}, u32[]{:S(2)}, u32[]{:S(2)}) collective-permute-start(bf16[2,2,128,256]{3,2,1,0:T(8,128)(2,1)S(1)} %half.7.refs_0_), channel_id=1, source_target_pairs={{0,2},{1,3},{2,0},{3,1},{4,6},{5,7},{6,4},{7,5},{8,10},{9,11},{10,... | collective-permute-start | bytes 786440 | tf_op jit(solution)/shard_map/ppermute | solution.py:38
  82.6 16.9 %collective-permute-start.33 = (bf16[2,128,1024]{2,1,0:T(8,128)(2,1)S(1)}, bf16[2,128,1024]{2,1,0:T(8,128)(2,1)S(1)}, u32[]{:S(2)}, u32[]{:S(2)}) collective-permute-start(bf16[2,128,1024]{2,1,0:T(8,128)(2,1)S(1)} %get-tuple-element.87.refs_0_), channel_id=1, source_target_pairs={{0,4},{1,5},{2,6},{3,7},{12,8},{13,9},{14,10},{15,11},{16,20},{17,... | collective-permute-start | bytes 1572872 | tf_op jit(solution)/shard_map/ppermute | solution.py:34
  87.8 13.0 %collective-permute-start.34 = (bf16[2,128,1024]{2,1,0:T(8,128)(2,1)S(1)}, bf16[2,128,1024]{2,1,0:T(8,128)(2,1)S(1)}, u32[]{:S(2)}, u32[]{:S(2)}) collective-permute-start(bf16[2,128,1024]{2,1,0:T(8,128)(2,1)S(1)} %add.40.refs_0_), channel_id=1, source_target_pairs={{4,8},{5,9},{6,10},{7,11},{8,4},{9,5},{10,6},{11,7},{20,24},{21,25... | collective-permute-start | bytes 1572872 | tf_op jit(solution)/shard_map/ppermute | solution.py:34
  89.2 15.3 %collective-permute-start.35 = (bf16[2,128,1024]{2,1,0:T(8,128)(2,1)S(1)}, bf16[2,128,1024]{2,1,0:T(8,128)(2,1)S(1)}, u32[]{:S(2)}, u32[]{:S(2)}) collective-permute-start(bf16[2,128,1024]{2,1,0:T(8,128)(2,1)S(1)} %add.41.refs_0_), channel_id=1, source_target_pairs={{4,0},{5,1},{6,2},{7,3},{8,12},{9,13},{10,14},{11,15},{20,16},{21,... | collective-permute-start | bytes 1572872 | tf_op jit(solution)/shard_map/ppermute | solution.py:34
  94.8 16.0 %collective-permute-start.38 = (bf16[2,128,1024]{2,1,0:T(8,128)(2,1)S(1)}, bf16[2,128,1024]{2,1,0:T(8,128)(2,1)S(1)}, u32[]{:S(2)}, u32[]{:S(2)}) collective-permute-start(bf16[2,128,1024]{2,1,0:T(8,128)(2,1)S(1)} %get-tuple-element.90.refs_0_), channel_id=1, source_target_pairs={{0,4},{1,5},{2,6},{3,7},{12,8},{13,9},{14,10},{15,11},{16,20},{17,... | collective-permute-start | bytes 1572872 | tf_op jit(solution)/shard_map/ppermute | solution.py:34
  100.1 12.1 %collective-permute-start.39 = (bf16[2,128,1024]{2,1,0:T(8,128)(2,1)S(1)}, bf16[2,128,1024]{2,1,0:T(8,128)(2,1)S(1)}, u32[]{:S(2)}, u32[]{:S(2)}) collective-permute-start(bf16[2,128,1024]{2,1,0:T(8,128)(2,1)S(1)} %add.42.refs_0_), channel_id=1, source_target_pairs={{4,8},{5,9},{6,10},{7,11},{8,4},{9,5},{10,6},{11,7},{20,24},{21,25... | collective-permute-start | bytes 1572872 | tf_op jit(solution)/shard_map/ppermute | solution.py:34
  101.5 15.6 %collective-permute-start.40 = (bf16[2,128,1024]{2,1,0:T(8,128)(2,1)S(1)}, bf16[2,128,1024]{2,1,0:T(8,128)(2,1)S(1)}, u32[]{:S(2)}, u32[]{:S(2)}) collective-permute-start(bf16[2,128,1024]{2,1,0:T(8,128)(2,1)S(1)} %add.43.refs_0_), channel_id=1, source_target_pairs={{4,0},{5,1},{6,2},{7,3},{8,12},{9,13},{10,14},{11,15},{20,16},{21,... | collective-permute-start | bytes 1572872 | tf_op jit(solution)/shard_map/ppermute | solution.py:34
  111.5 14.3 %collective-permute-start.44 = (bf16[2,128,1024]{2,1,0:T(8,128)(2,1)S(1)}, bf16[2,128,1024]{2,1,0:T(8,128)(2,1)S(1)}, u32[]{:S(2)}, u32[]{:S(2)}) collective-permute-start(bf16[2,128,1024]{2,1,0:T(8,128)(2,1)S(1)} %add.44.refs_0_), channel_id=1, source_target_pairs={{4,8},{5,9},{6,10},{7,11},{8,4},{9,5},{10,6},{11,7},{20,24},{21,25... | collective-permute-start | bytes 1572872 | tf_op jit(solution)/shard_map/ppermute | solution.py:34
  112.9 16.6 %collective-permute-start.45 = (bf16[2,128,1024]{2,1,0:T(8,128)(2,1)S(1)}, bf16[2,128,1024]{2,1,0:T(8,128)(2,1)S(1)}, u32[]{:S(2)}, u32[]{:S(2)}) collective-permute-start(bf16[2,128,1024]{2,1,0:T(8,128)(2,1)S(1)} %add.45.refs_0_), channel_id=1, source_target_pairs={{4,0},{5,1},{6,2},{7,3},{8,12},{9,13},{10,14},{11,15},{20,16},{21,... | collective-permute-start | bytes 1572872 | tf_op jit(solution)/shard_map/ppermute | solution.py:34
  126.5 15.0 %collective-permute-start.49 = (bf16[2,128,1024]{2,1,0:T(8,128)(2,1)S(1)}, bf16[2,128,1024]{2,1,0:T(8,128)(2,1)S(1)}, u32[]{:S(2)}, u32[]{:S(2)}) collective-permute-start(bf16[2,128,1024]{2,1,0:T(8,128)(2,1)S(1)} %add.46.refs_0_), channel_id=1, source_target_pairs={{4,0},{5,1},{6,2},{7,3},{8,12},{9,13},{10,14},{11,15},{20,16},{21,... | collective-permute-start | bytes 1572872 | tf_op jit(solution)/shard_map/ppermute | solution.py:34
  146.1 6.3 %collective-permute-start.53 = (bf16[2,128,256]{2,1,0:T(8,128)(2,1)S(1)}, bf16[2,128,256]{2,1,0:T(8,128)(2,1)S(1)}, u32[]{:S(2)}, u32[]{:S(2)}) collective-permute-start(bf16[2,128,256]{2,1,0:T(8,128)(2,1)S(1)} %bend_half.7.refs_0_), channel_id=1, source_target_pairs={{0,2},{1,3},{2,0},{3,1},{4,6},{5,7},{6,4},{7,5},{8,10},{9,11},{10,... | collective-permute-start | bytes 393224 | tf_op jit(solution)/shard_map/ppermute | solution.py:38
  (27 other events, 86.0 us)

commit v6 on v5

--- a/solution.py
+++ b/solution.py
@@ -206,7 +206,8 @@
 def update_kernel(chunks, where, sums, current, *refs):
     n = len(chunks)
     descents, residuals, curvatures = refs[:n], refs[n : 2 * n], refs[2 * n : 3 * n]
-    new_iterate, new_residual = refs[3 * n :]
+    *results, new_iterate, new_residual, sems = refs[3 * n :]
+    copies = []
     total = jnp.sum(sums[...], axis=0, keepdims=True)
     middle = total.shape[1] // 2
     step = total[:, :1] / total[:, middle : middle + 1]
@@ -222,6 +223,13 @@
                 new_residual[0, f, c, pl.ds(s * slab + start, size)] = (
                     residual[c, rows] - step * curvature[c, rows]
                 )
+        if start + size == current.shape[2]:
+            for k, (source, target) in enumerate(zip((new_iterate, new_residual), results)):
+                copy = pltpu.make_async_copy(source.at[0, f], target.at[0, f], sems.at[2 * f + k])
+                copy.start()
+                copies.append(copy)
+    for copy in copies:
+        copy.wait()
 
 
 class Chain:
@@ -229,7 +237,7 @@
         self.where = where
         self.last = None
 
-    def __call__(self, kernel, name, out_shape, *operands, scratch=(), flops=0, specs=None):
+    def __call__(self, kernel, name, out_shape, *operands, scratch=(), flops=0, specs=None, out=VMEM):
         token = [] if self.last is None else [self.last]
 
         def run(where, *refs):
@@ -238,7 +246,7 @@
         results = pl.pallas_call(
             run,
             in_specs=[SMEM] + [ANY] * len(token) + (specs or [VMEM] * len(operands)),
-            out_specs=[VMEM] * len(out_shape),
+            out_specs=[out] * len(out_shape),
             out_shape=out_shape,
             scratch_shapes=list(scratch),
             name=name,
@@ -395,6 +403,12 @@
         sums,
         current,
         *(v[name] for name in ("own", "residual", "curvature") for v in values),
+        out=HBM,
+        scratch=[
+            pltpu.VMEM(iterate.shape, f32),
+            pltpu.VMEM(spectrum.shape, f32),
+            pltpu.SemaphoreType.DMA((2 * freqs,)),
+        ],
     )
 
 

time: 166 us -> 166 us (level)
  no operation moved by 1% of the time
where the time goes in v6:
time: 166 us
  starting transfers between devices  64.9 us (39%)
  Pallas kernels  42.3 us (25%)
  waiting for transfers between devices  39.4 us (24%)
  blocking collectives  10.3 us (6%)
  local copies, waits for them, and re-layouts  6.58 us (4%)
    ppermute x24, starting transfers between devices, along_columns(): return lax.ppermute(value, 'freq', team_pairs(pairs))  48.5 us
    pallas_call x38, Pallas kernels, __call__(): pl.pallas_call(run, in_specs=[SMEM] + [ANY] * len(token) + (specs or [VME...  42.3 us
    ppermute x24, waiting for transfers between devices, along_columns(): return lax.ppermute(value, 'freq', team_pairs(pairs))  23.2 us
    ppermute x30, starting transfers between devices, swap(): lax.ppermute(value, 'freq', team_pairs([(d, d ^ 1 << bit) for d in range(...  16.4 us
    ppermute x30, waiting for transfers between devices, swap(): lax.ppermute(value, 'freq', team_pairs([(d, d ^ 1 << bit) for d in range(...  16.2 us
    all_to_all x1, blocking collectives, body(): sums = lax.all_to_all(spread[0], 'freq', 0, 0, axis_index_groups=members)  10.3 us
    unnamed x10, local copies, waits for them, and re-layouts  6.57 us
  transfers between devices with their start and end apart: 54, of which 26 were waited for; matrix products, arithmetic and copies ran while one was open for 0% of the time, Pallas kernels for 21%

profile of v6, /device:TPU:0, one launch (start us, length us, event | category | flops | bytes accessed | tf_op | source)
XLA Modules:
  0.0 165.8 jit_solution(16033633219999806392)
XLA Ops:
  2.4 3.1 %collective-permute-start = (bf16[2,32,1024]{2,1,0:T(8,128)(2,1)S(1)}, bf16[2,32,1024]{2,1,0:T(8,128)(2,1)S(1)}, u32[]{:S(2)}, u32[]{:S(2)}) collective-permute-start(bf16[2,32,1024]{2,1,0:T(8,128)(2,1)S(1)} %fusion.1.refs_2_.refs_1_), channel_id=1, source_target_pairs={{0,4},{1,5},{2,6},{3,7},{4,8},{5,9},{6,10},{7,11},{8,12},{9,13},{1... | collective-permute-start | bytes 393224 | tf_op jit(solution)/shard_map/ppermute | solution.py:34
  5.4 2.6 %collective-permute-start.1 = (bf16[2,32,1024]{2,1,0:T(8,128)(2,1)S(1)}, bf16[2,32,1024]{2,1,0:T(8,128)(2,1)S(1)}, u32[]{:S(2)}, u32[]{:S(2)}) collective-permute-start(bf16[2,32,1024]{2,1,0:T(8,128)(2,1)S(1)} %fusion.1.refs_2_.refs_1_), channel_id=1, source_target_pairs={{0,8},{1,9},{2,10},{3,11},{4,12},{5,13},{6,14},{7,15},{8,0},{9,1},... | collective-permute-start | bytes 393224 | tf_op jit(solution)/shard_map/ppermute | solution.py:34
  9.5 3.4 %copy-done.1 = bf16[1,2,2,1024,1024]{4,3,2,1,0:T(8,128)(2,1)S(1)} copy-done((bf16[1,2,2,1024,1024]{4,3,2,1,0:T(8,128)(2,1)S(1)}, bf16[1,2,2,1024,1024]{4,3,2,1,0:T(8,128)(2,1)}, u32[]{:S(2)}) %copy-start.1) | copy-done | bytes 8388632
  16.7 1.9 %image.4 = (f32[2,2,128,256]{3,2,1,0:T(8,128)S(1)}, f32[2,128,256]{2,1,0:T(8,128)S(1)}, f32[2,128,256]{2,1,0:T(8,128)S(1)}) custom-call(s32[4]{0:T(128)S(1)} %pad_add_fusion.where, f32[2,256,256]{2,1,0:T(8,128)S(1)} %get-tuple-element.62.refs_0_.refs_5_, bf16[2,32,1024]{2,1,0:T(8,128)(2,1)S(1)} %fusion.1.refs_2_.refs_1_, ...), custom_call_target="tpu_custom_call" | custom-call | bytes 1024 | tf_op jit(solution)/shard_map/image/pallas_call | solution.py:246
  22.7 3.3 %collective-permute-start.5 = (bf16[2,32,1024]{2,1,0:T(8,128)(2,1)S(1)}, bf16[2,32,1024]{2,1,0:T(8,128)(2,1)S(1)}, u32[]{:S(2)}, u32[]{:S(2)}) collective-permute-start(bf16[2,32,1024]{2,1,0:T(8,128)(2,1)S(1)} %get-tuple-element.67.refs_1_), channel_id=1, source_target_pairs={{0,4},{1,5},{2,6},{3,7},{4,8},{5,9},{6,10},{7,11},{8,12},{9,13},{1... | collective-permute-start | bytes 393224 | tf_op jit(solution)/shard_map/ppermute | solution.py:34
  28.4 3.1 %collective-permute-done.5.refs_2_ = bf16[2,32,1024]{2,1,0:T(8,128)(2,1)S(1)} collective-permute-done((bf16[2,32,1024]{2,1,0:T(8,128)(2,1)S(1)}, bf16[2,32,1024]{2,1,0:T(8,128)(2,1)S(1)}, u32[]{:S(2)}, u32[]{:S(2)}) %collective-permute-start.5) | collective-permute-done | bytes 131104 | tf_op jit(solution)/shard_map/ppermute | solution.py:34
  31.5 4.8 %collective-permute-done.6.refs_3_ = bf16[2,32,1024]{2,1,0:T(8,128)(2,1)S(1)} collective-permute-done((bf16[2,32,1024]{2,1,0:T(8,128)(2,1)S(1)}, bf16[2,32,1024]{2,1,0:T(8,128)(2,1)S(1)}, u32[]{:S(2)}, u32[]{:S(2)}) %collective-permute-start.6) | collective-permute-done | bytes 131104 | tf_op jit(solution)/shard_map/ppermute | solution.py:34
  36.3 1.9 %image.5 = (f32[2,2,128,256]{3,2,1,0:T(8,128)S(1)}, f32[2,128,256]{2,1,0:T(8,128)S(1)}, f32[2,128,256]{2,1,0:T(8,128)S(1)}) custom-call(s32[4]{0:T(128)S(1)} %pad_add_fusion.where, bf16[2,2,128,256]{3,2,1,0:T(8,128)(2,1)S(1)} %half.4.refs_0_, bf16[2,32,1024]{2,1,0:T(8,128)(2,1)S(1)} %get-tuple-element.67.refs_1_, ...), custom_call_target="tpu_custom_call" | custom-call | bytes 1024 | tf_op jit(solution)/shard_map/image/pallas_call | solution.py:246
  41.7 3.3 %collective-permute-start.13 = (bf16[2,32,1024]{2,1,0:T(8,128)(2,1)S(1)}, bf16[2,32,1024]{2,1,0:T(8,128)(2,1)S(1)}, u32[]{:S(2)}, u32[]{:S(2)}) collective-permute-start(bf16[2,32,1024]{2,1,0:T(8,128)(2,1)S(1)} %get-tuple-element.73.refs_1_), channel_id=1, source_target_pairs={{0,4},{1,5},{2,6},{3,7},{4,8},{5,9},{6,10},{7,11},{8,12},{9,13},{1... | collective-permute-start | bytes 393224 | tf_op jit(solution)/shard_map/ppermute | solution.py:34
  47.3 1.9 %descent.4 = (bf16[2,128,1024]{2,1,0:T(8,128)(2,1)S(1)}, f32[2,128,1024]{2,1,0:T(8,128)S(1)}) custom-call(s32[4]{0:T(128)S(1)} %pad_add_fusion.where, bf16[2,2,128,256]{3,2,1,0:T(8,128)(2,1)S(1)} %half.5.refs_0_, bf16[2,2,128,256]{3,2,1,0:T(8,128)(2,1)S(1)} %get-tuple-element.69.refs_0_.refs_1_, ...), custom_call_target="tpu_custom_call" | custom-call | bytes 1024 | tf_op jit(solution)/shard_map/descent/pallas_call | solution.py:246
  49.2 3.2 %collective-permute-start.20 = (bf16[2,128,1024]{2,1,0:T(8,128)(2,1)S(1)}, bf16[2,128,1024]{2,1,0:T(8,128)(2,1)S(1)}, u32[]{:S(2)}, u32[]{:S(2)}) collective-permute-start(bf16[2,128,1024]{2,1,0:T(8,128)(2,1)S(1)} %get-tuple-element.72.refs_0_), channel_id=1, source_target_pairs={{0,4},{1,5},{2,6},{3,7},{12,8},{13,9},{14,10},{15,11},{16,20},{17,... | collective-permute-start | bytes 1572872 | tf_op jit(solution)/shard_map/ppermute | solution.py:34
  53.4 2.2 %collective-permute-done.14.refs_3_ = bf16[2,32,1024]{2,1,0:T(8,128)(2,1)S(1)} collective-permute-done((bf16[2,32,1024]{2,1,0:T(8,128)(2,1)S(1)}, bf16[2,32,1024]{2,1,0:T(8,128)(2,1)S(1)}, u32[]{:S(2)}, u32[]{:S(2)}) %collective-permute-start.14) | collective-permute-done | bytes 131104 | tf_op jit(solution)/shard_map/ppermute | solution.py:34
  55.6 1.9 %image.6 = (f32[2,2,128,256]{3,2,1,0:T(8,128)S(1)}, f32[2,128,256]{2,1,0:T(8,128)S(1)}, f32[2,128,256]{2,1,0:T(8,128)S(1)}) custom-call(s32[4]{0:T(128)S(1)} %pad_add_fusion.where, bf16[2,128,1024]{2,1,0:T(8,128)(2,1)S(1)} %get-tuple-element.72.refs_0_, bf16[2,32,1024]{2,1,0:T(8,128)(2,1)S(1)} %get-tuple-element.73.refs_1_, ...), custom_call_target="tpu_custom_call" | custom-call | bytes 1024 | tf_op jit(solution)/shard_map/image/pallas_call | solution.py:246
  59.1 3.3 %collective-permute-start.21 = (bf16[2,32,1024]{2,1,0:T(8,128)(2,1)S(1)}, bf16[2,32,1024]{2,1,0:T(8,128)(2,1)S(1)}, u32[]{:S(2)}, u32[]{:S(2)}) collective-permute-start(bf16[2,32,1024]{2,1,0:T(8,128)(2,1)S(1)} %get-tuple-element.81.refs_1_), channel_id=1, source_target_pairs={{0,4},{1,5},{2,6},{3,7},{4,8},{5,9},{6,10},{7,11},{8,12},{9,13},{1... | collective-permute-start | bytes 393224 | tf_op jit(solution)/shard_map/ppermute | solution.py:34
  67.0 1.9 %descent.5 = (bf16[2,128,1024]{2,1,0:T(8,128)(2,1)S(1)}, f32[2,128,1024]{2,1,0:T(8,128)S(1)}) custom-call(s32[4]{0:T(128)S(1)} %pad_add_fusion.where, bf16[2,2,128,256]{3,2,1,0:T(8,128)(2,1)S(1)} %half.6.refs_0_, bf16[2,2,128,256]{3,2,1,0:T(8,128)(2,1)S(1)} %get-tuple-element.76.refs_0_.refs_1_, ...), custom_call_target="tpu_custom_call" | custom-call | bytes 1024 | tf_op jit(solution)/shard_map/descent/pallas_call | solution.py:246
  70.1 3.8 %collective-permute-start.29 = (bf16[2,128,1024]{2,1,0:T(8,128)(2,1)S(1)}, bf16[2,128,1024]{2,1,0:T(8,128)(2,1)S(1)}, u32[]{:S(2)}, u32[]{:S(2)}) collective-permute-start(bf16[2,128,1024]{2,1,0:T(8,128)(2,1)S(1)} %get-tuple-element.79.refs_0_), channel_id=1, source_target_pairs={{0,4},{1,5},{2,6},{3,7},{12,8},{13,9},{14,10},{15,11},{16,20},{17,... | collective-permute-start | bytes 1572872 | tf_op jit(solution)/shard_map/ppermute | solution.py:34
  75.8 1.9 %image.7 = (f32[2,2,128,256]{3,2,1,0:T(8,128)S(1)}, f32[2,128,256]{2,1,0:T(8,128)S(1)}, f32[2,128,256]{2,1,0:T(8,128)S(1)}) custom-call(s32[4]{0:T(128)S(1)} %pad_add_fusion.where, bf16[2,128,1024]{2,1,0:T(8,128)(2,1)S(1)} %add.39.refs_0_, bf16[2,32,1024]{2,1,0:T(8,128)(2,1)S(1)} %get-tuple-element.81.refs_1_, ...), custom_call_target="tpu_custom_call" | custom-call | bytes 1024 | tf_op jit(solution)/shard_map/image/pallas_call | solution.py:246
  80.7 1.9 %descent.6 = (bf16[2,128,1024]{2,1,0:T(8,128)(2,1)S(1)}, f32[2,128,1024]{2,1,0:T(8,128)S(1)}) custom-call(s32[4]{0:T(128)S(1)} %pad_add_fusion.where, bf16[2,2,128,256]{3,2,1,0:T(8,128)(2,1)S(1)} %half.7.refs_0_, bf16[2,2,128,256]{3,2,1,0:T(8,128)(2,1)S(1)} %get-tuple-element.84.refs_0_.refs_1_, ...), custom_call_target="tpu_custom_call" | custom-call | bytes 1024 | tf_op jit(solution)/shard_map/descent/pallas_call | solution.py:246
  82.6 4.6 %collective-permute-start.33 = (bf16[2,128,1024]{2,1,0:T(8,128)(2,1)S(1)}, bf16[2,128,1024]{2,1,0:T(8,128)(2,1)S(1)}, u32[]{:S(2)}, u32[]{:S(2)}) collective-permute-start(bf16[2,128,1024]{2,1,0:T(8,128)(2,1)S(1)} %get-tuple-element.87.refs_0_), channel_id=1, source_target_pairs={{0,4},{1,5},{2,6},{3,7},{12,8},{13,9},{14,10},{15,11},{16,20},{17,... | collective-permute-start | bytes 1572872 | tf_op jit(solution)/shard_map/ppermute | solution.py:34
  92.9 1.9 %descent.7 = (bf16[2,128,1024]{2,1,0:T(8,128)(2,1)S(1)}, f32[2,128,1024]{2,1,0:T(8,128)S(1)}) custom-call(s32[4]{0:T(128)S(1)} %pad_add_fusion.where, bf16[2,2,128,256]{3,2,1,0:T(8,128)(2,1)S(1)} %get-tuple-element.89.refs_0_.refs_1_, bf16[2,2,128,256]{3,2,1,0:T(8,128)(2,1)S(1)} %get-tuple-element.89.refs_0_.refs_1_, ...), custom_call_target="tpu_custom_call" | custom-call | bytes 1024 | tf_op jit(solution)/shard_map/descent/pallas_call | solution.py:246
  94.8 4.6 %collective-permute-start.38 = (bf16[2,128,1024]{2,1,0:T(8,128)(2,1)S(1)}, bf16[2,128,1024]{2,1,0:T(8,128)(2,1)S(1)}, u32[]{:S(2)}, u32[]{:S(2)}) collective-permute-start(bf16[2,128,1024]{2,1,0:T(8,128)(2,1)S(1)} %get-tuple-element.90.refs_0_), channel_id=1, source_target_pairs={{0,4},{1,5},{2,6},{3,7},{12,8},{13,9},{14,10},{15,11},{16,20},{17,... | collective-permute-start | bytes 1572872 | tf_op jit(solution)/shard_map/ppermute | solution.py:34
  104.5 2.0 %curvature.4 = (f32[2,2,128,256]{3,2,1,0:T(8,128)S(1)}, f32[2,128,256]{2,1,0:T(8,128)S(1)}, f32[2,128,256]{2,1,0:T(8,128)S(1)}, f32[2,32,1024]{2,1,0:T(8,128)S(1)}) custom-call(s32[4]{0:T(128)S(1)} %pad_add_fusion.where, bf16[2,128,1024]{2,1,0:T(8,128)(2,1)S(1)} %add.43.refs_0_, f32[2,128,1024]{2,1,0:T(8,128)S(1)} %get-tuple-element.80.refs_1_, ...), custom_call_target="tpu_custom_call" | custom-call | bytes 1024 | tf_op jit(solution)/shard_map/curvature/pallas_call | solution.py:246
  114.2 2.9 %collective-permute-done.40.refs_4_ = bf16[2,128,1024]{2,1,0:T(8,128)(2,1)S(1)} collective-permute-done((bf16[2,128,1024]{2,1,0:T(8,128)(2,1)S(1)}, bf16[2,128,1024]{2,1,0:T(8,128)(2,1)S(1)}, u32[]{:S(2)}, u32[]{:S(2)}) %collective-permute-start.40) | collective-permute-done | bytes 524320 | tf_op jit(solution)/shard_map/ppermute | solution.py:34
  117.1 2.0 %curvature.5 = (f32[2,2,128,256]{3,2,1,0:T(8,128)S(1)}, f32[2,128,256]{2,1,0:T(8,128)S(1)}, f32[2,128,256]{2,1,0:T(8,128)S(1)}, f32[2,32,1024]{2,1,0:T(8,128)S(1)}) custom-call(s32[4]{0:T(128)S(1)} %pad_add_fusion.where, bf16[2,128,1024]{2,1,0:T(8,128)(2,1)S(1)} %add.45.refs_0_, f32[2,128,1024]{2,1,0:T(8,128)S(1)} %get-tuple-element.88.refs_1_, ...), custom_call_target="tpu_custom_call" | custom-call | bytes 1024 | tf_op jit(solution)/shard_map/curvature/pallas_call | solution.py:246
  121.7 3.5 %collective-permute-done.43.refs_4_ = bf16[2,128,256]{2,1,0:T(8,128)(2,1)S(1)} collective-permute-done((bf16[2,128,256]{2,1,0:T(8,128)(2,1)S(1)}, bf16[2,128,256]{2,1,0:T(8,128)(2,1)S(1)}, u32[]{:S(2)}, u32[]{:S(2)}) %collective-permute-start.43) | collective-permute-done | bytes 131104 | tf_op jit(solution)/shard_map/ppermute | solution.py:38
  129.5 2.0 %curvature.6 = (f32[2,2,128,256]{3,2,1,0:T(8,128)S(1)}, f32[2,128,256]{2,1,0:T(8,128)S(1)}, f32[2,128,256]{2,1,0:T(8,128)S(1)}, f32[2,32,1024]{2,1,0:T(8,128)S(1)}) custom-call(s32[4]{0:T(128)S(1)} %pad_add_fusion.where, bf16[2,128,1024]{2,1,0:T(8,128)(2,1)S(1)} %add.46.refs_0_, f32[2,128,1024]{2,1,0:T(8,128)S(1)} %get-tuple-element.91.refs_1_, ...), custom_call_target="tpu_custom_call" | custom-call | bytes 1024 | tf_op jit(solution)/shard_map/curvature/pallas_call | solution.py:246
  134.1 3.5 %collective-permute-done.48.refs_4_ = bf16[2,128,256]{2,1,0:T(8,128)(2,1)S(1)} collective-permute-done((bf16[2,128,256]{2,1,0:T(8,128)(2,1)S(1)}, bf16[2,128,256]{2,1,0:T(8,128)(2,1)S(1)}, u32[]{:S(2)}, u32[]{:S(2)}) %collective-permute-start.48) | collective-permute-done | bytes 131104 | tf_op jit(solution)/shard_map/ppermute | solution.py:38
  138.3 3.2 %collective-permute-done.49.refs_4_ = bf16[2,128,1024]{2,1,0:T(8,128)(2,1)S(1)} collective-permute-done((bf16[2,128,1024]{2,1,0:T(8,128)(2,1)S(1)}, bf16[2,128,1024]{2,1,0:T(8,128)(2,1)S(1)}, u32[]{:S(2)}, u32[]{:S(2)}) %collective-permute-start.49) | collective-permute-done | bytes 524320 | tf_op jit(solution)/shard_map/ppermute | solution.py:34
  141.5 2.0 %curvature.7 = (f32[2,2,128,256]{3,2,1,0:T(8,128)S(1)}, f32[2,128,256]{2,1,0:T(8,128)S(1)}, f32[2,128,256]{2,1,0:T(8,128)S(1)}, f32[2,32,1024]{2,1,0:T(8,128)S(1)}) custom-call(s32[4]{0:T(128)S(1)} %pad_add_fusion.where, f32[2,8,128]{2,1,0:T(8,128)S(1)} %get-tuple-element.105.refs_0_.refs_6_, f32[2,128,1024]{2,1,0:T(8,128)S(1)} %get-tuple-element.95.refs_1_, ...), custom_call_target="tpu_custom_call" | custom-call | bytes 1024 | tf_op jit(solution)/shard_map/curvature/pallas_call | solution.py:246
  147.4 2.8 %collective-permute-done.52.refs_4_ = bf16[2,128,256]{2,1,0:T(8,128)(2,1)S(1)} collective-permute-done((bf16[2,128,256]{2,1,0:T(8,128)(2,1)S(1)}, bf16[2,128,256]{2,1,0:T(8,128)(2,1)S(1)}, u32[]{:S(2)}, u32[]{:S(2)}) %collective-permute-start.52) | collective-permute-done | bytes 131104 | tf_op jit(solution)/shard_map/ppermute | solution.py:38
  153.2 10.3 %all_to_all.11 = f32[16,1,128]{2,1,0:T(1,128)S(1)} all-to-all(f32[16,1,128]{2,1,0:T(1,128)S(1)} %bitcast.24), channel_id=1, replica_groups={{0,1,2,3,4,5,6,7,8,9,10,11,12,13,14,15},{16,17,18,19,20,21,22,23,24,25,..., dimensions={0} | all-to-all | bytes 16384 | tf_op jit(solution)/shard_map/all_to_all | solution.py:398
  163.5 2.1 %update.1 = (f32[1,2,2,64,1024]{4,3,2,1,0:T(8,128)}, f32[1,2,2,256,256]{4,3,2,1,0:T(8,128)}) custom-call(s32[4]{0:T(128)S(1)} %pad_add_fusion.where, f32[2,8,128]{2,1,0:T(8,128)S(1)} %get-tuple-element.112.refs_0_, f32[16,128]{1,0:T(8,128)S(1)} %bitcast.23, f32[2,2,64,1024]{3,2,1,0:T(8,128)S(1)} %bitcast.21, ...), custom_call_target="tpu_custom_call" | custom-call | bytes 1024 | tf_op jit(solution)/shard_map/update/pallas_call | solution.py:246
  (130 shorter events, 67.9 us)
Async XLA Ops:
  2.4 14.2 %collective-permute-start = (bf16[2,32,1024]{2,1,0:T(8,128)(2,1)S(1)}, bf16[2,32,1024]{2,1,0:T(8,128)(2,1)S(1)}, u32[]{:S(2)}, u32[]{:S(2)}) collective-permute-start(bf16[2,32,1024]{2,1,0:T(8,128)(2,1)S(1)} %fusion.1.refs_2_.refs_1_), channel_id=1, source_target_pairs={{0,4},{1,5},{2,6},{3,7},{4,8},{5,9},{6,10},{7,11},{8,12},{9,13},{1... | collective-permute-start | bytes 393224 | tf_op jit(solution)/shard_map/ppermute | solution.py:34
  5.4 11.2 %collective-permute-start.1 = (bf16[2,32,1024]{2,1,0:T(8,128)(2,1)S(1)}, bf16[2,32,1024]{2,1,0:T(8,128)(2,1)S(1)}, u32[]{:S(2)}, u32[]{:S(2)}) collective-permute-start(bf16[2,32,1024]{2,1,0:T(8,128)(2,1)S(1)} %fusion.1.refs_2_.refs_1_), channel_id=1, source_target_pairs={{0,8},{1,9},{2,10},{3,11},{4,12},{5,13},{6,14},{7,15},{8,0},{9,1},... | collective-permute-start | bytes 393224 | tf_op jit(solution)/shard_map/ppermute | solution.py:34
  8.0 8.6 %collective-permute-start.2 = (bf16[2,32,1024]{2,1,0:T(8,128)(2,1)S(1)}, bf16[2,32,1024]{2,1,0:T(8,128)(2,1)S(1)}, u32[]{:S(2)}, u32[]{:S(2)}) collective-permute-start(bf16[2,32,1024]{2,1,0:T(8,128)(2,1)S(1)} %fusion.1.refs_2_.refs_1_), channel_id=1, source_target_pairs={{0,12},{1,13},{2,14},{3,15},{4,0},{5,1},{6,2},{7,3},{8,4},{9,5},{1... | collective-permute-start | bytes 393224 | tf_op jit(solution)/shard_map/ppermute | solution.py:34
  19.1 19.6 %collective-permute-start.9 = (f32[2,256,256]{2,1,0:T(8,128)S(1)}, f32[2,256,256]{2,1,0:T(8,128)S(1)}, u32[]{:S(2)}, u32[]{:S(2)}) collective-permute-start(f32[2,256,256]{2,1,0:T(8,128)S(1)} %get-tuple-element.62.refs_0_.refs_5_), channel_id=1, source_target_pairs={{0,2},{1,3},{2,0},{3,1},{4,6},{5,7},{6,4},{7,5},{8,10},{9,11},{10,... | collective-permute-start | bytes 1572872 | tf_op jit(solution)/shard_map/ppermute | solution.py:38
  21.3 17.5 %collective-permute-start.8 = (bf16[2,2,128,256]{3,2,1,0:T(8,128)(2,1)S(1)}, bf16[2,2,128,256]{3,2,1,0:T(8,128)(2,1)S(1)}, u32[]{:S(2)}, u32[]{:S(2)}) collective-permute-start(bf16[2,2,128,256]{3,2,1,0:T(8,128)(2,1)S(1)} %half.4.refs_0_), channel_id=1, source_target_pairs={{0,2},{1,3},{2,0},{3,1},{4,6},{5,7},{6,4},{7,5},{8,10},{9,11},{10,... | collective-permute-start | bytes 786440 | tf_op jit(solution)/shard_map/ppermute | solution.py:38
  22.7 8.8 %collective-permute-start.5 = (bf16[2,32,1024]{2,1,0:T(8,128)(2,1)S(1)}, bf16[2,32,1024]{2,1,0:T(8,128)(2,1)S(1)}, u32[]{:S(2)}, u32[]{:S(2)}) collective-permute-start(bf16[2,32,1024]{2,1,0:T(8,128)(2,1)S(1)} %get-tuple-element.67.refs_1_), channel_id=1, source_target_pairs={{0,4},{1,5},{2,6},{3,7},{4,8},{5,9},{6,10},{7,11},{8,12},{9,13},{1... | collective-permute-start | bytes 393224 | tf_op jit(solution)/shard_map/ppermute | solution.py:34
  26.0 10.3 %collective-permute-start.6 = (bf16[2,32,1024]{2,1,0:T(8,128)(2,1)S(1)}, bf16[2,32,1024]{2,1,0:T(8,128)(2,1)S(1)}, u32[]{:S(2)}, u32[]{:S(2)}) collective-permute-start(bf16[2,32,1024]{2,1,0:T(8,128)(2,1)S(1)} %get-tuple-element.67.refs_1_), channel_id=1, source_target_pairs={{0,8},{1,9},{2,10},{3,11},{4,12},{5,13},{6,14},{7,15},{8,0},{9,1},... | collective-permute-start | bytes 393224 | tf_op jit(solution)/shard_map/ppermute | solution.py:34
  27.6 8.7 %collective-permute-start.7 = (bf16[2,32,1024]{2,1,0:T(8,128)(2,1)S(1)}, bf16[2,32,1024]{2,1,0:T(8,128)(2,1)S(1)}, u32[]{:S(2)}, u32[]{:S(2)}) collective-permute-start(bf16[2,32,1024]{2,1,0:T(8,128)(2,1)S(1)} %get-tuple-element.67.refs_1_), channel_id=1, source_target_pairs={{0,12},{1,13},{2,14},{3,15},{4,0},{5,1},{6,2},{7,3},{8,4},{9,5},{1... | collective-permute-start | bytes 393224 | tf_op jit(solution)/shard_map/ppermute | solution.py:34
  39.5 7.8 %collective-permute-start.12 = (bf16[2,2,128,256]{3,2,1,0:T(8,128)(2,1)S(1)}, bf16[2,2,128,256]{3,2,1,0:T(8,128)(2,1)S(1)}, u32[]{:S(2)}, u32[]{:S(2)}) collective-permute-start(bf16[2,2,128,256]{3,2,1,0:T(8,128)(2,1)S(1)} %get-tuple-element.69.refs_0_.refs_1_), channel_id=1, source_target_pairs={{0,1},{1,0},{2,3},{3,2},{4,5},{5,4},{6,7},{7,6},{8,9},{9,8},{10,11... | collective-permute-start | bytes 786440 | tf_op jit(solution)/shard_map/ppermute | solution.py:38
  40.8 17.2 %collective-permute-start.16 = (bf16[2,2,128,256]{3,2,1,0:T(8,128)(2,1)S(1)}, bf16[2,2,128,256]{3,2,1,0:T(8,128)(2,1)S(1)}, u32[]{:S(2)}, u32[]{:S(2)}) collective-permute-start(bf16[2,2,128,256]{3,2,1,0:T(8,128)(2,1)S(1)} %half.5.refs_0_), channel_id=1, source_target_pairs={{0,2},{1,3},{2,0},{3,1},{4,6},{5,7},{6,4},{7,5},{8,10},{9,11},{10,... | collective-permute-start | bytes 786440 | tf_op jit(solution)/shard_map/ppermute | solution.py:38
  41.7 10.8 %collective-permute-start.13 = (bf16[2,32,1024]{2,1,0:T(8,128)(2,1)S(1)}, bf16[2,32,1024]{2,1,0:T(8,128)(2,1)S(1)}, u32[]{:S(2)}, u32[]{:S(2)}) collective-permute-start(bf16[2,32,1024]{2,1,0:T(8,128)(2,1)S(1)} %get-tuple-element.73.refs_1_), channel_id=1, source_target_pairs={{0,4},{1,5},{2,6},{3,7},{4,8},{5,9},{6,10},{7,11},{8,12},{9,13},{1... | collective-permute-start | bytes 393224 | tf_op jit(solution)/shard_map/ppermute | solution.py:34
  44.9 10.6 %collective-permute-start.14 = (bf16[2,32,1024]{2,1,0:T(8,128)(2,1)S(1)}, bf16[2,32,1024]{2,1,0:T(8,128)(2,1)S(1)}, u32[]{:S(2)}, u32[]{:S(2)}) collective-permute-start(bf16[2,32,1024]{2,1,0:T(8,128)(2,1)S(1)} %get-tuple-element.73.refs_1_), channel_id=1, source_target_pairs={{0,8},{1,9},{2,10},{3,11},{4,12},{5,13},{6,14},{7,15},{8,0},{9,1},... | collective-permute-start | bytes 393224 | tf_op jit(solution)/shard_map/ppermute | solution.py:34
  46.6 9.0 %collective-permute-start.15 = (bf16[2,32,1024]{2,1,0:T(8,128)(2,1)S(1)}, bf16[2,32,1024]{2,1,0:T(8,128)(2,1)S(1)}, u32[]{:S(2)}, u32[]{:S(2)}) collective-permute-start(bf16[2,32,1024]{2,1,0:T(8,128)(2,1)S(1)} %get-tuple-element.73.refs_1_), channel_id=1, source_target_pairs={{0,12},{1,13},{2,14},{3,15},{4,0},{5,1},{6,2},{7,3},{8,4},{9,5},{1... | collective-permute-start | bytes 393224 | tf_op jit(solution)/shard_map/ppermute | solution.py:34
  49.2 16.5 %collective-permute-start.20 = (bf16[2,128,1024]{2,1,0:T(8,128)(2,1)S(1)}, bf16[2,128,1024]{2,1,0:T(8,128)(2,1)S(1)}, u32[]{:S(2)}, u32[]{:S(2)}) collective-permute-start(bf16[2,128,1024]{2,1,0:T(8,128)(2,1)S(1)} %get-tuple-element.72.refs_0_), channel_id=1, source_target_pairs={{0,4},{1,5},{2,6},{3,7},{12,8},{13,9},{14,10},{15,11},{16,20},{17,... | collective-permute-start | bytes 1572872 | tf_op jit(solution)/shard_map/ppermute | solution.py:34
  52.4 25.3 %collective-permute-start.25 = (f32[2,256,256]{2,1,0:T(8,128)S(1)}, f32[2,256,256]{2,1,0:T(8,128)S(1)}, u32[]{:S(2)}, u32[]{:S(2)}) collective-permute-start(f32[2,256,256]{2,1,0:T(8,128)S(1)} %get-tuple-element.83.refs_5_), channel_id=1, source_target_pairs={{0,2},{1,3},{2,0},{3,1},{4,6},{5,7},{6,4},{7,5},{8,10},{9,11},{10,... | collective-permute-start | bytes 1572872 | tf_op jit(solution)/shard_map/ppermute | solution.py:38
  59.1 11.1 %collective-permute-start.21 = (bf16[2,32,1024]{2,1,0:T(8,128)(2,1)S(1)}, bf16[2,32,1024]{2,1,0:T(8,128)(2,1)S(1)}, u32[]{:S(2)}, u32[]{:S(2)}) collective-permute-start(bf16[2,32,1024]{2,1,0:T(8,128)(2,1)S(1)} %get-tuple-element.81.refs_1_), channel_id=1, source_target_pairs={{0,4},{1,5},{2,6},{3,7},{4,8},{5,9},{6,10},{7,11},{8,12},{9,13},{1... | collective-permute-start | bytes 393224 | tf_op jit(solution)/shard_map/ppermute | solution.py:34
  62.4 12.7 %collective-permute-start.22 = (bf16[2,32,1024]{2,1,0:T(8,128)(2,1)S(1)}, bf16[2,32,1024]{2,1,0:T(8,128)(2,1)S(1)}, u32[]{:S(2)}, u32[]{:S(2)}) collective-permute-start(bf16[2,32,1024]{2,1,0:T(8,128)(2,1)S(1)} %get-tuple-element.81.refs_1_), channel_id=1, source_target_pairs={{0,8},{1,9},{2,10},{3,11},{4,12},{5,13},{6,14},{7,15},{8,0},{9,1},... | collective-permute-start | bytes 393224 | tf_op jit(solution)/shard_map/ppermute | solution.py:34
  63.7 12.1 %collective-permute-start.23 = (bf16[2,32,1024]{2,1,0:T(8,128)(2,1)S(1)}, bf16[2,32,1024]{2,1,0:T(8,128)(2,1)S(1)}, u32[]{:S(2)}, u32[]{:S(2)}) collective-permute-start(bf16[2,32,1024]{2,1,0:T(8,128)(2,1)S(1)} %get-tuple-element.81.refs_1_), channel_id=1, source_target_pairs={{0,12},{1,13},{2,14},{3,15},{4,0},{5,1},{6,2},{7,3},{8,4},{9,5},{1... | collective-permute-start | bytes 393224 | tf_op jit(solution)/shard_map/ppermute | solution.py:34
  65.7 12.5 %collective-permute-start.24 = (bf16[2,2,128,256]{3,2,1,0:T(8,128)(2,1)S(1)}, bf16[2,2,128,256]{3,2,1,0:T(8,128)(2,1)S(1)}, u32[]{:S(2)}, u32[]{:S(2)}) collective-permute-start(bf16[2,2,128,256]{3,2,1,0:T(8,128)(2,1)S(1)} %half.6.refs_0_), channel_id=1, source_target_pairs={{0,2},{1,3},{2,0},{3,1},{4,6},{5,7},{6,4},{7,5},{8,10},{9,11},{10,... | collective-permute-start | bytes 786440 | tf_op jit(solution)/shard_map/ppermute | solution.py:38
  70.1 17.0 %collective-permute-start.29 = (bf16[2,128,1024]{2,1,0:T(8,128)(2,1)S(1)}, bf16[2,128,1024]{2,1,0:T(8,128)(2,1)S(1)}, u32[]{:S(2)}, u32[]{:S(2)}) collective-permute-start(bf16[2,128,1024]{2,1,0:T(8,128)(2,1)S(1)} %get-tuple-element.79.refs_0_), channel_id=1, source_target_pairs={{0,4},{1,5},{2,6},{3,7},{12,8},{13,9},{14,10},{15,11},{16,20},{17,... | collective-permute-start | bytes 1572872 | tf_op jit(solution)/shard_map/ppermute | solution.py:34
  75.0 13.5 %collective-permute-start.30 = (bf16[2,128,1024]{2,1,0:T(8,128)(2,1)S(1)}, bf16[2,128,1024]{2,1,0:T(8,128)(2,1)S(1)}, u32[]{:S(2)}, u32[]{:S(2)}) collective-permute-start(bf16[2,128,1024]{2,1,0:T(8,128)(2,1)S(1)} %add.39.refs_0_), channel_id=1, source_target_pairs={{4,8},{5,9},{6,10},{7,11},{8,4},{9,5},{10,6},{11,7},{20,24},{21,25... | collective-permute-start | bytes 1572872 | tf_op jit(solution)/shard_map/ppermute | solution.py:34
  80.2 10.2 %collective-permute-start.31 = (bf16[2,2,128,256]{3,2,1,0:T(8,128)(2,1)S(1)}, bf16[2,2,128,256]{3,2,1,0:T(8,128)(2,1)S(1)}, u32[]{:S(2)}, u32[]{:S(2)}) collective-permute-start(bf16[2,2,128,256]{3,2,1,0:T(8,128)(2,1)S(1)} %half.7.refs_0_), channel_id=1, source_target_pairs={{0,2},{1,3},{2,0},{3,1},{4,6},{5,7},{6,4},{7,5},{8,10},{9,11},{10,... | collective-permute-start | bytes 786440 | tf_op jit(solution)/shard_map/ppermute | solution.py:38
  82.6 16.9 %collective-permute-start.33 = (bf16[2,128,1024]{2,1,0:T(8,128)(2,1)S(1)}, bf16[2,128,1024]{2,1,0:T(8,128)(2,1)S(1)}, u32[]{:S(2)}, u32[]{:S(2)}) collective-permute-start(bf16[2,128,1024]{2,1,0:T(8,128)(2,1)S(1)} %get-tuple-element.87.refs_0_), channel_id=1, source_target_pairs={{0,4},{1,5},{2,6},{3,7},{12,8},{13,9},{14,10},{15,11},{16,20},{17,... | collective-permute-start | bytes 1572872 | tf_op jit(solution)/shard_map/ppermute | solution.py:34
  87.8 13.0 %collective-permute-start.34 = (bf16[2,128,1024]{2,1,0:T(8,128)(2,1)S(1)}, bf16[2,128,1024]{2,1,0:T(8,128)(2,1)S(1)}, u32[]{:S(2)}, u32[]{:S(2)}) collective-permute-start(bf16[2,128,1024]{2,1,0:T(8,128)(2,1)S(1)} %add.40.refs_0_), channel_id=1, source_target_pairs={{4,8},{5,9},{6,10},{7,11},{8,4},{9,5},{10,6},{11,7},{20,24},{21,25... | collective-permute-start | bytes 1572872 | tf_op jit(solution)/shard_map/ppermute | solution.py:34
  89.2 15.3 %collective-permute-start.35 = (bf16[2,128,1024]{2,1,0:T(8,128)(2,1)S(1)}, bf16[2,128,1024]{2,1,0:T(8,128)(2,1)S(1)}, u32[]{:S(2)}, u32[]{:S(2)}) collective-permute-start(bf16[2,128,1024]{2,1,0:T(8,128)(2,1)S(1)} %add.41.refs_0_), channel_id=1, source_target_pairs={{4,0},{5,1},{6,2},{7,3},{8,12},{9,13},{10,14},{11,15},{20,16},{21,... | collective-permute-start | bytes 1572872 | tf_op jit(solution)/shard_map/ppermute | solution.py:34
  94.8 16.0 %collective-permute-start.38 = (bf16[2,128,1024]{2,1,0:T(8,128)(2,1)S(1)}, bf16[2,128,1024]{2,1,0:T(8,128)(2,1)S(1)}, u32[]{:S(2)}, u32[]{:S(2)}) collective-permute-start(bf16[2,128,1024]{2,1,0:T(8,128)(2,1)S(1)} %get-tuple-element.90.refs_0_), channel_id=1, source_target_pairs={{0,4},{1,5},{2,6},{3,7},{12,8},{13,9},{14,10},{15,11},{16,20},{17,... | collective-permute-start | bytes 1572872 | tf_op jit(solution)/shard_map/ppermute | solution.py:34
  100.1 12.1 %collective-permute-start.39 = (bf16[2,128,1024]{2,1,0:T(8,128)(2,1)S(1)}, bf16[2,128,1024]{2,1,0:T(8,128)(2,1)S(1)}, u32[]{:S(2)}, u32[]{:S(2)}) collective-permute-start(bf16[2,128,1024]{2,1,0:T(8,128)(2,1)S(1)} %add.42.refs_0_), channel_id=1, source_target_pairs={{4,8},{5,9},{6,10},{7,11},{8,4},{9,5},{10,6},{11,7},{20,24},{21,25... | collective-permute-start | bytes 1572872 | tf_op jit(solution)/shard_map/ppermute | solution.py:34
  101.5 15.6 %collective-permute-start.40 = (bf16[2,128,1024]{2,1,0:T(8,128)(2,1)S(1)}, bf16[2,128,1024]{2,1,0:T(8,128)(2,1)S(1)}, u32[]{:S(2)}, u32[]{:S(2)}) collective-permute-start(bf16[2,128,1024]{2,1,0:T(8,128)(2,1)S(1)} %add.43.refs_0_), channel_id=1, source_target_pairs={{4,0},{5,1},{6,2},{7,3},{8,12},{9,13},{10,14},{11,15},{20,16},{21,... | collective-permute-start | bytes 1572872 | tf_op jit(solution)/shard_map/ppermute | solution.py:34
  111.5 14.3 %collective-permute-start.44 = (bf16[2,128,1024]{2,1,0:T(8,128)(2,1)S(1)}, bf16[2,128,1024]{2,1,0:T(8,128)(2,1)S(1)}, u32[]{:S(2)}, u32[]{:S(2)}) collective-permute-start(bf16[2,128,1024]{2,1,0:T(8,128)(2,1)S(1)} %add.44.refs_0_), channel_id=1, source_target_pairs={{4,8},{5,9},{6,10},{7,11},{8,4},{9,5},{10,6},{11,7},{20,24},{21,25... | collective-permute-start | bytes 1572872 | tf_op jit(solution)/shard_map/ppermute | solution.py:34
  112.9 16.6 %collective-permute-start.45 = (bf16[2,128,1024]{2,1,0:T(8,128)(2,1)S(1)}, bf16[2,128,1024]{2,1,0:T(8,128)(2,1)S(1)}, u32[]{:S(2)}, u32[]{:S(2)}) collective-permute-start(bf16[2,128,1024]{2,1,0:T(8,128)(2,1)S(1)} %add.45.refs_0_), channel_id=1, source_target_pairs={{4,0},{5,1},{6,2},{7,3},{8,12},{9,13},{10,14},{11,15},{20,16},{21,... | collective-permute-start | bytes 1572872 | tf_op jit(solution)/shard_map/ppermute | solution.py:34
  126.5 15.0 %collective-permute-start.49 = (bf16[2,128,1024]{2,1,0:T(8,128)(2,1)S(1)}, bf16[2,128,1024]{2,1,0:T(8,128)(2,1)S(1)}, u32[]{:S(2)}, u32[]{:S(2)}) collective-permute-start(bf16[2,128,1024]{2,1,0:T(8,128)(2,1)S(1)} %add.46.refs_0_), channel_id=1, source_target_pairs={{4,0},{5,1},{6,2},{7,3},{8,12},{9,13},{10,14},{11,15},{20,16},{21,... | collective-permute-start | bytes 1572872 | tf_op jit(solution)/shard_map/ppermute | solution.py:34
  146.1 6.3 %collective-permute-start.53 = (bf16[2,128,256]{2,1,0:T(8,128)(2,1)S(1)}, bf16[2,128,256]{2,1,0:T(8,128)(2,1)S(1)}, u32[]{:S(2)}, u32[]{:S(2)}) collective-permute-start(bf16[2,128,256]{2,1,0:T(8,128)(2,1)S(1)} %bend_half.7.refs_0_), channel_id=1, source_target_pairs={{0,2},{1,3},{2,0},{3,1},{4,6},{5,7},{6,4},{7,5},{8,10},{9,11},{10,... | collective-permute-start | bytes 393224 | tf_op jit(solution)/shard_map/ppermute | solution.py:38
  (27 other events, 86.0 us)
